TPU v7x, 32 devices: a whole 2x2x4 slice. The times are simulated.
32 devices in a mesh: cell: 4 (over x, core), gene: 8 (over z, y).
Axes of the slice: x: 2, y: 2, z: 4, core: 2. Of those that a mesh axis runs over, the one named last changes fastest.
Arguments:
- query_rows: bfloat16 [4, 1024, 1536], P('cell', 'gene'), may hold values from -1.5 to 1.5
- key_rows: bfloat16 [4, 1024, 1536], P('cell', 'gene'), may hold values from -1.5 to 1.5
- value_rows: bfloat16 [4, 1024, 1536], P('cell', 'gene'), may hold values from -6 to 6
- output_rows: bfloat16 [4, 1024, 1536], P('cell', 'gene'), may hold values from -6 to 6
- output_grad: bfloat16 [4, 1024, 1536], P('cell', 'gene'), may hold values from -6 to 6
- row_lse: float32 [4, 1024, 12], P('cell', 'gene'), may hold values from 3 to 6
- block_bias: float32 [8, 12, 8], replicated, may hold values from -1.5 to 1.5
- block_index: int32 [8, 8], replicated, may hold values from 0 to 7, each once within a row
- block_count: int32 [8], replicated, may hold values from 1 to 8, 32 in all
Outputs:
- query_grad: bfloat16 [4, 1024, 1536], P('cell', 'gene')
- key_grad: bfloat16 [4, 1024, 1536], P('cell', 'gene')
- value_grad: bfloat16 [4, 1024, 1536], P('cell', 'gene')
- bias_grad: float32 [8, 12, 8], P('gene', None, 'cell')
Inputs may be any that keep to these rules, and one draw needn't show every extreme that they name: Each row of block_index lists every key block once; its first block_count entries are the listed ones, and one row block lists all 8. `block_count`: one row block has 8 listed key blocks.
All inputs are finite; a program needn't handle non-finite values.
Results may differ from a plain program's by a relative error of at most 0.0049.
Values may be sent and summed in bfloat16 or wider, within the bound.
No kernel may reach another device: no remote copies, remote signals or barrier semaphores. Data moves between devices by JAX's collectives and lax.ppermute only.
A program may use at most 128 MiB of HBM per device.

v0:
```python
import functools
import math

import jax
import jax.numpy as jnp
from jax import lax
from jax.experimental import pallas as pl
from jax.experimental.pallas import tpu as pltpu
from jax.sharding import PartitionSpec as P

BLOCK = 128
STAT_ROWS = 16
SUM_ROWS = 16
VMEM_LIMIT = 56 * 1024 * 1024


def split_three(row):
    high = row.astype(jnp.bfloat16).astype(jnp.float32)
    middle = (row - high).astype(jnp.bfloat16).astype(jnp.float32)
    return [high, middle, row - high - middle]


def pack_far_kernel(plan, query, output, grad, lse, *outs):
    members, width, head_size = plan["members"], plan["width"], plan["head_size"]
    mine = lax.axis_index("gene") % members
    for hop in range(members):
        owner = mine ^ hop
        columns = pl.ds(pl.multiple_of(owner * width, head_size), width)
        grad_part, target = grad[0, :, columns], outs[hop]
        products = grad_part.astype(jnp.float32) * output[0, :, columns].astype(jnp.float32)
        target[0:BLOCK, :] = query[0, :, columns]
        target[BLOCK : 2 * BLOCK, :] = grad_part
        for head in range(plan["share"]):
            lanes = slice(head * head_size, (head + 1) * head_size)
            delta = jnp.sum(jnp.transpose(products[:, lanes]), axis=0, keepdims=True)
            saved = lse[0, pl.ds(owner * plan["share"] + head, 1), :]
            rows = split_three(saved) + split_three(delta)
            rows.append(jnp.zeros((STAT_ROWS - 6, BLOCK), jnp.float32))
            stats = jnp.concatenate(rows, axis=0).astype(jnp.bfloat16)
            target[2 * BLOCK : 2 * BLOCK + STAT_ROWS, lanes] = stats


def pack_near_kernel(plan, key, value, *refs):
    members, width, head_size = plan["members"], plan["width"], plan["head_size"]
    mine = lax.axis_index("gene") % members
    base = 2 * BLOCK + STAT_ROWS
    for hop in range(members):
        columns = pl.ds(pl.multiple_of((mine ^ hop) * width, head_size), width)
        near = refs[members + hop]
        near[0:base, :] = refs[hop][...]
        near[base : base + BLOCK, :] = key[0, :, columns]
        near[base + BLOCK : base + 2 * BLOCK, :] = value[0, :, columns]


def table_kernel(plan, bias, index, count, bias_out, mask_out):
    members, share, blocks = plan["members"], plan["share"], plan["blocks"]
    heads = members * share
    me = lax.axis_index("gene")
    mine = me % members
    for hop in range(blocks):
        row = me ^ hop
        for side in range(members):
            mask_out[hop * members + side] = 0
            for head in range(share):
                bias_out[(head * blocks + hop) * members + side] = 0.0

        def listed(slot, carry, hop=hop, row=row):
            column = index[row * blocks + slot]
            side = column ^ me

            @pl.when(side < members)
            def _():
                mask_out[hop * members + side] = 1
                for head in range(share):
                    bias_out[(head * blocks + hop) * members + side] = bias[
                        (row * heads + mine * share + head) * blocks + slot
                    ]

            return carry

        lax.fori_loop(0, count[row], listed, 0)


def stage_kernel(plan, first, last, bias, mask, *refs):
    blocks, members, share = plan["blocks"], plan["members"], plan["share"]
    head_size, scale = plan["head_size"], plan["scale"]
    count = last - first
    near = refs[:members]
    rest = refs[members:]
    if first == 0:
        pieces = near
        outs, sum_refs, rest = rest[:count], rest[count : count + 2], rest[count + 2 :]
        grads_out = None
    else:
        pieces, sum_refs, rest = rest[:count], rest[count : count + 2], rest[count + 2 :]
        outs, grads_out, rest = rest[:count], rest[count : count + members], rest[count + members :]
    weights_low, grads_low = rest
    base = 2 * BLOCK + STAT_ROWS
    nt = (((1,), (1,)), ((), ()))
    nn = (((1,), (0,)), ((), ()))
    tn = (((0,), (0,)), ((), ()))
    dot = functools.partial(lax.dot_general, preferred_element_type=jnp.float32)

    def one_head(head, carry):
        lanes = pl.ds(pl.multiple_of(head * head_size, head_size), head_size)
        keys = jnp.concatenate([near[s][base : base + BLOCK, lanes] for s in range(members)], axis=0)
        values = jnp.concatenate(
            [near[s][base + BLOCK : base + 2 * BLOCK, lanes] for s in range(members)], axis=0
        )
        for hop in range(count):
            piece = pieces[hop]
            scores = dot(keys, piece[0:BLOCK, lanes], nt)
            weight_grads = dot(values, piece[BLOCK : 2 * BLOCK, lanes], nt)
            stats = piece[2 * BLOCK : base, lanes].astype(jnp.float32)
            saved = stats[0:1] + stats[1:2] + stats[2:3]
            delta = stats[3:4] + stats[4:5] + stats[5:6]
            place = slice(hop * BLOCK, (hop + 1) * BLOCK)
            rows = []
            for side in range(members):
                part = slice(side * BLOCK, (side + 1) * BLOCK)
                at = (first + hop) * members + side
                live = mask[at] > 0
                shift = bias[head * (blocks * members) + at] - saved
                grown = jnp.exp(scores[part] * scale + shift)
                weights = jnp.where(live, grown, 0.0)
                score_grads = weights * (weight_grads[part] - delta)
                weights_low[part, place] = weights.astype(jnp.bfloat16)
                grads_low[part, place] = score_grads.astype(jnp.bfloat16)
                rows += split_three(jnp.sum(score_grads, axis=0, keepdims=True))
            rows.append(jnp.zeros((SUM_ROWS - 3 * members, BLOCK), jnp.float32))
            outs[hop][BLOCK : BLOCK + SUM_ROWS, lanes] = jnp.concatenate(rows, axis=0).astype(
                jnp.bfloat16
            )
        queries = jnp.concatenate([piece[0:BLOCK, lanes] for piece in pieces], axis=0)
        grads = jnp.concatenate([piece[BLOCK : 2 * BLOCK, lanes] for piece in pieces], axis=0)
        value_grad = dot(weights_low[...], grads, nn)
        key_grad = dot(grads_low[...], queries, nn)
        query_grad = dot(grads_low[...], keys, tn) * scale
        for hop in range(count):
            part = slice(hop * BLOCK, (hop + 1) * BLOCK)
            outs[hop][0:BLOCK, lanes] = query_grad[part].astype(jnp.bfloat16)
        if grads_out is None:
            sum_refs[0][:, lanes] = key_grad
            sum_refs[1][:, lanes] = value_grad
        else:
            key_grad = (key_grad + sum_refs[0][:, lanes]) * scale
            value_grad = value_grad + sum_refs[1][:, lanes]
            for hop in range(members):
                part = slice(hop * BLOCK, (hop + 1) * BLOCK)
                grads_out[hop][0:BLOCK, lanes] = key_grad[part].astype(jnp.bfloat16)
                grads_out[hop][BLOCK : 2 * BLOCK, lanes] = value_grad[part].astype(jnp.bfloat16)
        return carry

    lax.fori_loop(0, share, one_head, 0)


def query_kernel(plan, index, *refs):
    blocks, members, share = plan["blocks"], plan["members"], plan["share"]
    width, head_size = plan["width"], plan["head_size"]
    pieces = refs[:blocks]
    query_grad, bias_out, slots, sums = refs[blocks:]
    me = lax.axis_index("gene")
    mine = me % members
    for slot in range(blocks):
        slots[index[me * blocks + slot]] = slot
    for hop in range(members):
        owner = mine ^ hop
        columns = pl.ds(pl.multiple_of(owner * width, head_size), width)
        total = jnp.zeros((BLOCK, width), jnp.float32)
        for other in range(hop, blocks, members):
            total = total + pieces[other][0:BLOCK, :].astype(jnp.float32)
            for head in range(share):
                lanes = slice(head * head_size, (head + 1) * head_size)
                rows = pieces[other][BLOCK : BLOCK + SUM_ROWS, lanes].astype(jnp.float32)
                for side in range(members):
                    slot = slots[me ^ other ^ side]
                    sums[pl.ds((owner * share + head) * blocks + slot, 1), :] = (
                        rows[3 * side : 3 * side + 1]
                        + rows[3 * side + 1 : 3 * side + 2]
                        + rows[3 * side + 2 : 3 * side + 3]
                    )
        query_grad[0, :, columns] = total.astype(jnp.bfloat16)
    bias_out[...] = jnp.sum(jnp.transpose(sums[...]), axis=0, keepdims=True)


def owner_kernel(plan, *refs):
    members, width, head_size = plan["members"], plan["width"], plan["head_size"]
    pieces = refs[:members]
    key_grad, value_grad = refs[members:]
    mine = lax.axis_index("gene") % members
    for hop in range(members):
        columns = pl.ds(pl.multiple_of((mine ^ hop) * width, head_size), width)
        key_grad[0, :, columns] = pieces[hop][0:BLOCK, :]
        value_grad[0, :, columns] = pieces[hop][BLOCK : 2 * BLOCK, :]


def call(kernel, outs, scratch=(), smem_in=0, smem_out=False, count=0):
    places = [pl.BlockSpec(memory_space=pltpu.SMEM)] * smem_in
    places += [pl.BlockSpec(memory_space=pltpu.VMEM)] * count
    space = pltpu.SMEM if smem_out else pltpu.VMEM
    return pl.pallas_call(
        kernel,
        out_shape=outs,
        in_specs=places,
        out_specs=[pl.BlockSpec(memory_space=space)] * len(outs),
        scratch_shapes=list(scratch),
        compiler_params=pltpu.CompilerParams(vmem_limit_bytes=VMEM_LIMIT),
    )


def shards(
    query_rows,
    key_rows,
    value_rows,
    output_rows,
    output_grad,
    row_lse,
    block_bias,
    block_index,
    block_count,
):
    row_width = query_rows.shape[2]
    head_count = row_lse.shape[2]
    blocks = block_bias.shape[0]
    members = math.gcd(blocks, head_count)
    share = head_count // members
    head_size = row_width // head_count
    width = share * head_size
    plan = dict(
        blocks=blocks,
        members=members,
        share=share,
        head_size=head_size,
        width=width,
        scale=1.0 / math.sqrt(head_size),
    )
    low, full = jnp.bfloat16, jnp.float32
    base = 2 * BLOCK + STAT_ROWS
    near = jax.ShapeDtypeStruct((base + 2 * BLOCK, width), low)
    far = jax.ShapeDtypeStruct((base, width), low)

    def move(array, hop):
        return lax.ppermute(array, "gene", [(i, i ^ hop) for i in range(blocks)])

    far_sent = call(functools.partial(pack_far_kernel, plan), [far] * members, count=4)(
        query_rows, output_rows, output_grad, jnp.transpose(row_lse, (0, 2, 1))
    )
    near_sent = call(functools.partial(pack_near_kernel, plan), [near] * members, count=2 + members)(
        key_rows, value_rows, *far_sent
    )
    far_pieces = [move(far_sent[hop % members], hop) for hop in range(members, blocks)]
    near_pieces = [near_sent[0]] + [move(near_sent[hop], hop) for hop in range(1, members)]
    tables = call(
        functools.partial(table_kernel, plan),
        [
            jax.ShapeDtypeStruct((share * blocks * members,), full),
            jax.ShapeDtypeStruct((blocks * members,), jnp.int32),
        ],
        smem_in=3,
        smem_out=True,
    )(block_bias.reshape(-1), block_index.reshape(-1), block_count)
    query_out = jax.ShapeDtypeStruct((BLOCK + SUM_ROWS, width), low)
    owner_out = jax.ShapeDtypeStruct((2 * BLOCK, width), low)
    partial = jax.ShapeDtypeStruct((members * BLOCK, width), full)

    def stage(first, last, outs, *arrays):
        scratch = pltpu.VMEM((members * BLOCK, (last - first) * BLOCK), low)
        return call(
            functools.partial(stage_kernel, plan, first, last),
            outs,
            scratch=[scratch, scratch],
            smem_in=2,
            count=len(arrays),
        )(*tables, *arrays)

    made = stage(0, members, [query_out] * members + [partial] * 2, *near_pieces)
    near_query, partials = made[:members], made[members:]
    near_query = [near_query[0]] + [move(near_query[hop], hop) for hop in range(1, members)]
    made = stage(
        members,
        blocks,
        [query_out] * (blocks - members) + [owner_out] * members,
        *near_pieces,
        *far_pieces,
        *partials,
    )
    far_query = [move(made[hop - members], hop) for hop in range(members, blocks)]
    owned = made[blocks - members :]
    owned = [owned[0]] + [move(owned[hop], hop) for hop in range(1, members)]
    whole = jax.ShapeDtypeStruct((1, BLOCK, row_width), low)
    query_grad, sums = call(
        functools.partial(query_kernel, plan),
        [whole, jax.ShapeDtypeStruct((1, head_count * blocks), full)],
        scratch=[pltpu.SMEM((blocks,), jnp.int32), pltpu.VMEM((head_count * blocks, BLOCK), full)],
        smem_in=1,
        count=blocks,
    )(block_index.reshape(-1), *near_query, *far_query)
    key_grad, value_grad = call(functools.partial(owner_kernel, plan), [whole] * 2, count=members)(
        *owned
    )
    bias_grad = lax.psum_scatter(
        sums.reshape(1, head_count, blocks), "cell", scatter_dimension=2, tiled=True
    )
    return (query_grad, key_grad, value_grad, bias_grad)


def solution(mesh):
    rows = P("cell", "gene", None)
    in_specs = (rows,) * 6 + (P(),) * 3
    out_specs = (rows, rows, rows, P("gene", None, "cell"))
    return jax.shard_map(shards, mesh=mesh, in_specs=in_specs, out_specs=out_specs, check_vma=False)
```

profile of v0, /device:TPU:0, one launch (start us, length us, event | category | flops | bytes accessed | tf_op | source)
XLA Modules:
  0.0 95.5 jit_solution(3690947416614388162)
XLA Ops:
  0.6 1.3 %copy.23 = f32[1,128,12]{1,2,0:T(8,128)} copy(f32[1,128,12]{1,0,2:T(1,128)} %param.14) | data formatting | bytes 12288 | tf_op args[5]
  1.9 2.3 %shard_map.121 = (bf16[272,384]{1,0:T(8,128)(2,1)}, bf16[272,384]{1,0:T(8,128)(2,1)}, bf16[272,384]{1,0:T(8,128)(2,1)}, bf16[272,384]{1,0:T(8,128)(2,1)}) custom-call(bf16[1,128,1536]{2,1,0:T(8,128)(2,1)} %query.1, bf16[1,128,1536]{2,1,0:T(8,128)(2,1)} %output.1, bf16[1,128,1536]{2,1,0:T(8,128)(2,1)} %grad.1, f32[1,12,128]{2,1,0:T(8,128)} %bitcast.5), custom_call_target="tpu_custom_call" | custom-call | tf_op jit(solution)/shard_map/pallas_call | solution.py:245
  4.3 0.0 copy-start.21
  4.3 2.7 %shard_map.122 = (bf16[528,384]{1,0:T(8,128)(2,1)}, bf16[528,384]{1,0:T(8,128)(2,1)}, bf16[528,384]{1,0:T(8,128)(2,1)}, bf16[528,384]{1,0:T(8,128)(2,1)}) custom-call(bf16[1,128,1536]{2,1,0:T(8,128)(2,1)} %key.1, bf16[1,128,1536]{2,1,0:T(8,128)(2,1)} %value.1, bf16[272,384]{1,0:T(8,128)(2,1)} %get-tuple-element.34.refs_0_, ...), custom_call_target="tpu_custom_call" | custom-call | tf_op jit(solution)/shard_map/pallas_call | solution.py:248
  7.0 3.0 %collective-permute-start = (bf16[528,384]{1,0:T(8,128)(2,1)}, bf16[528,384]{1,0:T(8,128)(2,1)S(1)}, u32[]{:S(2)}, u32[]{:S(2)}) collective-permute-start(bf16[528,384]{1,0:T(8,128)(2,1)} %get-tuple-element.39), channel_id=1, source_target_pairs={{0,1},{1,0},{2,3},{3,2},{4,5},{5,4},{6,7},{7,6},{8,9},{9,8},{10,11... | collective-permute-start | bytes 1216520 | tf_op jit(solution)/shard_map/ppermute | solution.py:243
  10.0 1.6 %collective-permute-start.1 = (bf16[528,384]{1,0:T(8,128)(2,1)}, bf16[528,384]{1,0:T(8,128)(2,1)S(1)}, u32[]{:S(2)}, u32[]{:S(2)}) collective-permute-start(bf16[528,384]{1,0:T(8,128)(2,1)} %get-tuple-element.40), channel_id=1, source_target_pairs={{0,2},{1,3},{2,0},{3,1},{4,6},{5,7},{6,4},{7,5},{8,10},{9,11},{10,... | collective-permute-start | bytes 1216520 | tf_op jit(solution)/shard_map/ppermute | solution.py:243
  11.5 3.0 %collective-permute-start.6 = (bf16[272,384]{1,0:T(8,128)(2,1)S(1)}, bf16[272,384]{1,0:T(8,128)(2,1)S(1)}, u32[]{:S(2)}, u32[]{:S(2)}) collective-permute-start(bf16[272,384]{1,0:T(8,128)(2,1)S(1)} %copy-done.6), channel_id=1, source_target_pairs={{0,4},{1,5},{2,6},{3,7},{4,0},{5,1},{6,2},{7,3},{8,12},{9,13},{10,... | collective-permute-start | bytes 626696 | tf_op jit(solution)/shard_map/ppermute | solution.py:243
  14.5 1.3 %collective-permute-start.7 = (bf16[272,384]{1,0:T(8,128)(2,1)S(1)}, bf16[272,384]{1,0:T(8,128)(2,1)S(1)}, u32[]{:S(2)}, u32[]{:S(2)}) collective-permute-start(bf16[272,384]{1,0:T(8,128)(2,1)S(1)} %copy-done.5), channel_id=1, source_target_pairs={{0,5},{1,4},{2,7},{3,6},{4,1},{5,0},{6,3},{7,2},{8,13},{9,12},{10,... | collective-permute-start | bytes 626696 | tf_op jit(solution)/shard_map/ppermute | solution.py:243
  15.8 7.3 %collective-permute-done.refs_1_ = bf16[528,384]{1,0:T(8,128)(2,1)S(1)} collective-permute-done((bf16[528,384]{1,0:T(8,128)(2,1)}, bf16[528,384]{1,0:T(8,128)(2,1)S(1)}, u32[]{:S(2)}, u32[]{:S(2)}) %collective-permute-start) | collective-permute-done | bytes 405536 | tf_op jit(solution)/shard_map/ppermute | solution.py:243
  23.1 2.6 %collective-permute-start.8 = (bf16[272,384]{1,0:T(8,128)(2,1)S(1)}, bf16[272,384]{1,0:T(8,128)(2,1)S(1)}, u32[]{:S(2)}, u32[]{:S(2)}) collective-permute-start(bf16[272,384]{1,0:T(8,128)(2,1)S(1)} %copy-done.4), channel_id=1, source_target_pairs={{0,6},{1,7},{2,4},{3,5},{4,2},{5,3},{6,0},{7,1},{8,14},{9,15},{10,... | collective-permute-start | bytes 626696 | tf_op jit(solution)/shard_map/ppermute | solution.py:243
  25.7 5.7 %collective-permute-done.1.refs_2_ = bf16[528,384]{1,0:T(8,128)(2,1)S(1)} collective-permute-done((bf16[528,384]{1,0:T(8,128)(2,1)}, bf16[528,384]{1,0:T(8,128)(2,1)S(1)}, u32[]{:S(2)}, u32[]{:S(2)}) %collective-permute-start.1) | collective-permute-done | bytes 405536 | tf_op jit(solution)/shard_map/ppermute | solution.py:243
  31.4 3.5 %collective-permute-start.9 = (bf16[272,384]{1,0:T(8,128)(2,1)S(1)}, bf16[272,384]{1,0:T(8,128)(2,1)S(1)}, u32[]{:S(2)}, u32[]{:S(2)}) collective-permute-start(bf16[272,384]{1,0:T(8,128)(2,1)S(1)} %copy-done.3), channel_id=1, source_target_pairs={{0,7},{1,6},{2,5},{3,4},{4,3},{5,2},{6,1},{7,0},{8,15},{9,14},{10,... | collective-permute-start | bytes 626696 | tf_op jit(solution)/shard_map/ppermute | solution.py:243
  35.0 0.6 reshape.18.index
  35.6 0.1 copy.18
  35.7 0.7 reshape.19.bias
  36.4 1.8 %shard_map.120 = (f32[96]{0:T(128)}, s32[32]{0:T(128)}) custom-call(f32[768]{0:T(1024)} %reshape.19.bias, s32[64]{0:T(128)} %reshape.18.index, s32[8]{0:T(128)} %count.1), custom_call_target="tpu_custom_call" | custom-call | tf_op jit(solution)/shard_map/pallas_call | solution.py:253
  38.2 0.3 collective-permute-done.2.refs_3_
  38.4 0.7 copy-done.2
  39.2 5.5 %shard_map.123 = (bf16[144,384]{1,0:T(8,128)(2,1)}, bf16[144,384]{1,0:T(8,128)(2,1)}, bf16[144,384]{1,0:T(8,128)(2,1)}, bf16[144,384]{1,0:T(8,128)(2,1)}, f32[512,384]{1,0:T(8,128)}, /*index=5*/f32[512,384]{1,0:T(8,128)}) custom-call(f32[96]{0:T(128)} %get-tuple-element.32.bias, s32[32]{0:T(128)} %get-tuple-element.33.mask, ...), custom_call_target="tpu_custom_call" | custom-call | tf_op jit(solution)/shard_map/pallas_call | solution.py:268
  44.6 1.7 %collective-permute-start.3 = (bf16[144,384]{1,0:T(8,128)(2,1)}, bf16[144,384]{1,0:T(8,128)(2,1)S(1)}, u32[]{:S(2)}, u32[]{:S(2)}) collective-permute-start(bf16[144,384]{1,0:T(8,128)(2,1)} %get-tuple-element.43), channel_id=1, source_target_pairs={{0,1},{1,0},{2,3},{3,2},{4,5},{5,4},{6,7},{7,6},{8,9},{9,8},{10,11... | collective-permute-start | bytes 331784 | tf_op jit(solution)/shard_map/ppermute | solution.py:243
  46.4 0.0 copy-start.8
  46.4 1.8 %collective-permute-start.5 = (bf16[144,384]{1,0:T(8,128)(2,1)}, bf16[144,384]{1,0:T(8,128)(2,1)S(1)}, u32[]{:S(2)}, u32[]{:S(2)}) collective-permute-start(bf16[144,384]{1,0:T(8,128)(2,1)} %get-tuple-element.45), channel_id=1, source_target_pairs={{0,3},{1,2},{2,1},{3,0},{4,7},{5,6},{6,5},{7,4},{8,11},{9,10},{10,... | collective-permute-start | bytes 331784 | tf_op jit(solution)/shard_map/ppermute | solution.py:243
  48.2 1.7 %collective-permute-done.9.refs_7_ = bf16[272,384]{1,0:T(8,128)(2,1)S(1)} collective-permute-done((bf16[272,384]{1,0:T(8,128)(2,1)S(1)}, bf16[272,384]{1,0:T(8,128)(2,1)S(1)}, u32[]{:S(2)}, u32[]{:S(2)}) %collective-permute-start.9) | collective-permute-done | bytes 208928 | tf_op jit(solution)/shard_map/ppermute | solution.py:243
  49.8 0.7 copy-done.10
  50.5 6.4 %shard_map.124 = (bf16[144,384]{1,0:T(8,128)(2,1)}, bf16[144,384]{1,0:T(8,128)(2,1)}, bf16[144,384]{1,0:T(8,128)(2,1)}, bf16[144,384]{1,0:T(8,128)(2,1)}, bf16[2...) custom-call(f32[96]{0:T(128)} %get-tuple-element.32.bias, ...), custom_call_target="tpu_custom_call" | custom-call | tf_op jit(solution)/shard_map/pallas_call | solution.py:268
  56.9 8.6 %collective-permute-start.10 = (bf16[144,384]{1,0:T(8,128)(2,1)}, bf16[144,384]{1,0:T(8,128)(2,1)S(1)}, u32[]{:S(2)}, u32[]{:S(2)}) collective-permute-start(bf16[144,384]{1,0:T(8,128)(2,1)} %get-tuple-element.48), channel_id=1, source_target_pairs={{0,4},{1,5},{2,6},{3,7},{4,0},{5,1},{6,2},{7,3},{8,12},{9,13},{10,... | collective-permute-start | bytes 331784 | tf_op jit(solution)/shard_map/ppermute | solution.py:243
  65.5 0.8 collective-permute-start.11
  66.3 4.2 %collective-permute-start.12 = (bf16[144,384]{1,0:T(8,128)(2,1)}, bf16[144,384]{1,0:T(8,128)(2,1)S(1)}, u32[]{:S(2)}, u32[]{:S(2)}) collective-permute-start(bf16[144,384]{1,0:T(8,128)(2,1)} %get-tuple-element.50), channel_id=1, source_target_pairs={{0,6},{1,7},{2,4},{3,5},{4,2},{5,3},{6,0},{7,1},{8,14},{9,15},{10,... | collective-permute-start | bytes 331784 | tf_op jit(solution)/shard_map/ppermute | solution.py:243
  70.5 0.2 collective-permute-start.13
  70.8 1.3 %collective-permute-start.14 = (bf16[256,384]{1,0:T(8,128)(2,1)}, bf16[256,384]{1,0:T(8,128)(2,1)S(1)}, u32[]{:S(2)}, u32[]{:S(2)}) collective-permute-start(bf16[256,384]{1,0:T(8,128)(2,1)} %get-tuple-element.54), channel_id=1, source_target_pairs={{0,1},{1,0},{2,3},{3,2},{4,5},{5,4},{6,7},{7,6},{8,9},{9,8},{10,11... | collective-permute-start | bytes 589832 | tf_op jit(solution)/shard_map/ppermute | solution.py:243
  72.1 3.6 %collective-permute-done.10.refs_4_ = bf16[144,384]{1,0:T(8,128)(2,1)S(1)} collective-permute-done((bf16[144,384]{1,0:T(8,128)(2,1)}, bf16[144,384]{1,0:T(8,128)(2,1)S(1)}, u32[]{:S(2)}, u32[]{:S(2)}) %collective-permute-start.10) | collective-permute-done | bytes 110624 | tf_op jit(solution)/shard_map/ppermute | solution.py:243
  75.7 4.2 %collective-permute-done.11.refs_5_ = bf16[144,384]{1,0:T(8,128)(2,1)S(1)} collective-permute-done((bf16[144,384]{1,0:T(8,128)(2,1)}, bf16[144,384]{1,0:T(8,128)(2,1)S(1)}, u32[]{:S(2)}, u32[]{:S(2)}) %collective-permute-start.11) | collective-permute-done | bytes 110624 | tf_op jit(solution)/shard_map/ppermute | solution.py:243
  80.0 0.7 copy-done.24
  80.6 0.6 dynamic-slice
  81.9 0.6 copy-done.19
  82.5 0.1 copy-done.20
  82.5 2.2 %shard_map.125 = (bf16[1,128,1536]{2,1,0:T(8,128)(2,1)}, f32[1,96]{1,0:T(1,128)}) custom-call(s32[64]{0:T(128)} %reshape.18.index, bf16[144,384]{1,0:T(8,128)(2,1)} %get-tuple-element.42.refs_0_, bf16[144,384]{1,0:T(8,128)(2,1)} %copy-done.14, bf16[144,384]{1,0:T(8,128)(2,1)} %copy-done.15, bf16[144,384]{1,0:T(8,128)(2,1)} %copy-done.16, ...), custom_call_target="tpu_custom_call" | custom-call | tf_op jit(solution)/shard_map/pallas_call | solution.py:291
  84.8 0.5 broadcast.3
  85.3 0.2 copy-done.23
  85.4 0.7 reduce.3
  86.1 0.1 reshape.20
  86.2 0.1 copy.20
  86.3 5.6 %all-reduce = f32[1,12,8]{1,0,2:T(1,128)S(1)} all-reduce(f32[1,12,8]{1,0,2:T(1,128)S(1)} %copy.20), channel_id=2, replica_groups=mesh['cell'=4,'gene'=8] {'cell'}, use_global_device_ids=true, to_apply=%region_0.0.clone | all-reduce | flops 96 | bytes 768
  91.9 0.6 constant_dynamic-slice_fusion
  92.5 0.6 copy-done.11
  93.2 0.1 copy-done.12
  93.2 0.1 copy-done.13
  93.3 2.2 %shard_map.126 = (bf16[1,128,1536]{2,1,0:T(8,128)(2,1)}, bf16[1,128,1536]{2,1,0:T(8,128)(2,1)}) custom-call(bf16[256,384]{1,0:T(8,128)(2,1)} %get-tuple-element.53.refs_0_, bf16[256,384]{1,0:T(8,128)(2,1)} %copy-done.11, bf16[256,384]{1,0:T(8,128)(2,1)} %copy-done.12, bf16[256,384]{1,0:T(8,128)(2,1)} %copy-done.13), custom_call_target="tpu_custom_call" | custom-call | tf_op jit(solution)/shard_map/pallas_call | solution.py:298
  (54 shorter events, 0.1 us)
Async XLA Ops:
  4.3 7.3 %copy-start.6 = (bf16[272,384]{1,0:T(8,128)(2,1)S(1)}, bf16[272,384]{1,0:T(8,128)(2,1)}, u32[]{:S(2)}) copy-start(bf16[272,384]{1,0:T(8,128)(2,1)} %get-tuple-element.34.refs_0_) | copy-start | bytes 626692
  4.3 10.3 %copy-start.5 = (bf16[272,384]{1,0:T(8,128)(2,1)S(1)}, bf16[272,384]{1,0:T(8,128)(2,1)}, u32[]{:S(2)}) copy-start(bf16[272,384]{1,0:T(8,128)(2,1)} %get-tuple-element.35.refs_1_) | copy-start | bytes 626692
  4.3 18.9 %copy-start.4 = (bf16[272,384]{1,0:T(8,128)(2,1)S(1)}, bf16[272,384]{1,0:T(8,128)(2,1)}, u32[]{:S(2)}) copy-start(bf16[272,384]{1,0:T(8,128)(2,1)} %get-tuple-element.36.refs_2_) | copy-start | bytes 626692
  4.3 27.2 %copy-start.3 = (bf16[272,384]{1,0:T(8,128)(2,1)S(1)}, bf16[272,384]{1,0:T(8,128)(2,1)}, u32[]{:S(2)}) copy-start(bf16[272,384]{1,0:T(8,128)(2,1)} %get-tuple-element.37.refs_3_) | copy-start | bytes 626692
  4.3 31.3 %copy-start.21 = (f32[8,12,8]{1,2,0:T(8,128)S(1)}, f32[8,12,8]{1,2,0:T(8,128)}, u32[]{:S(2)}) copy-start(f32[8,12,8]{1,2,0:T(8,128)} %param.15) | copy-start | bytes 9220
  7.0 28.0 %copy-start.22 = (s32[8,8]{1,0:T(8,128)S(1)}, s32[8,8]{1,0:T(8,128)}, u32[]{:S(2)}) copy-start(s32[8,8]{1,0:T(8,128)} %param.16) | copy-start | bytes 772
  7.0 16.1 %collective-permute-start = (bf16[528,384]{1,0:T(8,128)(2,1)}, bf16[528,384]{1,0:T(8,128)(2,1)S(1)}, u32[]{:S(2)}, u32[]{:S(2)}) collective-permute-start(bf16[528,384]{1,0:T(8,128)(2,1)} %get-tuple-element.39), channel_id=1, source_target_pairs={{0,1},{1,0},{2,3},{3,2},{4,5},{5,4},{6,7},{7,6},{8,9},{9,8},{10,11... | collective-permute-start | bytes 1216520 | tf_op jit(solution)/shard_map/ppermute | solution.py:243
  10.0 21.5 %collective-permute-start.1 = (bf16[528,384]{1,0:T(8,128)(2,1)}, bf16[528,384]{1,0:T(8,128)(2,1)S(1)}, u32[]{:S(2)}, u32[]{:S(2)}) collective-permute-start(bf16[528,384]{1,0:T(8,128)(2,1)} %get-tuple-element.40), channel_id=1, source_target_pairs={{0,2},{1,3},{2,0},{3,1},{4,6},{5,7},{6,4},{7,5},{8,10},{9,11},{10,... | collective-permute-start | bytes 1216520 | tf_op jit(solution)/shard_map/ppermute | solution.py:243
  11.5 26.9 %collective-permute-start.2 = (bf16[528,384]{1,0:T(8,128)(2,1)}, bf16[528,384]{1,0:T(8,128)(2,1)S(1)}, u32[]{:S(2)}, u32[]{:S(2)}) collective-permute-start(bf16[528,384]{1,0:T(8,128)(2,1)} %get-tuple-element.41), channel_id=1, source_target_pairs={{0,3},{1,2},{2,1},{3,0},{4,7},{5,6},{6,5},{7,4},{8,11},{9,10},{10,... | collective-permute-start | bytes 1216520 | tf_op jit(solution)/shard_map/ppermute | solution.py:243
  11.5 34.8 %collective-permute-start.6 = (bf16[272,384]{1,0:T(8,128)(2,1)S(1)}, bf16[272,384]{1,0:T(8,128)(2,1)S(1)}, u32[]{:S(2)}, u32[]{:S(2)}) collective-permute-start(bf16[272,384]{1,0:T(8,128)(2,1)S(1)} %copy-done.6), channel_id=1, source_target_pairs={{0,4},{1,5},{2,6},{3,7},{4,0},{5,1},{6,2},{7,3},{8,12},{9,13},{10,... | collective-permute-start | bytes 626696 | tf_op jit(solution)/shard_map/ppermute | solution.py:243
  14.5 31.8 %collective-permute-start.7 = (bf16[272,384]{1,0:T(8,128)(2,1)S(1)}, bf16[272,384]{1,0:T(8,128)(2,1)S(1)}, u32[]{:S(2)}, u32[]{:S(2)}) collective-permute-start(bf16[272,384]{1,0:T(8,128)(2,1)S(1)} %copy-done.5), channel_id=1, source_target_pairs={{0,5},{1,4},{2,7},{3,6},{4,1},{5,0},{6,3},{7,2},{8,13},{9,12},{10,... | collective-permute-start | bytes 626696 | tf_op jit(solution)/shard_map/ppermute | solution.py:243
  23.1 15.3 %copy-start = (bf16[528,384]{1,0:T(8,128)(2,1)}, bf16[528,384]{1,0:T(8,128)(2,1)S(1)}, u32[]{:S(2)}) copy-start(bf16[528,384]{1,0:T(8,128)(2,1)S(1)} %collective-permute-done.refs_1_) | copy-start | bytes 1216516
  23.1 25.0 %collective-permute-start.8 = (bf16[272,384]{1,0:T(8,128)(2,1)S(1)}, bf16[272,384]{1,0:T(8,128)(2,1)S(1)}, u32[]{:S(2)}, u32[]{:S(2)}) collective-permute-start(bf16[272,384]{1,0:T(8,128)(2,1)S(1)} %copy-done.4), channel_id=1, source_target_pairs={{0,6},{1,7},{2,4},{3,5},{4,2},{5,3},{6,0},{7,1},{8,14},{9,15},{10,... | collective-permute-start | bytes 626696 | tf_op jit(solution)/shard_map/ppermute | solution.py:243
  31.4 7.0 %copy-start.1 = (bf16[528,384]{1,0:T(8,128)(2,1)}, bf16[528,384]{1,0:T(8,128)(2,1)S(1)}, u32[]{:S(2)}) copy-start(bf16[528,384]{1,0:T(8,128)(2,1)S(1)} %collective-permute-done.1.refs_2_) | copy-start | bytes 1216516
  31.4 18.4 %collective-permute-start.9 = (bf16[272,384]{1,0:T(8,128)(2,1)S(1)}, bf16[272,384]{1,0:T(8,128)(2,1)S(1)}, u32[]{:S(2)}, u32[]{:S(2)}) collective-permute-start(bf16[272,384]{1,0:T(8,128)(2,1)S(1)} %copy-done.3), channel_id=1, source_target_pairs={{0,7},{1,6},{2,5},{3,4},{4,3},{5,2},{6,1},{7,0},{8,15},{9,14},{10,... | collective-permute-start | bytes 626696 | tf_op jit(solution)/shard_map/ppermute | solution.py:243
  38.4 0.8 copy-start.2
  44.6 21.7 %collective-permute-start.3 = (bf16[144,384]{1,0:T(8,128)(2,1)}, bf16[144,384]{1,0:T(8,128)(2,1)S(1)}, u32[]{:S(2)}, u32[]{:S(2)}) collective-permute-start(bf16[144,384]{1,0:T(8,128)(2,1)} %get-tuple-element.43), channel_id=1, source_target_pairs={{0,1},{1,0},{2,3},{3,2},{4,5},{5,4},{6,7},{7,6},{8,9},{9,8},{10,11... | collective-permute-start | bytes 331784 | tf_op jit(solution)/shard_map/ppermute | solution.py:243
  46.3 3.5 %copy-start.7 = (bf16[272,384]{1,0:T(8,128)(2,1)}, bf16[272,384]{1,0:T(8,128)(2,1)S(1)}, u32[]{:S(2)}) copy-start(bf16[272,384]{1,0:T(8,128)(2,1)S(1)} %collective-permute-done.6.refs_4_) | copy-start | bytes 626692
  46.3 24.2 %collective-permute-start.4 = (bf16[144,384]{1,0:T(8,128)(2,1)}, bf16[144,384]{1,0:T(8,128)(2,1)S(1)}, u32[]{:S(2)}, u32[]{:S(2)}) collective-permute-start(bf16[144,384]{1,0:T(8,128)(2,1)} %get-tuple-element.44), channel_id=1, source_target_pairs={{0,2},{1,3},{2,0},{3,1},{4,6},{5,7},{6,4},{7,5},{8,10},{9,11},{10,... | collective-permute-start | bytes 331784 | tf_op jit(solution)/shard_map/ppermute | solution.py:243
  46.4 3.5 %copy-start.8 = (bf16[272,384]{1,0:T(8,128)(2,1)}, bf16[272,384]{1,0:T(8,128)(2,1)S(1)}, u32[]{:S(2)}) copy-start(bf16[272,384]{1,0:T(8,128)(2,1)S(1)} %collective-permute-done.7.refs_5_) | copy-start | bytes 626692
  46.4 24.4 %collective-permute-start.5 = (bf16[144,384]{1,0:T(8,128)(2,1)}, bf16[144,384]{1,0:T(8,128)(2,1)S(1)}, u32[]{:S(2)}, u32[]{:S(2)}) collective-permute-start(bf16[144,384]{1,0:T(8,128)(2,1)} %get-tuple-element.45), channel_id=1, source_target_pairs={{0,3},{1,2},{2,1},{3,0},{4,7},{5,6},{6,5},{7,4},{8,11},{9,10},{10,... | collective-permute-start | bytes 331784 | tf_op jit(solution)/shard_map/ppermute | solution.py:243
  48.2 1.7 %copy-start.9 = (bf16[272,384]{1,0:T(8,128)(2,1)}, bf16[272,384]{1,0:T(8,128)(2,1)S(1)}, u32[]{:S(2)}) copy-start(bf16[272,384]{1,0:T(8,128)(2,1)S(1)} %collective-permute-done.8.refs_6_) | copy-start | bytes 626692
  49.8 0.7 copy-start.10
  56.9 18.8 %collective-permute-start.10 = (bf16[144,384]{1,0:T(8,128)(2,1)}, bf16[144,384]{1,0:T(8,128)(2,1)S(1)}, u32[]{:S(2)}, u32[]{:S(2)}) collective-permute-start(bf16[144,384]{1,0:T(8,128)(2,1)} %get-tuple-element.48), channel_id=1, source_target_pairs={{0,4},{1,5},{2,6},{3,7},{4,0},{5,1},{6,2},{7,3},{8,12},{9,13},{10,... | collective-permute-start | bytes 331784 | tf_op jit(solution)/shard_map/ppermute | solution.py:243
  65.5 14.5 %collective-permute-start.11 = (bf16[144,384]{1,0:T(8,128)(2,1)}, bf16[144,384]{1,0:T(8,128)(2,1)S(1)}, u32[]{:S(2)}, u32[]{:S(2)}) collective-permute-start(bf16[144,384]{1,0:T(8,128)(2,1)} %get-tuple-element.49), channel_id=1, source_target_pairs={{0,5},{1,4},{2,7},{3,6},{4,1},{5,0},{6,3},{7,2},{8,13},{9,12},{10,... | collective-permute-start | bytes 331784 | tf_op jit(solution)/shard_map/ppermute | solution.py:243
  66.3 15.6 %copy-start.14 = (bf16[144,384]{1,0:T(8,128)(2,1)}, bf16[144,384]{1,0:T(8,128)(2,1)S(1)}, u32[]{:S(2)}) copy-start(bf16[144,384]{1,0:T(8,128)(2,1)S(1)} %collective-permute-done.3.refs_1_) | copy-start | bytes 331780
  66.3 15.5 %collective-permute-start.12 = (bf16[144,384]{1,0:T(8,128)(2,1)}, bf16[144,384]{1,0:T(8,128)(2,1)S(1)}, u32[]{:S(2)}, u32[]{:S(2)}) collective-permute-start(bf16[144,384]{1,0:T(8,128)(2,1)} %get-tuple-element.50), channel_id=1, source_target_pairs={{0,6},{1,7},{2,4},{3,5},{4,2},{5,3},{6,0},{7,1},{8,14},{9,15},{10,... | collective-permute-start | bytes 331784 | tf_op jit(solution)/shard_map/ppermute | solution.py:243
  70.5 11.3 %copy-start.15 = (bf16[144,384]{1,0:T(8,128)(2,1)}, bf16[144,384]{1,0:T(8,128)(2,1)S(1)}, u32[]{:S(2)}) copy-start(bf16[144,384]{1,0:T(8,128)(2,1)S(1)} %collective-permute-done.4.refs_2_) | copy-start | bytes 331780
  70.5 11.3 %collective-permute-start.13 = (bf16[144,384]{1,0:T(8,128)(2,1)}, bf16[144,384]{1,0:T(8,128)(2,1)S(1)}, u32[]{:S(2)}, u32[]{:S(2)}) collective-permute-start(bf16[144,384]{1,0:T(8,128)(2,1)} %get-tuple-element.51), channel_id=1, source_target_pairs={{0,7},{1,6},{2,5},{3,4},{4,3},{5,2},{6,1},{7,0},{8,15},{9,14},{10,... | collective-permute-start | bytes 331784 | tf_op jit(solution)/shard_map/ppermute | solution.py:243
  70.8 11.1 %copy-start.16 = (bf16[144,384]{1,0:T(8,128)(2,1)}, bf16[144,384]{1,0:T(8,128)(2,1)S(1)}, u32[]{:S(2)}) copy-start(bf16[144,384]{1,0:T(8,128)(2,1)S(1)} %collective-permute-done.5.refs_3_) | copy-start | bytes 331780
  70.8 21.7 %collective-permute-start.14 = (bf16[256,384]{1,0:T(8,128)(2,1)}, bf16[256,384]{1,0:T(8,128)(2,1)S(1)}, u32[]{:S(2)}, u32[]{:S(2)}) collective-permute-start(bf16[256,384]{1,0:T(8,128)(2,1)} %get-tuple-element.54), channel_id=1, source_target_pairs={{0,1},{1,0},{2,3},{3,2},{4,5},{5,4},{6,7},{7,6},{8,9},{9,8},{10,11... | collective-permute-start | bytes 589832 | tf_op jit(solution)/shard_map/ppermute | solution.py:243
  75.7 6.2 %copy-start.17 = (bf16[144,384]{1,0:T(8,128)(2,1)}, bf16[144,384]{1,0:T(8,128)(2,1)S(1)}, u32[]{:S(2)}) copy-start(bf16[144,384]{1,0:T(8,128)(2,1)S(1)} %collective-permute-done.10.refs_4_) | copy-start | bytes 331780
  75.7 16.8 %collective-permute-start.15 = (bf16[256,384]{1,0:T(8,128)(2,1)}, bf16[256,384]{1,0:T(8,128)(2,1)S(1)}, u32[]{:S(2)}, u32[]{:S(2)}) collective-permute-start(bf16[256,384]{1,0:T(8,128)(2,1)} %get-tuple-element.55), channel_id=1, source_target_pairs={{0,2},{1,3},{2,0},{3,1},{4,6},{5,7},{6,4},{7,5},{8,10},{9,11},{10,... | collective-permute-start | bytes 589832 | tf_op jit(solution)/shard_map/ppermute | solution.py:243
  79.9 2.0 %copy-start.18 = (bf16[144,384]{1,0:T(8,128)(2,1)}, bf16[144,384]{1,0:T(8,128)(2,1)S(1)}, u32[]{:S(2)}) copy-start(bf16[144,384]{1,0:T(8,128)(2,1)S(1)} %collective-permute-done.11.refs_5_) | copy-start | bytes 331780
  79.9 12.6 %collective-permute-start.16 = (bf16[256,384]{1,0:T(8,128)(2,1)}, bf16[256,384]{1,0:T(8,128)(2,1)S(1)}, u32[]{:S(2)}, u32[]{:S(2)}) collective-permute-start(bf16[256,384]{1,0:T(8,128)(2,1)} %get-tuple-element.56), channel_id=1, source_target_pairs={{0,3},{1,2},{2,1},{3,0},{4,7},{5,6},{6,5},{7,4},{8,11},{9,10},{10,... | collective-permute-start | bytes 589832 | tf_op jit(solution)/shard_map/ppermute | solution.py:243
  79.9 0.7 copy-start.24
  81.8 0.6 copy-start.19
  81.9 0.7 copy-start.20
  84.8 0.7 copy-start.23
  92.5 0.7 copy-start.11
  92.5 0.7 copy-start.12
  92.5 0.8 copy-start.13
where the time goes:
time: 95.9 us; the launch traced here: 95.5 us
  starting transfers between devices  33.7 us (35%)
  Pallas kernels  23 us (24%)
  waiting for transfers between devices  22.8 us (24%)
  local copies, waits for them, and re-layouts  8.21 us (9%)
  blocking collectives  5.64 us (6%)
  between operations  1.47 us (2%)
    ppermute x17, starting transfers between devices, move(): return lax.ppermute(array, 'gene', [(i, i ^ hop) for i in range(blocks)])  33.7 us
    ppermute x17, waiting for transfers between devices, move(): return lax.ppermute(array, 'gene', [(i, i ^ hop) for i in range(blocks)])  22.8 us
    pallas_call x2, Pallas kernels, stage(): call(functools.partial(stage_kernel, plan, first, last), outs, scratch=[s...  11.8 us
    unnamed x54, local copies, waits for them, and re-layouts  6.26 us
    unnamed x1, blocking collectives  5.64 us
    pallas_call x1, Pallas kernels, shards(): call(functools.partial(pack_near_kernel, plan), [near] * members, count=2...  2.7 us
    pallas_call x1, Pallas kernels, shards(): call(functools.partial(pack_far_kernel, plan), [far] * members, count=4)  2.34 us
    pallas_call x1, Pallas kernels, shards(): call(functools.partial(query_kernel, plan), [whole, jax.ShapeDtypeStruct(...  2.23 us
  transfers between devices with their start and end apart: 17, of which 6 were waited for; matrix products, arithmetic and copies ran while one was open for 4% of the time, Pallas kernels for 17%

commit v1 on v0

v1 whole, which is shorter than its diff:
```python
import functools
import math

import jax
import jax.numpy as jnp
from jax import lax
from jax.experimental import pallas as pl
from jax.experimental.pallas import tpu as pltpu
from jax.sharding import PartitionSpec as P

BLOCK = 128
ROW_TILE = 16
VMEM_LIMIT = 60 * 1024 * 1024
STAGE_LIMIT = 40 * 1024 * 1024
FAR_STAGES = 1
LOG2E = math.log2(math.e)
UNLISTED = -1e30


def split_two(row):
    high = row.astype(jnp.bfloat16).astype(jnp.float32)
    return [high, row - high]


def pack_kernel(plan, query, key, value, output, grad, lse, *outs):
    members, share, head_size = plan["members"], plan["share"], plan["head_size"]
    width, stat_rows = share * head_size, plan["stat_rows"]
    mine = lax.axis_index("gene") % members
    for hop in range(members):
        owner = mine ^ hop
        near, far = outs[members].at[owner], outs[hop]
        start = pl.multiple_of(owner * width, head_size)
        rows = []
        for head in range(share):
            columns = pl.ds(start + head * head_size, head_size)
            query_part, grad_part = query[0, :, columns], grad[0, :, columns]
            products = grad_part.astype(jnp.float32) * output[0, :, columns].astype(jnp.float32)
            top = 2 * BLOCK * head
            far[top : top + BLOCK, :] = query_part
            far[top + BLOCK : top + 2 * BLOCK, :] = grad_part
            top = 4 * BLOCK * head
            near[top : top + BLOCK, :] = query_part
            near[top + BLOCK : top + 2 * BLOCK, :] = grad_part
            near[top + 2 * BLOCK : top + 3 * BLOCK, :] = key[0, :, columns]
            near[top + 3 * BLOCK : top + 4 * BLOCK, :] = value[0, :, columns]
            delta = jnp.sum(jnp.transpose(products), axis=0, keepdims=True)
            rows += split_two(lse[owner * share + head]) + split_two(delta)
        rows.append(jnp.zeros((stat_rows - 4 * share, BLOCK), jnp.float32))
        stats = jnp.concatenate(rows, axis=0).astype(jnp.bfloat16)
        far[2 * BLOCK * share : 2 * BLOCK * share + stat_rows, :] = stats
        near[4 * BLOCK * share : 4 * BLOCK * share + stat_rows, :] = stats


def table_kernel(plan, bias, index, count, shift):
    members, share, blocks = plan["members"], plan["share"], plan["blocks"]
    heads = members * share
    me = lax.axis_index("gene")
    mine = me % members
    for place in range(blocks):
        row = me ^ place
        for at in range(members * share):
            shift[place * members * share + at] = UNLISTED

        def listed(slot, carry, place=place, row=row):
            side = index[row * blocks + slot] ^ me

            @pl.when(side < members)
            def _():
                for head in range(share):
                    shift[(place * members + side) * share + head] = LOG2E * bias[
                        (row * heads + mine * share + head) * blocks + slot
                    ]

            return carry

        lax.fori_loop(0, count[row], listed, 0)


def stage_kernel(plan, places, first, last, shift, *refs):
    members, share, scale = plan["members"], plan["share"], plan["scale"]
    count = len(places)
    mine = lax.axis_index("gene") % members
    near, rest = [refs[0].at[mine ^ hop] for hop in range(members)], refs[1:]
    fresh = [place for place in places if place >= members]
    pieces = [near[place] for place in places if place < members] + list(rest[: len(fresh)])
    steps = [(4 if place < members else 2) * BLOCK for place in places]
    rest = rest[len(fresh) :]
    before = None
    if not first:
        before, rest = rest[:2], rest[2:]
    outs, rest = rest[:count], rest[count:]
    if last:
        owned, rest = rest[:members], rest[members:]
    else:
        after, rest = rest[:2], rest[2:]
    weights_low, grads_low, sums = rest
    nt = (((1,), (1,)), ((), ()))
    nn = (((1,), (0,)), ((), ()))
    tn = (((0,), (0,)), ((), ()))
    dot = functools.partial(lax.dot_general, preferred_element_type=jnp.float32)
    stats = [
        piece[step * share : step * share + plan["stat_rows"], :].astype(jnp.float32)
        for piece, step in zip(pieces, steps)
    ]
    wide = 2 if count % 2 == 0 else 1
    total_rows = share * members
    if plan["sum_rows"] > total_rows:
        for at in range(count):
            sums[at, total_rows:, :] = jnp.zeros((plan["sum_rows"] - total_rows, BLOCK), jnp.float32)

    def own(side, head, which):
        top = 4 * BLOCK * head + (2 + which) * BLOCK
        return near[side][top : top + BLOCK, :]

    def rows(at, head, which):
        top = steps[at] * head + which * BLOCK
        return pieces[at][top : top + BLOCK, :]

    for head in range(share):
        for group in range(0, count, wide):
            ats = range(group, group + wide)
            queries = jnp.concatenate([rows(at, head, 0) for at in ats], axis=0)
            grads = jnp.concatenate([rows(at, head, 1) for at in ats], axis=0)
            line = jnp.concatenate([stats[at][4 * head : 4 * head + 4] for at in ats], axis=1)
            saved = (line[0:1] + line[1:2]) * LOG2E
            delta = line[2:3] + line[3:4]
            spot = slice(group * BLOCK, (group + wide) * BLOCK)
            for side in range(members):
                part = slice(side * BLOCK, (side + 1) * BLOCK)
                scores = dot(own(side, head, 0), queries, nt)
                weight_grads = dot(own(side, head, 1), grads, nt)
                shifts = [
                    jnp.full((1, BLOCK), shift[(places[at] * members + side) * share + head])
                    for at in ats
                ]
                offset = jnp.concatenate(shifts, axis=1) - saved
                weights = jnp.exp2(scores * (scale * LOG2E) + offset)
                score_grads = weights * (weight_grads - delta)
                weights_low[part, spot] = weights.astype(jnp.bfloat16)
                grads_low[part, spot] = score_grads.astype(jnp.bfloat16)
                column_sums = jnp.sum(score_grads, axis=0, keepdims=True)
                row = head * members + side
                for at in ats:
                    lanes = slice((at - group) * BLOCK, (at - group + 1) * BLOCK)
                    sums[at, row : row + 1, :] = column_sums[:, lanes]
        keys = jnp.concatenate([own(side, head, 0) for side in range(members)], axis=0)
        queries = jnp.concatenate([rows(at, head, 0) for at in range(count)], axis=0)
        grads = jnp.concatenate([rows(at, head, 1) for at in range(count)], axis=0)
        query_grad = dot(grads_low[...], keys, tn) * scale
        for at in range(count):
            outs[at][head * BLOCK : (head + 1) * BLOCK, :] = query_grad[
                at * BLOCK : (at + 1) * BLOCK
            ].astype(jnp.bfloat16)
        value_grad = dot(weights_low[...], grads, nn)
        key_grad = dot(grads_low[...], queries, nn)
        if before is not None:
            key_grad = key_grad + before[0][head]
            value_grad = value_grad + before[1][head]
        if last:
            key_grad = key_grad * scale
            top = 2 * BLOCK * head
            for side in range(members):
                part = slice(side * BLOCK, (side + 1) * BLOCK)
                owned[side][top : top + BLOCK, :] = key_grad[part].astype(jnp.bfloat16)
                owned[side][top + BLOCK : top + 2 * BLOCK, :] = value_grad[part].astype(jnp.bfloat16)
        else:
            after[0][head] = key_grad
            after[1][head] = value_grad
    lane = lax.broadcasted_iota(jnp.int32, (plan["sum_rows"], BLOCK), 1)
    for at in range(count):
        total = jnp.sum(sums[at], axis=1, keepdims=True)
        high, low = split_two(total)
        middle, low = split_two(low)
        spread = jnp.where(lane == 1, middle, jnp.where(lane == 2, low, 0.0))
        spread = jnp.where(lane == 0, high, spread)
        outs[at][share * BLOCK : share * BLOCK + plan["sum_rows"], :] = spread.astype(jnp.bfloat16)


def query_kernel(plan, index, *refs):
    blocks, members, share = plan["blocks"], plan["members"], plan["share"]
    head_size, cells = plan["head_size"], plan["cells"]
    heads, per_cell = members * share, blocks // cells
    pieces, query_grad, parts = refs[:blocks], refs[blocks], refs[blocks + 1 : blocks + 1 + cells]
    slots, sums, table = refs[blocks + 1 + cells :]
    me, cell = lax.axis_index("gene"), lax.axis_index("cell")
    mine = me % members
    for slot in range(blocks):
        slots[index[me * blocks + slot]] = slot
    for hop in range(members):
        owner = mine ^ hop
        for other in range(hop, blocks, members):
            rows = pieces[other][share * BLOCK : share * BLOCK + plan["sum_rows"], :]
            rows = rows.astype(jnp.float32)
            for side in range(members):
                slot = slots[me ^ other ^ side]
                for head in range(share):
                    at = head * members + side
                    sums[pl.ds(slot * heads + owner * share + head, 1), :] = rows[at : at + 1]
    line = jnp.sum(jnp.transpose(sums[...]), axis=0, keepdims=True)
    for slot in range(blocks):
        table[slot : slot + 1, 0:heads] = line[:, slot * heads : (slot + 1) * heads]
    for hop in range(cells):
        for slot in range(per_cell):
            parts[hop][slot : slot + 1, :] = table[pl.ds((cell ^ hop) * per_cell + slot, 1), 0:heads]
    for hop in range(members):
        start = pl.multiple_of((mine ^ hop) * (share * head_size), head_size)
        for head in range(share):
            top = head * BLOCK
            total = pieces[hop][top : top + BLOCK, :].astype(jnp.float32)
            for other in range(members + hop, blocks, members):
                total = total + pieces[other][top : top + BLOCK, :].astype(jnp.float32)
            columns = pl.ds(start + head * head_size, head_size)
            query_grad[0, :, columns] = total.astype(jnp.bfloat16)


def owner_kernel(plan, *refs):
    members, share, head_size = plan["members"], plan["share"], plan["head_size"]
    key_grad, value_grad = refs[members:]
    mine = lax.axis_index("gene") % members
    for hop in range(members):
        start = pl.multiple_of((mine ^ hop) * (share * head_size), head_size)
        for head in range(share):
            columns, top = pl.ds(start + head * head_size, head_size), 2 * BLOCK * head
            key_grad[0, :, columns] = refs[hop][top : top + BLOCK, :]
            value_grad[0, :, columns] = refs[hop][top + BLOCK : top + 2 * BLOCK, :]


def call(kernel, outs, scratch=(), smem_in=0, smem_out=False, count=0, limit=VMEM_LIMIT):
    places = [pl.BlockSpec(memory_space=pltpu.SMEM)] * smem_in
    places += [pl.BlockSpec(memory_space=pltpu.VMEM)] * count
    space = pltpu.SMEM if smem_out else pltpu.VMEM
    return pl.pallas_call(
        kernel,
        out_shape=outs,
        in_specs=places,
        out_specs=[pl.BlockSpec(memory_space=space)] * len(outs),
        scratch_shapes=list(scratch),
        compiler_params=pltpu.CompilerParams(vmem_limit_bytes=limit),
    )


def shards(
    query_rows,
    key_rows,
    value_rows,
    output_rows,
    output_grad,
    row_lse,
    block_bias,
    block_index,
    block_count,
):
    row_width = query_rows.shape[2]
    head_count = row_lse.shape[2]
    blocks = block_bias.shape[0]
    members = math.gcd(blocks, head_count)
    share = head_count // members
    head_size = row_width // head_count
    low, full = jnp.bfloat16, jnp.float32
    stat_rows = -(-4 * share // ROW_TILE) * ROW_TILE
    sum_rows = -(-share * members // ROW_TILE) * ROW_TILE
    far_rows = 2 * BLOCK * share + stat_rows
    plan = dict(
        blocks=blocks,
        members=members,
        share=share,
        head_size=head_size,
        stat_rows=stat_rows,
        sum_rows=sum_rows,
        far_rows=far_rows,
        scale=1.0 / math.sqrt(head_size),
    )

    cells = lax.axis_size("cell")
    plan["cells"] = cells
    near_rows = 4 * BLOCK * share + stat_rows
    near_in = jax.ShapeDtypeStruct((members, near_rows, BLOCK), low)
    far_in = jax.ShapeDtypeStruct((far_rows, BLOCK), low)
    sent = call(functools.partial(pack_kernel, plan), [far_in] * members + [near_in], count=6)(
        query_rows, key_rows, value_rows, output_rows, output_grad, jnp.transpose(row_lse, (2, 0, 1))
    )
    groups = [list(range(at, at + members)) for at in range(0, blocks, members)]

    def exchange(array):
        return lax.all_to_all(array, "gene", 0, 0, axis_index_groups=groups)

    def move(array, hop, axis="gene", size=blocks):
        return lax.ppermute(array, axis, [(i, i ^ hop) for i in range(size)])

    far = {hop: move(sent[hop % members], hop) for hop in range(members, blocks)}
    near = exchange(sent[members])
    (table,) = call(
        functools.partial(table_kernel, plan),
        [jax.ShapeDtypeStruct((blocks * members * share,), full)],
        smem_in=3,
        smem_out=True,
    )(block_bias.reshape(-1), block_index.reshape(-1), block_count)
    query_out = jax.ShapeDtypeStruct((share * BLOCK + sum_rows, BLOCK), low)
    partial_out = jax.ShapeDtypeStruct((share, members * BLOCK, BLOCK), full)
    owner_out = jax.ShapeDtypeStruct((2 * BLOCK * share, BLOCK), low)

    def stage(places, first, last, partials):
        count = len(places)
        pieces = [far[place] for place in places if place >= members]
        scratch = pltpu.VMEM((members * BLOCK, count * BLOCK), low)
        made = call(
            functools.partial(stage_kernel, plan, places, first, last),
            [query_out] * count + ([owner_out] * members if last else [partial_out] * 2),
            scratch=[scratch, scratch, pltpu.VMEM((count, sum_rows, BLOCK), full)],
            smem_in=1,
            count=1 + len(pieces) + len(partials),
            limit=STAGE_LIMIT,
        )(table, near, *pieces, *partials)
        return made[:count], made[count:]

    queries, partials, begin = [], [], 0
    for end in (members + (blocks - members) // 2, blocks):
        places = tuple(range(begin, end))
        made, partials = stage(places, begin == 0, end == blocks, partials)
        queries += [move(piece, place) if place else piece for piece, place in zip(made, places)]
        begin = end
    owned = [partials[0]] + [move(partials[hop], hop) for hop in range(1, members)]
    whole = jax.ShapeDtypeStruct((1, BLOCK, row_width), low)
    part_out = jax.ShapeDtypeStruct((blocks // cells, head_count), full)
    query_grad, *parts = call(
        functools.partial(query_kernel, plan),
        [whole] + [part_out] * cells,
        scratch=[
            pltpu.SMEM((blocks,), jnp.int32),
            pltpu.VMEM((head_count * blocks, BLOCK), full),
            pltpu.VMEM((blocks, BLOCK), full),
        ],
        smem_in=1,
        count=blocks,
    )(block_index.reshape(-1), *queries)
    parts = [parts[0]] + [move(parts[hop], hop, "cell", cells) for hop in range(1, cells)]
    key_grad, value_grad = call(functools.partial(owner_kernel, plan), [whole] * 2, count=members)(
        *owned
    )
    bias_grad = jnp.transpose(functools.reduce(jnp.add, parts))[None]
    return (query_grad, key_grad, value_grad, bias_grad)


def solution(mesh):
    rows = P("cell", "gene", None)
    in_specs = (rows,) * 6 + (P(),) * 3
    out_specs = (rows, rows, rows, P("gene", None, "cell"))
    return jax.shard_map(shards, mesh=mesh, in_specs=in_specs, out_specs=out_specs, check_vma=False)
```

time: 95.9 us -> 83.3 us (0.87)
  Pallas kernels: 23 us -> 15.9 us
  blocking collectives: 5.64 us -> 0 us
  local copies, waits for them, and re-layouts: 8.21 us -> 4.23 us
  starting transfers between devices: 33.7 us -> 37.2 us
    pallas_call x6 -> x5, Pallas kernels: 20.8 us -> 13.6 us  [the longest x2 6.42 us: stage(): call(functools.partial(stage_kernel, plan, places, first, last), [query_o...]
    unnamed x1 -> x0, blocking collectives: 5.64 us -> none
    all_to_all x0 -> x1, starting transfers between devices: none -> 5.39 us  [exchange(): return lax.all_to_all(array, 'gene', 0, 0, axis_index_groups=groups)]
    unnamed x54 -> x39, local copies, waits for them, and re-layouts: 6.26 us -> 2.88 us
    ppermute x17, starting transfers between devices: 33.7 us -> 31.8 us  [move(): return lax.ppermute(array, axis, [(i, i ^ hop) for i in range(size)])]
    broadcast_in_dim x0 -> x1, other arithmetic: none -> 1.24 us  [shards(): bias_grad = jnp.transpose(functools.reduce(jnp.add, parts))[None]]
    all_to_all x0 -> x1, waiting for transfers between devices: none -> 1.01 us  [exchange(): return lax.all_to_all(array, 'gene', 0, 0, axis_index_groups=groups)]
  transfers between devices with their start and end apart: 17 -> 18, of which waited for: 6 -> 8; matrix products, arithmetic and copies ran while one was open for 4% -> 3% of each run, Pallas kernels for 17% -> 12%
where the time goes in v1:
time: 83.3 us; the launch traced here: 83 us
  starting transfers between devices  37.2 us (45%)
  waiting for transfers between devices  23.6 us (28%)
  Pallas kernels  15.9 us (19%)
  local copies, waits for them, and re-layouts  4.23 us (5%)
  other arithmetic  1.24 us (1%)
  between operations  0.84 us (1%)
    ppermute x17, starting transfers between devices, move(): return lax.ppermute(array, axis, [(i, i ^ hop) for i in range(size)])  31.8 us
    ppermute x17, waiting for transfers between devices, move(): return lax.ppermute(array, axis, [(i, i ^ hop) for i in range(size)])  22.6 us
    pallas_call x2, Pallas kernels, stage(): call(functools.partial(stage_kernel, plan, places, first, last), [query_o...  6.42 us
    all_to_all x1, starting transfers between devices, exchange(): return lax.all_to_all(array, 'gene', 0, 0, axis_index_groups=groups)  5.39 us
    pallas_call x1, Pallas kernels, shards(): call(functools.partial(pack_kernel, plan), [far_in] * members + [near_in]...  3.33 us
    unnamed x39, local copies, waits for them, and re-layouts  2.88 us
    pallas_call x1, Pallas kernels, shards(): call(functools.partial(owner_kernel, plan), [whole] * 2, count=members)  2.23 us
    pallas_call x1, Pallas kernels, shards(): call(functools.partial(query_kernel, plan), [whole] + [part_out] * cells,...  2.12 us
  transfers between devices with their start and end apart: 18, of which 8 were waited for; matrix products, arithmetic and copies ran while one was open for 3% of the time, Pallas kernels for 12%

profile of v1, /device:TPU:0, one launch (start us, length us, event | category | flops | bytes accessed | tf_op | source)
XLA Modules:
  0.0 83.0 jit_solution(1808650628726349554)
XLA Ops:
  0.6 3.3 %shard_map.121 = (bf16[784,128]{1,0:T(8,128)(2,1)}, bf16[784,128]{1,0:T(8,128)(2,1)}, bf16[784,128]{1,0:T(8,128)(2,1)}, bf16[784,128]{1,0:T(8,128)(2,1)}, bf16[4,1552,128]{2,1,0:T(8,128)(2,1)}) custom-call(bf16[1,128,1536]{2,1,0:T(8,128)(2,1)} %query.1, bf16[1,128,1536]{2,1,0:T(8,128)(2,1)} %key.1, bf16[1,128,1536]{2,1,0:T(8,128)(2,1)} %value.1, ...), custom_call_target="tpu_custom_call" | custom-call | tf_op jit(solution)/shard_map/pallas_call | solution.py:279
  4.0 0.0 copy-start.14
  4.0 0.0 copy-start.13
  4.0 5.4 %all-to-all-start = ((bf16[4,1552,128]{2,1,0:T(8,128)(2,1)}), bf16[4,1552,128]{2,1,0:T(8,128)(2,1)S(1)}, u32[]{:S(2)}, u32[]{:S(2)}) async-start(bf16[4,1552,128]{2,1,0:T(8,128)(2,1)} %get-tuple-element.30), calls=%async_computation | async-start | bytes 3178496 | tf_op jit(solution)/shard_map/all_to_all | solution.py:285
  9.4 2.6 %collective-permute-start = (bf16[784,128]{1,0:T(8,128)(2,1)S(1)}, bf16[784,128]{1,0:T(8,128)(2,1)S(1)}, u32[]{:S(2)}, u32[]{:S(2)}) collective-permute-start(bf16[784,128]{1,0:T(8,128)(2,1)S(1)} %copy-done.18), channel_id=1, source_target_pairs={{0,4},{1,5},{2,6},{3,7},{4,0},{5,1},{6,2},{7,3},{8,12},{9,13},{10,... | collective-permute-start | bytes 602120 | tf_op jit(solution)/shard_map/ppermute | solution.py:288
  12.0 1.8 %collective-permute-start.1 = (bf16[784,128]{1,0:T(8,128)(2,1)S(1)}, bf16[784,128]{1,0:T(8,128)(2,1)S(1)}, u32[]{:S(2)}, u32[]{:S(2)}) collective-permute-start(bf16[784,128]{1,0:T(8,128)(2,1)S(1)} %copy-done.17), channel_id=1, source_target_pairs={{0,5},{1,4},{2,7},{3,6},{4,1},{5,0},{6,3},{7,2},{8,13},{9,12},{10,... | collective-permute-start | bytes 602120 | tf_op jit(solution)/shard_map/ppermute | solution.py:288
  13.8 3.5 %collective-permute-start.7 = (bf16[784,128]{1,0:T(8,128)(2,1)S(1)}, bf16[784,128]{1,0:T(8,128)(2,1)S(1)}, u32[]{:S(2)}, u32[]{:S(2)}) collective-permute-start(bf16[784,128]{1,0:T(8,128)(2,1)S(1)} %copy-done.16), channel_id=1, source_target_pairs={{0,6},{1,7},{2,4},{3,5},{4,2},{5,3},{6,0},{7,1},{8,14},{9,15},{10,... | collective-permute-start | bytes 602120 | tf_op jit(solution)/shard_map/ppermute | solution.py:288
  17.3 0.1 collective-permute-start.8
  17.4 0.7 reshape.15.index
  18.0 0.1 copy.13
  18.1 0.7 reshape.16.bias
  18.8 1.8 %shard_map.120.shift = f32[96]{0:T(128)} custom-call(f32[768]{0:T(1024)} %reshape.16.bias, s32[64]{0:T(128)} %reshape.15.index, s32[8]{0:T(128)} %count.1), custom_call_target="tpu_custom_call" | custom-call | tf_op jit(solution)/shard_map/pallas_call | solution.py:292
  20.6 11.5 %collective-permute-done.refs_1_ = bf16[784,128]{1,0:T(8,128)(2,1)S(1)} collective-permute-done((bf16[784,128]{1,0:T(8,128)(2,1)S(1)}, bf16[784,128]{1,0:T(8,128)(2,1)S(1)}, u32[]{:S(2)}, u32[]{:S(2)}) %collective-permute-start) | collective-permute-done | bytes 200736 | tf_op jit(solution)/shard_map/ppermute | solution.py:288
  32.1 4.3 %collective-permute-done.1.refs_2_ = bf16[784,128]{1,0:T(8,128)(2,1)S(1)} collective-permute-done((bf16[784,128]{1,0:T(8,128)(2,1)S(1)}, bf16[784,128]{1,0:T(8,128)(2,1)S(1)}, u32[]{:S(2)}, u32[]{:S(2)}) %collective-permute-start.1) | collective-permute-done | bytes 200736 | tf_op jit(solution)/shard_map/ppermute | solution.py:288
  36.4 1.0 %all-to-all-done.refs_0_ = bf16[4,1552,128]{2,1,0:T(8,128)(2,1)S(1)} async-done(((bf16[4,1552,128]{2,1,0:T(8,128)(2,1)}), bf16[4,1552,128]{2,1,0:T(8,128)(2,1)S(1)}, u32[]{:S(2)}, u32[]{:S(2)}) %all-to-all-start) | async-done | bytes 1589280 | tf_op jit(solution)/shard_map/all_to_all | solution.py:285
  37.4 0.7 copy-done.2
  38.1 4.2 %shard_map.122 = (bf16[400,128]{1,0:T(8,128)(2,1)S(1)}, bf16[400,128]{1,0:T(8,128)(2,1)S(1)}, bf16[400,128]{1,0:T(8,128)(2,1)S(1)}, bf16[400,128]{1,0:T(8,128)(2...) custom-call(f32[96]{0:T(128)S(1)} %copy-done.2, ...), custom_call_target="tpu_custom_call" | custom-call | tf_op jit(solution)/shard_map/pallas_call | solution.py:306
  42.3 0.0 copy-start.1
  42.3 1.5 %collective-permute-start.2 = (bf16[400,128]{1,0:T(8,128)(2,1)S(1)}, bf16[400,128]{1,0:T(8,128)(2,1)S(1)}, u32[]{:S(2)}, u32[]{:S(2)}) collective-permute-start(bf16[400,128]{1,0:T(8,128)(2,1)S(1)} %get-tuple-element.34), channel_id=1, source_target_pairs={{0,1},{1,0},{2,3},{3,2},{4,5},{5,4},{6,7},{7,6},{8,9},{9,8},{10,11... | collective-permute-start | bytes 307208 | tf_op jit(solution)/shard_map/ppermute | solution.py:288
  43.8 4.0 %collective-permute-start.3 = (bf16[400,128]{1,0:T(8,128)(2,1)S(1)}, bf16[400,128]{1,0:T(8,128)(2,1)S(1)}, u32[]{:S(2)}, u32[]{:S(2)}) collective-permute-start(bf16[400,128]{1,0:T(8,128)(2,1)S(1)} %get-tuple-element.35), channel_id=1, source_target_pairs={{0,2},{1,3},{2,0},{3,1},{4,6},{5,7},{6,4},{7,5},{8,10},{9,11},{10,... | collective-permute-start | bytes 307208 | tf_op jit(solution)/shard_map/ppermute | solution.py:288
  47.8 0.9 %collective-permute-start.4 = (bf16[400,128]{1,0:T(8,128)(2,1)S(1)}, bf16[400,128]{1,0:T(8,128)(2,1)S(1)}, u32[]{:S(2)}, u32[]{:S(2)}) collective-permute-start(bf16[400,128]{1,0:T(8,128)(2,1)S(1)} %get-tuple-element.36), channel_id=1, source_target_pairs={{0,3},{1,2},{2,1},{3,0},{4,7},{5,6},{6,5},{7,4},{8,11},{9,10},{10,... | collective-permute-start | bytes 307208 | tf_op jit(solution)/shard_map/ppermute | solution.py:288
  48.7 0.0 collective-permute-done.7.refs_1_
  48.7 6.9 %collective-permute-start.5 = (bf16[400,128]{1,0:T(8,128)(2,1)S(1)}, bf16[400,128]{1,0:T(8,128)(2,1)S(1)}, u32[]{:S(2)}, u32[]{:S(2)}) collective-permute-start(bf16[400,128]{1,0:T(8,128)(2,1)S(1)} %get-tuple-element.37), channel_id=1, source_target_pairs={{0,4},{1,5},{2,6},{3,7},{4,0},{5,1},{6,2},{7,3},{8,12},{9,13},{10,... | collective-permute-start | bytes 307208 | tf_op jit(solution)/shard_map/ppermute | solution.py:288
  55.6 0.0 collective-permute-done.8.refs_2_
  55.6 1.0 %collective-permute-start.6 = (bf16[400,128]{1,0:T(8,128)(2,1)S(1)}, bf16[400,128]{1,0:T(8,128)(2,1)S(1)}, u32[]{:S(2)}, u32[]{:S(2)}) collective-permute-start(bf16[400,128]{1,0:T(8,128)(2,1)S(1)} %get-tuple-element.38), channel_id=1, source_target_pairs={{0,5},{1,4},{2,7},{3,6},{4,1},{5,0},{6,3},{7,2},{8,13},{9,12},{10,... | collective-permute-start | bytes 307208 | tf_op jit(solution)/shard_map/ppermute | solution.py:288
  56.6 2.3 %shard_map.123 = (bf16[400,128]{1,0:T(8,128)(2,1)S(1)}, bf16[400,128]{1,0:T(8,128)(2,1)S(1)}, bf16[768,128]{1,0:T(8,128)(2,1)S(1)}, bf16[768,128]{1,0:T(8,128)(2...) custom-call(f32[96]{0:T(128)S(1)} %copy-done.2, bf16[4,1552,128]{2,1,0:T(8,128)(2,1)S(1)} %all-to-all-done.refs_0_, ...), custom_call_target="tpu_custom_call" | custom-call | tf_op jit(solution)/shard_map/pallas_call | solution.py:306
  58.9 0.7 copy-done
  59.5 0.0 collective-permute-done.2.refs_1_
  59.5 4.3 %collective-permute-start.9 = (bf16[400,128]{1,0:T(8,128)(2,1)S(1)}, bf16[400,128]{1,0:T(8,128)(2,1)S(1)}, u32[]{:S(2)}, u32[]{:S(2)}) collective-permute-start(bf16[400,128]{1,0:T(8,128)(2,1)S(1)} %get-tuple-element.43), channel_id=1, source_target_pairs={{0,6},{1,7},{2,4},{3,5},{4,2},{5,3},{6,0},{7,1},{8,14},{9,15},{10,... | collective-permute-start | bytes 307208 | tf_op jit(solution)/shard_map/ppermute | solution.py:288
  63.9 0.0 collective-permute-start.10
  63.9 0.0 collective-permute-done.4.refs_3_
  63.9 1.5 %collective-permute-start.11 = (bf16[768,128]{1,0:T(8,128)(2,1)S(1)}, bf16[768,128]{1,0:T(8,128)(2,1)S(1)}, u32[]{:S(2)}, u32[]{:S(2)}) collective-permute-start(bf16[768,128]{1,0:T(8,128)(2,1)S(1)} %get-tuple-element.47), channel_id=1, source_target_pairs={{0,1},{1,0},{2,3},{3,2},{4,5},{5,4},{6,7},{7,6},{8,9},{9,8},{10,11... | collective-permute-start | bytes 589832 | tf_op jit(solution)/shard_map/ppermute | solution.py:288
  65.4 0.0 collective-permute-done.5.refs_4_
  65.4 2.0 %collective-permute-start.13 = (bf16[768,128]{1,0:T(8,128)(2,1)S(1)}, bf16[768,128]{1,0:T(8,128)(2,1)S(1)}, u32[]{:S(2)}, u32[]{:S(2)}) collective-permute-start(bf16[768,128]{1,0:T(8,128)(2,1)S(1)} %get-tuple-element.49), channel_id=1, source_target_pairs={{0,3},{1,2},{2,1},{3,0},{4,7},{5,6},{6,5},{7,4},{8,11},{9,10},{10,... | collective-permute-start | bytes 589832 | tf_op jit(solution)/shard_map/ppermute | solution.py:288
  67.5 0.2 collective-permute-done.9.refs_6_
  67.7 3.7 %collective-permute-done.10.refs_7_ = bf16[400,128]{1,0:T(8,128)(2,1)S(1)} collective-permute-done((bf16[400,128]{1,0:T(8,128)(2,1)S(1)}, bf16[400,128]{1,0:T(8,128)(2,1)S(1)}, u32[]{:S(2)}, u32[]{:S(2)}) %collective-permute-start.10) | collective-permute-done | bytes 102432 | tf_op jit(solution)/shard_map/ppermute | solution.py:288
  71.4 0.6 copy-done.12
  72.0 2.1 %shard_map.124 = (bf16[1,128,1536]{2,1,0:T(8,128)(2,1)}, f32[2,12]{1,0:T(2,128)}, f32[2,12]{1,0:T(2,128)}, f32[2,12]{1,0:T(2,128)}, f32[2,12]{1,0:T(2,128)}) custom-call(s32[64]{0:T(128)} %reshape.15.index, bf16[400,128]{1,0:T(8,128)(2,1)} %copy-done.1, bf16[400,128]{1,0:T(8,128)(2,1)} %copy-done.6, bf16[400,128]{1,0:T(8,128)(2,1)} %copy-done.7, ...), custom_call_target="tpu_custom_call" | custom-call | tf_op jit(solution)/shard_map/pallas_call | solution.py:325
  74.1 1.6 %collective-permute-start.15 = (f32[2,12]{1,0:T(2,128)}, f32[2,12]{1,0:T(2,128)S(1)}, u32[]{:S(2)}, u32[]{:S(2)}) collective-permute-start(f32[2,12]{1,0:T(2,128)} %get-tuple-element.54), channel_id=1, source_target_pairs={{0,16},{8,24},{16,0},{24,8},{1,17},{9,25},{17,1},{25,9},{2,18},{10... | collective-permute-start | bytes 296 | tf_op jit(solution)/shard_map/ppermute | solution.py:288
  75.6 1.6 %collective-permute-done.16 = f32[2,12]{1,0:T(2,128)S(1)} collective-permute-done((f32[2,12]{1,0:T(2,128)}, f32[2,12]{1,0:T(2,128)S(1)}, u32[]{:S(2)}, u32[]{:S(2)}) %collective-permute-start.16) | collective-permute-done | bytes 128 | tf_op jit(solution)/shard_map/ppermute | solution.py:288
  77.3 0.1 collective-permute-start.14
  77.4 0.5 collective-permute-done.15
  77.9 0.7 collective-permute-done.14
  78.6 1.2 %add_bitcast_fusion = f32[1,12,2]{1,2,0:T(2,128)} fusion(f32[2,12]{1,0:T(2,128)S(1)} %collective-permute-done.16, f32[2,12]{1,0:T(2,128)S(1)} %collective-permute-done.15, f32[2,12]{1,0:T(2,128)} %get-tuple-element.52, f32[2,12]{1,0:T(2,128)S(1)} %collective-permute-done.14), kind=kLoop, calls=%fused_computation | loop fusion | flops 72 | bytes 480 | tf_op jit(solution)/shard_map/broadcast_in_dim | solution.py:340
  79.9 0.6 copy-done.3
  80.6 0.1 copy-done.4
  80.7 0.1 copy-done.5
  80.7 2.2 %shard_map.125 = (bf16[1,128,1536]{2,1,0:T(8,128)(2,1)}, bf16[1,128,1536]{2,1,0:T(8,128)(2,1)}) custom-call(bf16[768,128]{1,0:T(8,128)(2,1)} %copy-done, bf16[768,128]{1,0:T(8,128)(2,1)} %copy-done.3, bf16[768,128]{1,0:T(8,128)(2,1)} %copy-done.4, bf16[768,128]{1,0:T(8,128)(2,1)} %copy-done.5), custom_call_target="tpu_custom_call" | custom-call | tf_op jit(solution)/shard_map/pallas_call | solution.py:337
  (36 shorter events, 0.1 us)
Async XLA Ops:
  4.0 5.4 %copy-start.18 = (bf16[784,128]{1,0:T(8,128)(2,1)S(1)}, bf16[784,128]{1,0:T(8,128)(2,1)}, u32[]{:S(2)}) copy-start(bf16[784,128]{1,0:T(8,128)(2,1)} %get-tuple-element.31) | copy-start | bytes 602116
  4.0 8.0 %copy-start.17 = (bf16[784,128]{1,0:T(8,128)(2,1)S(1)}, bf16[784,128]{1,0:T(8,128)(2,1)}, u32[]{:S(2)}) copy-start(bf16[784,128]{1,0:T(8,128)(2,1)} %get-tuple-element.32) | copy-start | bytes 602116
  4.0 9.8 %copy-start.16 = (bf16[784,128]{1,0:T(8,128)(2,1)S(1)}, bf16[784,128]{1,0:T(8,128)(2,1)}, u32[]{:S(2)}) copy-start(bf16[784,128]{1,0:T(8,128)(2,1)} %get-tuple-element.39) | copy-start | bytes 602116
  4.0 13.3 %copy-start.15 = (bf16[784,128]{1,0:T(8,128)(2,1)S(1)}, bf16[784,128]{1,0:T(8,128)(2,1)}, u32[]{:S(2)}) copy-start(bf16[784,128]{1,0:T(8,128)(2,1)} %get-tuple-element.40) | copy-start | bytes 602116
  4.0 13.4 %copy-start.14 = (s32[8,8]{1,0:T(8,128)S(1)}, s32[8,8]{1,0:T(8,128)}, u32[]{:S(2)}) copy-start(s32[8,8]{1,0:T(8,128)} %param.16) | copy-start | bytes 772
  4.0 14.0 %copy-start.13 = (f32[8,12,8]{1,2,0:T(8,128)S(1)}, f32[8,12,8]{1,2,0:T(8,128)}, u32[]{:S(2)}) copy-start(f32[8,12,8]{1,2,0:T(8,128)} %param.15) | copy-start | bytes 9220
  4.0 33.4 %all-to-all-start = ((bf16[4,1552,128]{2,1,0:T(8,128)(2,1)}), bf16[4,1552,128]{2,1,0:T(8,128)(2,1)S(1)}, u32[]{:S(2)}, u32[]{:S(2)}) async-start(bf16[4,1552,128]{2,1,0:T(8,128)(2,1)} %get-tuple-element.30), calls=%async_computation | async-start | bytes 3178496 | tf_op jit(solution)/shard_map/all_to_all | solution.py:285
  9.4 22.7 %collective-permute-start = (bf16[784,128]{1,0:T(8,128)(2,1)S(1)}, bf16[784,128]{1,0:T(8,128)(2,1)S(1)}, u32[]{:S(2)}, u32[]{:S(2)}) collective-permute-start(bf16[784,128]{1,0:T(8,128)(2,1)S(1)} %copy-done.18), channel_id=1, source_target_pairs={{0,4},{1,5},{2,6},{3,7},{4,0},{5,1},{6,2},{7,3},{8,12},{9,13},{10,... | collective-permute-start | bytes 602120 | tf_op jit(solution)/shard_map/ppermute | solution.py:288
  12.0 24.4 %collective-permute-start.1 = (bf16[784,128]{1,0:T(8,128)(2,1)S(1)}, bf16[784,128]{1,0:T(8,128)(2,1)S(1)}, u32[]{:S(2)}, u32[]{:S(2)}) collective-permute-start(bf16[784,128]{1,0:T(8,128)(2,1)S(1)} %copy-done.17), channel_id=1, source_target_pairs={{0,5},{1,4},{2,7},{3,6},{4,1},{5,0},{6,3},{7,2},{8,13},{9,12},{10,... | collective-permute-start | bytes 602120 | tf_op jit(solution)/shard_map/ppermute | solution.py:288
  13.8 34.9 %collective-permute-start.7 = (bf16[784,128]{1,0:T(8,128)(2,1)S(1)}, bf16[784,128]{1,0:T(8,128)(2,1)S(1)}, u32[]{:S(2)}, u32[]{:S(2)}) collective-permute-start(bf16[784,128]{1,0:T(8,128)(2,1)S(1)} %copy-done.16), channel_id=1, source_target_pairs={{0,6},{1,7},{2,4},{3,5},{4,2},{5,3},{6,0},{7,1},{8,14},{9,15},{10,... | collective-permute-start | bytes 602120 | tf_op jit(solution)/shard_map/ppermute | solution.py:288
  17.3 38.3 %collective-permute-start.8 = (bf16[784,128]{1,0:T(8,128)(2,1)S(1)}, bf16[784,128]{1,0:T(8,128)(2,1)S(1)}, u32[]{:S(2)}, u32[]{:S(2)}) collective-permute-start(bf16[784,128]{1,0:T(8,128)(2,1)S(1)} %copy-done.15), channel_id=1, source_target_pairs={{0,7},{1,6},{2,5},{3,4},{4,3},{5,2},{6,1},{7,0},{8,15},{9,14},{10,... | collective-permute-start | bytes 602120 | tf_op jit(solution)/shard_map/ppermute | solution.py:288
  37.4 0.7 copy-start.2
  42.3 16.6 %copy-start.1 = (bf16[400,128]{1,0:T(8,128)(2,1)}, bf16[400,128]{1,0:T(8,128)(2,1)S(1)}, u32[]{:S(2)}) copy-start(bf16[400,128]{1,0:T(8,128)(2,1)S(1)} %get-tuple-element.33.refs_0_) | copy-start | bytes 307204
  42.3 17.2 %collective-permute-start.2 = (bf16[400,128]{1,0:T(8,128)(2,1)S(1)}, bf16[400,128]{1,0:T(8,128)(2,1)S(1)}, u32[]{:S(2)}, u32[]{:S(2)}) collective-permute-start(bf16[400,128]{1,0:T(8,128)(2,1)S(1)} %get-tuple-element.34), channel_id=1, source_target_pairs={{0,1},{1,0},{2,3},{3,2},{4,5},{5,4},{6,7},{7,6},{8,9},{9,8},{10,11... | collective-permute-start | bytes 307208 | tf_op jit(solution)/shard_map/ppermute | solution.py:288
  43.8 20.0 %collective-permute-start.3 = (bf16[400,128]{1,0:T(8,128)(2,1)S(1)}, bf16[400,128]{1,0:T(8,128)(2,1)S(1)}, u32[]{:S(2)}, u32[]{:S(2)}) collective-permute-start(bf16[400,128]{1,0:T(8,128)(2,1)S(1)} %get-tuple-element.35), channel_id=1, source_target_pairs={{0,2},{1,3},{2,0},{3,1},{4,6},{5,7},{6,4},{7,5},{8,10},{9,11},{10,... | collective-permute-start | bytes 307208 | tf_op jit(solution)/shard_map/ppermute | solution.py:288
  47.8 16.1 %collective-permute-start.4 = (bf16[400,128]{1,0:T(8,128)(2,1)S(1)}, bf16[400,128]{1,0:T(8,128)(2,1)S(1)}, u32[]{:S(2)}, u32[]{:S(2)}) collective-permute-start(bf16[400,128]{1,0:T(8,128)(2,1)S(1)} %get-tuple-element.36), channel_id=1, source_target_pairs={{0,3},{1,2},{2,1},{3,0},{4,7},{5,6},{6,5},{7,4},{8,11},{9,10},{10,... | collective-permute-start | bytes 307208 | tf_op jit(solution)/shard_map/ppermute | solution.py:288
  48.7 16.7 %collective-permute-start.5 = (bf16[400,128]{1,0:T(8,128)(2,1)S(1)}, bf16[400,128]{1,0:T(8,128)(2,1)S(1)}, u32[]{:S(2)}, u32[]{:S(2)}) collective-permute-start(bf16[400,128]{1,0:T(8,128)(2,1)S(1)} %get-tuple-element.37), channel_id=1, source_target_pairs={{0,4},{1,5},{2,6},{3,7},{4,0},{5,1},{6,2},{7,3},{8,12},{9,13},{10,... | collective-permute-start | bytes 307208 | tf_op jit(solution)/shard_map/ppermute | solution.py:288
  55.6 9.8 %collective-permute-start.6 = (bf16[400,128]{1,0:T(8,128)(2,1)S(1)}, bf16[400,128]{1,0:T(8,128)(2,1)S(1)}, u32[]{:S(2)}, u32[]{:S(2)}) collective-permute-start(bf16[400,128]{1,0:T(8,128)(2,1)S(1)} %get-tuple-element.38), channel_id=1, source_target_pairs={{0,5},{1,4},{2,7},{3,6},{4,1},{5,0},{6,3},{7,2},{8,13},{9,12},{10,... | collective-permute-start | bytes 307208 | tf_op jit(solution)/shard_map/ppermute | solution.py:288
  58.8 0.7 copy-start
  59.5 11.8 %copy-start.6 = (bf16[400,128]{1,0:T(8,128)(2,1)}, bf16[400,128]{1,0:T(8,128)(2,1)S(1)}, u32[]{:S(2)}) copy-start(bf16[400,128]{1,0:T(8,128)(2,1)S(1)} %collective-permute-done.2.refs_1_) | copy-start | bytes 307204
  59.5 8.1 %collective-permute-start.9 = (bf16[400,128]{1,0:T(8,128)(2,1)S(1)}, bf16[400,128]{1,0:T(8,128)(2,1)S(1)}, u32[]{:S(2)}, u32[]{:S(2)}) collective-permute-start(bf16[400,128]{1,0:T(8,128)(2,1)S(1)} %get-tuple-element.43), channel_id=1, source_target_pairs={{0,6},{1,7},{2,4},{3,5},{4,2},{5,3},{6,0},{7,1},{8,14},{9,15},{10,... | collective-permute-start | bytes 307208 | tf_op jit(solution)/shard_map/ppermute | solution.py:288
  63.9 7.5 %copy-start.7 = (bf16[400,128]{1,0:T(8,128)(2,1)}, bf16[400,128]{1,0:T(8,128)(2,1)S(1)}, u32[]{:S(2)}) copy-start(bf16[400,128]{1,0:T(8,128)(2,1)S(1)} %collective-permute-done.3.refs_2_) | copy-start | bytes 307204
  63.9 7.5 %collective-permute-start.10 = (bf16[400,128]{1,0:T(8,128)(2,1)S(1)}, bf16[400,128]{1,0:T(8,128)(2,1)S(1)}, u32[]{:S(2)}, u32[]{:S(2)}) collective-permute-start(bf16[400,128]{1,0:T(8,128)(2,1)S(1)} %get-tuple-element.44), channel_id=1, source_target_pairs={{0,7},{1,6},{2,5},{3,4},{4,3},{5,2},{6,1},{7,0},{8,15},{9,14},{10,... | collective-permute-start | bytes 307208 | tf_op jit(solution)/shard_map/ppermute | solution.py:288
  63.9 7.5 %copy-start.8 = (bf16[400,128]{1,0:T(8,128)(2,1)}, bf16[400,128]{1,0:T(8,128)(2,1)S(1)}, u32[]{:S(2)}) copy-start(bf16[400,128]{1,0:T(8,128)(2,1)S(1)} %collective-permute-done.4.refs_3_) | copy-start | bytes 307204
  63.9 16.0 %collective-permute-start.11 = (bf16[768,128]{1,0:T(8,128)(2,1)S(1)}, bf16[768,128]{1,0:T(8,128)(2,1)S(1)}, u32[]{:S(2)}, u32[]{:S(2)}) collective-permute-start(bf16[768,128]{1,0:T(8,128)(2,1)S(1)} %get-tuple-element.47), channel_id=1, source_target_pairs={{0,1},{1,0},{2,3},{3,2},{4,5},{5,4},{6,7},{7,6},{8,9},{9,8},{10,11... | collective-permute-start | bytes 589832 | tf_op jit(solution)/shard_map/ppermute | solution.py:288
  65.4 5.9 %copy-start.9 = (bf16[400,128]{1,0:T(8,128)(2,1)}, bf16[400,128]{1,0:T(8,128)(2,1)S(1)}, u32[]{:S(2)}) copy-start(bf16[400,128]{1,0:T(8,128)(2,1)S(1)} %collective-permute-done.5.refs_4_) | copy-start | bytes 307204
  65.4 14.5 %collective-permute-start.12 = (bf16[768,128]{1,0:T(8,128)(2,1)S(1)}, bf16[768,128]{1,0:T(8,128)(2,1)S(1)}, u32[]{:S(2)}, u32[]{:S(2)}) collective-permute-start(bf16[768,128]{1,0:T(8,128)(2,1)S(1)} %get-tuple-element.48), channel_id=1, source_target_pairs={{0,2},{1,3},{2,0},{3,1},{4,6},{5,7},{6,4},{7,5},{8,10},{9,11},{10,... | collective-permute-start | bytes 589832 | tf_op jit(solution)/shard_map/ppermute | solution.py:288
  65.4 5.9 %copy-start.10 = (bf16[400,128]{1,0:T(8,128)(2,1)}, bf16[400,128]{1,0:T(8,128)(2,1)S(1)}, u32[]{:S(2)}) copy-start(bf16[400,128]{1,0:T(8,128)(2,1)S(1)} %collective-permute-done.6.refs_5_) | copy-start | bytes 307204
  65.4 14.5 %collective-permute-start.13 = (bf16[768,128]{1,0:T(8,128)(2,1)S(1)}, bf16[768,128]{1,0:T(8,128)(2,1)S(1)}, u32[]{:S(2)}, u32[]{:S(2)}) collective-permute-start(bf16[768,128]{1,0:T(8,128)(2,1)S(1)} %get-tuple-element.49), channel_id=1, source_target_pairs={{0,3},{1,2},{2,1},{3,0},{4,7},{5,6},{6,5},{7,4},{8,11},{9,10},{10,... | collective-permute-start | bytes 589832 | tf_op jit(solution)/shard_map/ppermute | solution.py:288
  67.7 3.7 %copy-start.11 = (bf16[400,128]{1,0:T(8,128)(2,1)}, bf16[400,128]{1,0:T(8,128)(2,1)S(1)}, u32[]{:S(2)}) copy-start(bf16[400,128]{1,0:T(8,128)(2,1)S(1)} %collective-permute-done.9.refs_6_) | copy-start | bytes 307204
  71.3 0.6 copy-start.12
  74.1 3.2 %collective-permute-start.16 = (f32[2,12]{1,0:T(2,128)}, f32[2,12]{1,0:T(2,128)S(1)}, u32[]{:S(2)}, u32[]{:S(2)}) collective-permute-start(f32[2,12]{1,0:T(2,128)} %get-tuple-element.55), channel_id=1, source_target_pairs={{0,24},{8,16},{16,8},{24,0},{1,25},{9,17},{17,9},{25,1},{2,26},{10... | collective-permute-start | bytes 296 | tf_op jit(solution)/shard_map/ppermute | solution.py:288
  74.1 3.8 %collective-permute-start.15 = (f32[2,12]{1,0:T(2,128)}, f32[2,12]{1,0:T(2,128)S(1)}, u32[]{:S(2)}, u32[]{:S(2)}) collective-permute-start(f32[2,12]{1,0:T(2,128)} %get-tuple-element.54), channel_id=1, source_target_pairs={{0,16},{8,24},{16,0},{24,8},{1,17},{9,25},{17,1},{25,9},{2,18},{10... | collective-permute-start | bytes 296 | tf_op jit(solution)/shard_map/ppermute | solution.py:288
  77.3 1.4 %collective-permute-start.14 = (f32[2,12]{1,0:T(2,128)}, f32[2,12]{1,0:T(2,128)S(1)}, u32[]{:S(2)}, u32[]{:S(2)}) collective-permute-start(f32[2,12]{1,0:T(2,128)} %get-tuple-element.53), channel_id=1, source_target_pairs={{0,8},{8,0},{16,24},{24,16},{1,9},{9,1},{17,25},{25,17},{2,10},{10... | collective-permute-start | bytes 296 | tf_op jit(solution)/shard_map/ppermute | solution.py:288
  79.9 0.7 copy-start.3
  79.9 0.8 copy-start.4
  79.9 0.8 copy-start.5

commit v2 on v1

--- a/solution.py
+++ b/solution.py
@@ -176,12 +176,11 @@
         outs[at][share * BLOCK : share * BLOCK + plan["sum_rows"], :] = spread.astype(jnp.bfloat16)
 
 
-def query_kernel(plan, index, *refs):
-    blocks, members, share = plan["blocks"], plan["members"], plan["share"]
-    head_size, cells = plan["head_size"], plan["cells"]
+def bias_kernel(plan, index, *refs):
+    blocks, members, share, cells = plan["blocks"], plan["members"], plan["share"], plan["cells"]
     heads, per_cell = members * share, blocks // cells
-    pieces, query_grad, parts = refs[:blocks], refs[blocks], refs[blocks + 1 : blocks + 1 + cells]
-    slots, sums, table = refs[blocks + 1 + cells :]
+    pieces, parts = refs[:blocks], refs[blocks : blocks + cells]
+    slots, sums, table = refs[blocks + cells :]
     me, cell = lax.axis_index("gene"), lax.axis_index("cell")
     mine = me % members
     for slot in range(blocks):
@@ -202,27 +201,26 @@
     for hop in range(cells):
         for slot in range(per_cell):
             parts[hop][slot : slot + 1, :] = table[pl.ds((cell ^ hop) * per_cell + slot, 1), 0:heads]
+
+
+def unpack_kernel(plan, *refs):
+    blocks, members, share = plan["blocks"], plan["members"], plan["share"]
+    head_size = plan["head_size"]
+    pieces, owned = refs[:blocks], refs[blocks : blocks + members]
+    query_grad, key_grad, value_grad = refs[-3:]
+    mine = lax.axis_index("gene") % members
     for hop in range(members):
         start = pl.multiple_of((mine ^ hop) * (share * head_size), head_size)
         for head in range(share):
+            columns = pl.ds(start + head * head_size, head_size)
             top = head * BLOCK
             total = pieces[hop][top : top + BLOCK, :].astype(jnp.float32)
             for other in range(members + hop, blocks, members):
                 total = total + pieces[other][top : top + BLOCK, :].astype(jnp.float32)
-            columns = pl.ds(start + head * head_size, head_size)
             query_grad[0, :, columns] = total.astype(jnp.bfloat16)
-
-
-def owner_kernel(plan, *refs):
-    members, share, head_size = plan["members"], plan["share"], plan["head_size"]
-    key_grad, value_grad = refs[members:]
-    mine = lax.axis_index("gene") % members
-    for hop in range(members):
-        start = pl.multiple_of((mine ^ hop) * (share * head_size), head_size)
-        for head in range(share):
-            columns, top = pl.ds(start + head * head_size, head_size), 2 * BLOCK * head
-            key_grad[0, :, columns] = refs[hop][top : top + BLOCK, :]
-            value_grad[0, :, columns] = refs[hop][top + BLOCK : top + 2 * BLOCK, :]
+            top = 2 * BLOCK * head
+            key_grad[0, :, columns] = owned[hop][top : top + BLOCK, :]
+            value_grad[0, :, columns] = owned[hop][top + BLOCK : top + 2 * BLOCK, :]
 
 
 def call(kernel, outs, scratch=(), smem_in=0, smem_out=False, count=0, limit=VMEM_LIMIT):
@@ -322,9 +320,9 @@
     owned = [partials[0]] + [move(partials[hop], hop) for hop in range(1, members)]
     whole = jax.ShapeDtypeStruct((1, BLOCK, row_width), low)
     part_out = jax.ShapeDtypeStruct((blocks // cells, head_count), full)
-    query_grad, *parts = call(
-        functools.partial(query_kernel, plan),
-        [whole] + [part_out] * cells,
+    parts = call(
+        functools.partial(bias_kernel, plan),
+        [part_out] * cells,
         scratch=[
             pltpu.SMEM((blocks,), jnp.int32),
             pltpu.VMEM((head_count * blocks, BLOCK), full),
@@ -332,11 +330,15 @@
         ],
         smem_in=1,
         count=blocks,
+        limit=STAGE_LIMIT,
     )(block_index.reshape(-1), *queries)
+    query_grad, key_grad, value_grad = call(
+        functools.partial(unpack_kernel, plan),
+        [whole] * 3,
+        count=blocks + members + 1,
+        limit=STAGE_LIMIT,
+    )(*queries, *owned, parts[0])
     parts = [parts[0]] + [move(parts[hop], hop, "cell", cells) for hop in range(1, cells)]
-    key_grad, value_grad = call(functools.partial(owner_kernel, plan), [whole] * 2, count=members)(
-        *owned
-    )
     bias_grad = jnp.transpose(functools.reduce(jnp.add, parts))[None]
     return (query_grad, key_grad, value_grad, bias_grad)
 

time: 83.3 us -> 77.8 us (0.934)
  Pallas kernels: 15.9 us -> 13.6 us
  local copies, waits for them, and re-layouts: 4.23 us -> 2.08 us
  waiting for transfers between devices: 23.6 us -> 22.5 us
    pallas_call x2, Pallas kernels: 4.35 us -> 2 us  [the longest x1 1.21 us: shards(): call(functools.partial(unpack_kernel, plan), [whole] * 3, count=blocks +...]
    unnamed x39 -> x17, local copies, waits for them, and re-layouts: 2.88 us -> 0.8 us
    ppermute x17, waiting for transfers between devices: 22.6 us -> 21.5 us  [move(): return lax.ppermute(array, axis, [(i, i ^ hop) for i in range(size)])]
    ppermute x17, starting transfers between devices: 31.8 us -> 32.6 us  [move(): return lax.ppermute(array, axis, [(i, i ^ hop) for i in range(size)])]
  transfers between devices with their start and end apart: 18 -> 18, of which waited for: 8 -> 7; matrix products, arithmetic and copies ran while one was open for 3% -> 3% of each run, Pallas kernels for 12% -> 12%
where the time goes in v2:
time: 77.8 us; the launch traced here: 77.5 us
  starting transfers between devices  38 us (49%)
  waiting for transfers between devices  22.5 us (29%)
  Pallas kernels  13.6 us (17%)
  local copies, waits for them, and re-layouts  2.08 us (3%)
    ppermute x17, starting transfers between devices, move(): return lax.ppermute(array, axis, [(i, i ^ hop) for i in range(size)])  32.6 us
    ppermute x17, waiting for transfers between devices, move(): return lax.ppermute(array, axis, [(i, i ^ hop) for i in range(size)])  21.5 us
    pallas_call x2, Pallas kernels, stage(): call(functools.partial(stage_kernel, plan, places, first, last), [query_o...  6.43 us
    all_to_all x1, starting transfers between devices, exchange(): return lax.all_to_all(array, 'gene', 0, 0, axis_index_groups=groups)  5.39 us
    pallas_call x1, Pallas kernels, shards(): call(functools.partial(pack_kernel, plan), [far_in] * members + [near_in]...  3.35 us
    pallas_call x1, Pallas kernels, shards(): call(functools.partial(table_kernel, plan), [jax.ShapeDtypeStruct((blocks...  1.78 us
  transfers between devices with their start and end apart: 18, of which 7 were waited for; matrix products, arithmetic and copies ran while one was open for 3% of the time, Pallas kernels for 12%

profile of v2, /device:TPU:0, one launch (start us, length us, event | category | flops | bytes accessed | tf_op | source)
XLA Modules:
  0.0 77.5 jit_solution(14460393524333821461)
XLA Ops:
  0.6 3.3 %shard_map.121 = (bf16[784,128]{1,0:T(8,128)(2,1)}, bf16[784,128]{1,0:T(8,128)(2,1)}, bf16[784,128]{1,0:T(8,128)(2,1)}, bf16[784,128]{1,0:T(8,128)(2,1)}, bf16[4,1552,128]{2,1,0:T(8,128)(2,1)}) custom-call(bf16[1,128,1536]{2,1,0:T(8,128)(2,1)} %query.1, bf16[1,128,1536]{2,1,0:T(8,128)(2,1)} %key.1, bf16[1,128,1536]{2,1,0:T(8,128)(2,1)} %value.1, ...), custom_call_target="tpu_custom_call" | custom-call | tf_op jit(solution)/shard_map/pallas_call | solution.py:277
  4.0 0.0 copy-start.2
  4.0 0.0 copy-start.3
  4.0 5.4 %all-to-all-start = ((bf16[4,1552,128]{2,1,0:T(8,128)(2,1)}), bf16[4,1552,128]{2,1,0:T(8,128)(2,1)S(1)}, u32[]{:S(2)}, u32[]{:S(2)}) async-start(bf16[4,1552,128]{2,1,0:T(8,128)(2,1)} %get-tuple-element.30), calls=%async_computation | async-start | bytes 3178496 | tf_op jit(solution)/shard_map/all_to_all | solution.py:283
  9.4 2.6 %collective-permute-start = (bf16[784,128]{1,0:T(8,128)(2,1)S(1)}, bf16[784,128]{1,0:T(8,128)(2,1)S(1)}, u32[]{:S(2)}, u32[]{:S(2)}) collective-permute-start(bf16[784,128]{1,0:T(8,128)(2,1)S(1)} %copy-done.7), channel_id=1, source_target_pairs={{0,4},{1,5},{2,6},{3,7},{4,0},{5,1},{6,2},{7,3},{8,12},{9,13},{10,... | collective-permute-start | bytes 602120 | tf_op jit(solution)/shard_map/ppermute | solution.py:286
  12.0 1.8 %collective-permute-start.1 = (bf16[784,128]{1,0:T(8,128)(2,1)S(1)}, bf16[784,128]{1,0:T(8,128)(2,1)S(1)}, u32[]{:S(2)}, u32[]{:S(2)}) collective-permute-start(bf16[784,128]{1,0:T(8,128)(2,1)S(1)} %copy-done.6), channel_id=1, source_target_pairs={{0,5},{1,4},{2,7},{3,6},{4,1},{5,0},{6,3},{7,2},{8,13},{9,12},{10,... | collective-permute-start | bytes 602120 | tf_op jit(solution)/shard_map/ppermute | solution.py:286
  13.8 3.5 %collective-permute-start.7 = (bf16[784,128]{1,0:T(8,128)(2,1)S(1)}, bf16[784,128]{1,0:T(8,128)(2,1)S(1)}, u32[]{:S(2)}, u32[]{:S(2)}) collective-permute-start(bf16[784,128]{1,0:T(8,128)(2,1)S(1)} %copy-done.5), channel_id=1, source_target_pairs={{0,6},{1,7},{2,4},{3,5},{4,2},{5,3},{6,0},{7,1},{8,14},{9,15},{10,... | collective-permute-start | bytes 602120 | tf_op jit(solution)/shard_map/ppermute | solution.py:286
  17.3 0.1 collective-permute-start.8
  17.4 0.1 copy.13
  17.5 0.7 reshape.15.bias
  18.2 0.6 reshape.16.index
  18.8 1.8 %shard_map.120.shift = f32[96]{0:T(128)} custom-call(f32[768]{0:T(1024)} %reshape.15.bias, s32[64]{0:T(128)} %reshape.16.index, s32[8]{0:T(128)} %count.1), custom_call_target="tpu_custom_call" | custom-call | tf_op jit(solution)/shard_map/pallas_call | solution.py:290
  20.6 11.6 %collective-permute-done.refs_1_ = bf16[784,128]{1,0:T(8,128)(2,1)S(1)} collective-permute-done((bf16[784,128]{1,0:T(8,128)(2,1)S(1)}, bf16[784,128]{1,0:T(8,128)(2,1)S(1)}, u32[]{:S(2)}, u32[]{:S(2)}) %collective-permute-start) | collective-permute-done | bytes 200736 | tf_op jit(solution)/shard_map/ppermute | solution.py:286
  32.1 4.3 %collective-permute-done.1.refs_2_ = bf16[784,128]{1,0:T(8,128)(2,1)S(1)} collective-permute-done((bf16[784,128]{1,0:T(8,128)(2,1)S(1)}, bf16[784,128]{1,0:T(8,128)(2,1)S(1)}, u32[]{:S(2)}, u32[]{:S(2)}) %collective-permute-start.1) | collective-permute-done | bytes 200736 | tf_op jit(solution)/shard_map/ppermute | solution.py:286
  36.4 1.0 %all-to-all-done.refs_0_ = bf16[4,1552,128]{2,1,0:T(8,128)(2,1)S(1)} async-done(((bf16[4,1552,128]{2,1,0:T(8,128)(2,1)}), bf16[4,1552,128]{2,1,0:T(8,128)(2,1)S(1)}, u32[]{:S(2)}, u32[]{:S(2)}) %all-to-all-start) | async-done | bytes 1589280 | tf_op jit(solution)/shard_map/all_to_all | solution.py:283
  37.5 0.7 copy-done.1
  38.1 4.2 %shard_map.122 = (bf16[400,128]{1,0:T(8,128)(2,1)S(1)}, bf16[400,128]{1,0:T(8,128)(2,1)S(1)}, bf16[400,128]{1,0:T(8,128)(2,1)S(1)}, bf16[400,128]{1,0:T(8,128)(2...) custom-call(f32[96]{0:T(128)S(1)} %copy-done.1, ...), custom_call_target="tpu_custom_call" | custom-call | tf_op jit(solution)/shard_map/pallas_call | solution.py:304
  42.3 1.5 %collective-permute-start.2 = (bf16[400,128]{1,0:T(8,128)(2,1)S(1)}, bf16[400,128]{1,0:T(8,128)(2,1)S(1)}, u32[]{:S(2)}, u32[]{:S(2)}) collective-permute-start(bf16[400,128]{1,0:T(8,128)(2,1)S(1)} %get-tuple-element.34), channel_id=1, source_target_pairs={{0,1},{1,0},{2,3},{3,2},{4,5},{5,4},{6,7},{7,6},{8,9},{9,8},{10,11... | collective-permute-start | bytes 307208 | tf_op jit(solution)/shard_map/ppermute | solution.py:286
  43.8 4.0 %collective-permute-start.3 = (bf16[400,128]{1,0:T(8,128)(2,1)S(1)}, bf16[400,128]{1,0:T(8,128)(2,1)S(1)}, u32[]{:S(2)}, u32[]{:S(2)}) collective-permute-start(bf16[400,128]{1,0:T(8,128)(2,1)S(1)} %get-tuple-element.35), channel_id=1, source_target_pairs={{0,2},{1,3},{2,0},{3,1},{4,6},{5,7},{6,4},{7,5},{8,10},{9,11},{10,... | collective-permute-start | bytes 307208 | tf_op jit(solution)/shard_map/ppermute | solution.py:286
  47.8 0.9 %collective-permute-start.4 = (bf16[400,128]{1,0:T(8,128)(2,1)S(1)}, bf16[400,128]{1,0:T(8,128)(2,1)S(1)}, u32[]{:S(2)}, u32[]{:S(2)}) collective-permute-start(bf16[400,128]{1,0:T(8,128)(2,1)S(1)} %get-tuple-element.36), channel_id=1, source_target_pairs={{0,3},{1,2},{2,1},{3,0},{4,7},{5,6},{6,5},{7,4},{8,11},{9,10},{10,... | collective-permute-start | bytes 307208 | tf_op jit(solution)/shard_map/ppermute | solution.py:286
  48.7 0.0 collective-permute-done.7.refs_1_
  48.7 6.9 %collective-permute-start.5 = (bf16[400,128]{1,0:T(8,128)(2,1)S(1)}, bf16[400,128]{1,0:T(8,128)(2,1)S(1)}, u32[]{:S(2)}, u32[]{:S(2)}) collective-permute-start(bf16[400,128]{1,0:T(8,128)(2,1)S(1)} %get-tuple-element.37), channel_id=1, source_target_pairs={{0,4},{1,5},{2,6},{3,7},{4,0},{5,1},{6,2},{7,3},{8,12},{9,13},{10,... | collective-permute-start | bytes 307208 | tf_op jit(solution)/shard_map/ppermute | solution.py:286
  55.6 0.0 collective-permute-done.8.refs_2_
  55.6 1.0 %collective-permute-start.6 = (bf16[400,128]{1,0:T(8,128)(2,1)S(1)}, bf16[400,128]{1,0:T(8,128)(2,1)S(1)}, u32[]{:S(2)}, u32[]{:S(2)}) collective-permute-start(bf16[400,128]{1,0:T(8,128)(2,1)S(1)} %get-tuple-element.38), channel_id=1, source_target_pairs={{0,5},{1,4},{2,7},{3,6},{4,1},{5,0},{6,3},{7,2},{8,13},{9,12},{10,... | collective-permute-start | bytes 307208 | tf_op jit(solution)/shard_map/ppermute | solution.py:286
  56.6 2.3 %shard_map.123 = (bf16[400,128]{1,0:T(8,128)(2,1)S(1)}, bf16[400,128]{1,0:T(8,128)(2,1)S(1)}, bf16[768,128]{1,0:T(8,128)(2,1)S(1)}, bf16[768,128]{1,0:T(8,128)(2...) custom-call(f32[96]{0:T(128)S(1)} %copy-done.1, bf16[4,1552,128]{2,1,0:T(8,128)(2,1)S(1)} %all-to-all-done.refs_0_, ...), custom_call_target="tpu_custom_call" | custom-call | tf_op jit(solution)/shard_map/pallas_call | solution.py:304
  58.9 0.0 collective-permute-done.2.refs_1_
  58.9 4.4 %collective-permute-start.9 = (bf16[400,128]{1,0:T(8,128)(2,1)S(1)}, bf16[400,128]{1,0:T(8,128)(2,1)S(1)}, u32[]{:S(2)}, u32[]{:S(2)}) collective-permute-start(bf16[400,128]{1,0:T(8,128)(2,1)S(1)} %get-tuple-element.43), channel_id=1, source_target_pairs={{0,6},{1,7},{2,4},{3,5},{4,2},{5,3},{6,0},{7,1},{8,14},{9,15},{10,... | collective-permute-start | bytes 307208 | tf_op jit(solution)/shard_map/ppermute | solution.py:286
  63.2 0.0 collective-permute-done.3.refs_2_
  63.2 0.0 collective-permute-start.10
  63.2 0.0 collective-permute-done.4.refs_3_
  63.3 1.5 %collective-permute-start.11 = (bf16[768,128]{1,0:T(8,128)(2,1)S(1)}, bf16[768,128]{1,0:T(8,128)(2,1)S(1)}, u32[]{:S(2)}, u32[]{:S(2)}) collective-permute-start(bf16[768,128]{1,0:T(8,128)(2,1)S(1)} %get-tuple-element.46), channel_id=1, source_target_pairs={{0,1},{1,0},{2,3},{3,2},{4,5},{5,4},{6,7},{7,6},{8,9},{9,8},{10,11... | collective-permute-start | bytes 589832 | tf_op jit(solution)/shard_map/ppermute | solution.py:286
  64.8 0.0 collective-permute-done.5.refs_4_
  64.8 0.0 collective-permute-start.12
  64.8 0.0 collective-permute-done.6.refs_5_
  64.8 2.7 %collective-permute-start.13 = (bf16[768,128]{1,0:T(8,128)(2,1)S(1)}, bf16[768,128]{1,0:T(8,128)(2,1)S(1)}, u32[]{:S(2)}, u32[]{:S(2)}) collective-permute-start(bf16[768,128]{1,0:T(8,128)(2,1)S(1)} %get-tuple-element.48), channel_id=1, source_target_pairs={{0,3},{1,2},{2,1},{3,0},{4,7},{5,6},{6,5},{7,4},{8,11},{9,10},{10,... | collective-permute-start | bytes 589832 | tf_op jit(solution)/shard_map/ppermute | solution.py:286
  67.5 0.0 collective-permute-done.9.refs_6_
  67.6 3.1 %collective-permute-done.10.refs_7_ = bf16[400,128]{1,0:T(8,128)(2,1)S(1)} collective-permute-done((bf16[400,128]{1,0:T(8,128)(2,1)S(1)}, bf16[400,128]{1,0:T(8,128)(2,1)S(1)}, u32[]{:S(2)}, u32[]{:S(2)}) %collective-permute-start.10) | collective-permute-done | bytes 102432 | tf_op jit(solution)/shard_map/ppermute | solution.py:286
  70.7 0.8 %shard_map.124 = (f32[2,12]{1,0:T(2,128)S(1)}, f32[2,12]{1,0:T(2,128)S(1)}, f32[2,12]{1,0:T(2,128)S(1)}, f32[2,12]{1,0:T(2,128)S(1)}) custom-call(s32[64]{0:T(128)S(1)} %copy-done, bf16[400,128]{1,0:T(8,128)(2,1)S(1)} %get-tuple-element.33.refs_0_, bf16[400,128]{1,0:T(8,128)(2,1)S(1)} %collective-permute-done.2.refs_1_, ...), custom_call_target="tpu_custom_call" | custom-call | tf_op jit(solution)/shard_map/pallas_call | solution.py:323
  71.5 0.1 collective-permute-start.16
  71.6 1.6 %collective-permute-start.15 = (f32[2,12]{1,0:T(2,128)S(1)}, f32[2,12]{1,0:T(2,128)S(1)}, u32[]{:S(2)}, u32[]{:S(2)}) collective-permute-start(f32[2,12]{1,0:T(2,128)S(1)} %get-tuple-element.54), channel_id=1, source_target_pairs={{0,16},{8,24},{16,0},{24,8},{1,17},{9,25},{17,1},{25,9},{2,18},{10... | collective-permute-start | bytes 296 | tf_op jit(solution)/shard_map/ppermute | solution.py:286
  73.1 1.4 %collective-permute-done.16 = f32[2,12]{1,0:T(2,128)S(1)} collective-permute-done((f32[2,12]{1,0:T(2,128)S(1)}, f32[2,12]{1,0:T(2,128)S(1)}, u32[]{:S(2)}, u32[]{:S(2)}) %collective-permute-start.16) | collective-permute-done | bytes 128 | tf_op jit(solution)/shard_map/ppermute | solution.py:286
  74.6 0.1 collective-permute-start.14
  74.7 0.5 collective-permute-done.15
  75.2 0.5 collective-permute-done.14
  75.7 0.6 add_bitcast_fusion
  76.3 0.0 collective-permute-done.11.refs_9_
  76.3 0.0 collective-permute-done.12.refs_10_
  76.3 1.2 %shard_map.125 = (bf16[1,128,1536]{2,1,0:T(8,128)(2,1)}, bf16[1,128,1536]{2,1,0:T(8,128)(2,1)}, bf16[1,128,1536]{2,1,0:T(8,128)(2,1)}) custom-call(bf16[400,128]{1,0:T(8,128)(2,1)S(1)} %get-tuple-element.33.refs_0_, bf16[400,128]{1,0:T(8,128)(2,1)S(1)} %collective-permute-done.2.refs_1_, bf16[400,128]{1,0:T(8,128)(2,1)S(1)} %collective-permute-done.3.refs_2_, ...), custom_call_target="tpu_custom_call" | custom-call | tf_op jit(solution)/shard_map/pallas_call | solution.py:335
  (14 shorter events, 0.0 us)
Async XLA Ops:
  4.0 5.4 %copy-start.7 = (bf16[784,128]{1,0:T(8,128)(2,1)S(1)}, bf16[784,128]{1,0:T(8,128)(2,1)}, u32[]{:S(2)}) copy-start(bf16[784,128]{1,0:T(8,128)(2,1)} %get-tuple-element.31) | copy-start | bytes 602116
  4.0 8.0 %copy-start.6 = (bf16[784,128]{1,0:T(8,128)(2,1)S(1)}, bf16[784,128]{1,0:T(8,128)(2,1)}, u32[]{:S(2)}) copy-start(bf16[784,128]{1,0:T(8,128)(2,1)} %get-tuple-element.32) | copy-start | bytes 602116
  4.0 9.8 %copy-start.5 = (bf16[784,128]{1,0:T(8,128)(2,1)S(1)}, bf16[784,128]{1,0:T(8,128)(2,1)}, u32[]{:S(2)}) copy-start(bf16[784,128]{1,0:T(8,128)(2,1)} %get-tuple-element.39) | copy-start | bytes 602116
  4.0 13.3 %copy-start.4 = (bf16[784,128]{1,0:T(8,128)(2,1)S(1)}, bf16[784,128]{1,0:T(8,128)(2,1)}, u32[]{:S(2)}) copy-start(bf16[784,128]{1,0:T(8,128)(2,1)} %get-tuple-element.40) | copy-start | bytes 602116
  4.0 13.4 %copy-start.2 = (f32[8,12,8]{1,2,0:T(8,128)S(1)}, f32[8,12,8]{1,2,0:T(8,128)}, u32[]{:S(2)}) copy-start(f32[8,12,8]{1,2,0:T(8,128)} %param.15) | copy-start | bytes 9220
  4.0 14.2 %copy-start.3 = (s32[8,8]{1,0:T(8,128)S(1)}, s32[8,8]{1,0:T(8,128)}, u32[]{:S(2)}) copy-start(s32[8,8]{1,0:T(8,128)} %param.16) | copy-start | bytes 772
  4.0 33.4 %all-to-all-start = ((bf16[4,1552,128]{2,1,0:T(8,128)(2,1)}), bf16[4,1552,128]{2,1,0:T(8,128)(2,1)S(1)}, u32[]{:S(2)}, u32[]{:S(2)}) async-start(bf16[4,1552,128]{2,1,0:T(8,128)(2,1)} %get-tuple-element.30), calls=%async_computation | async-start | bytes 3178496 | tf_op jit(solution)/shard_map/all_to_all | solution.py:283
  9.4 22.7 %collective-permute-start = (bf16[784,128]{1,0:T(8,128)(2,1)S(1)}, bf16[784,128]{1,0:T(8,128)(2,1)S(1)}, u32[]{:S(2)}, u32[]{:S(2)}) collective-permute-start(bf16[784,128]{1,0:T(8,128)(2,1)S(1)} %copy-done.7), channel_id=1, source_target_pairs={{0,4},{1,5},{2,6},{3,7},{4,0},{5,1},{6,2},{7,3},{8,12},{9,13},{10,... | collective-permute-start | bytes 602120 | tf_op jit(solution)/shard_map/ppermute | solution.py:286
  12.0 24.4 %collective-permute-start.1 = (bf16[784,128]{1,0:T(8,128)(2,1)S(1)}, bf16[784,128]{1,0:T(8,128)(2,1)S(1)}, u32[]{:S(2)}, u32[]{:S(2)}) collective-permute-start(bf16[784,128]{1,0:T(8,128)(2,1)S(1)} %copy-done.6), channel_id=1, source_target_pairs={{0,5},{1,4},{2,7},{3,6},{4,1},{5,0},{6,3},{7,2},{8,13},{9,12},{10,... | collective-permute-start | bytes 602120 | tf_op jit(solution)/shard_map/ppermute | solution.py:286
  13.8 34.9 %collective-permute-start.7 = (bf16[784,128]{1,0:T(8,128)(2,1)S(1)}, bf16[784,128]{1,0:T(8,128)(2,1)S(1)}, u32[]{:S(2)}, u32[]{:S(2)}) collective-permute-start(bf16[784,128]{1,0:T(8,128)(2,1)S(1)} %copy-done.5), channel_id=1, source_target_pairs={{0,6},{1,7},{2,4},{3,5},{4,2},{5,3},{6,0},{7,1},{8,14},{9,15},{10,... | collective-permute-start | bytes 602120 | tf_op jit(solution)/shard_map/ppermute | solution.py:286
  17.3 38.3 %collective-permute-start.8 = (bf16[784,128]{1,0:T(8,128)(2,1)S(1)}, bf16[784,128]{1,0:T(8,128)(2,1)S(1)}, u32[]{:S(2)}, u32[]{:S(2)}) collective-permute-start(bf16[784,128]{1,0:T(8,128)(2,1)S(1)} %copy-done.4), channel_id=1, source_target_pairs={{0,7},{1,6},{2,5},{3,4},{4,3},{5,2},{6,1},{7,0},{8,15},{9,14},{10,... | collective-permute-start | bytes 602120 | tf_op jit(solution)/shard_map/ppermute | solution.py:286
  37.5 0.7 copy-start.1
  42.3 16.6 %collective-permute-start.2 = (bf16[400,128]{1,0:T(8,128)(2,1)S(1)}, bf16[400,128]{1,0:T(8,128)(2,1)S(1)}, u32[]{:S(2)}, u32[]{:S(2)}) collective-permute-start(bf16[400,128]{1,0:T(8,128)(2,1)S(1)} %get-tuple-element.34), channel_id=1, source_target_pairs={{0,1},{1,0},{2,3},{3,2},{4,5},{5,4},{6,7},{7,6},{8,9},{9,8},{10,11... | collective-permute-start | bytes 307208 | tf_op jit(solution)/shard_map/ppermute | solution.py:286
  43.8 19.4 %collective-permute-start.3 = (bf16[400,128]{1,0:T(8,128)(2,1)S(1)}, bf16[400,128]{1,0:T(8,128)(2,1)S(1)}, u32[]{:S(2)}, u32[]{:S(2)}) collective-permute-start(bf16[400,128]{1,0:T(8,128)(2,1)S(1)} %get-tuple-element.35), channel_id=1, source_target_pairs={{0,2},{1,3},{2,0},{3,1},{4,6},{5,7},{6,4},{7,5},{8,10},{9,11},{10,... | collective-permute-start | bytes 307208 | tf_op jit(solution)/shard_map/ppermute | solution.py:286
  47.8 15.4 %collective-permute-start.4 = (bf16[400,128]{1,0:T(8,128)(2,1)S(1)}, bf16[400,128]{1,0:T(8,128)(2,1)S(1)}, u32[]{:S(2)}, u32[]{:S(2)}) collective-permute-start(bf16[400,128]{1,0:T(8,128)(2,1)S(1)} %get-tuple-element.36), channel_id=1, source_target_pairs={{0,3},{1,2},{2,1},{3,0},{4,7},{5,6},{6,5},{7,4},{8,11},{9,10},{10,... | collective-permute-start | bytes 307208 | tf_op jit(solution)/shard_map/ppermute | solution.py:286
  48.7 16.1 %collective-permute-start.5 = (bf16[400,128]{1,0:T(8,128)(2,1)S(1)}, bf16[400,128]{1,0:T(8,128)(2,1)S(1)}, u32[]{:S(2)}, u32[]{:S(2)}) collective-permute-start(bf16[400,128]{1,0:T(8,128)(2,1)S(1)} %get-tuple-element.37), channel_id=1, source_target_pairs={{0,4},{1,5},{2,6},{3,7},{4,0},{5,1},{6,2},{7,3},{8,12},{9,13},{10,... | collective-permute-start | bytes 307208 | tf_op jit(solution)/shard_map/ppermute | solution.py:286
  55.6 9.2 %collective-permute-start.6 = (bf16[400,128]{1,0:T(8,128)(2,1)S(1)}, bf16[400,128]{1,0:T(8,128)(2,1)S(1)}, u32[]{:S(2)}, u32[]{:S(2)}) collective-permute-start(bf16[400,128]{1,0:T(8,128)(2,1)S(1)} %get-tuple-element.38), channel_id=1, source_target_pairs={{0,5},{1,4},{2,7},{3,6},{4,1},{5,0},{6,3},{7,2},{8,13},{9,12},{10,... | collective-permute-start | bytes 307208 | tf_op jit(solution)/shard_map/ppermute | solution.py:286
  56.6 14.1 %copy-start = (s32[64]{0:T(128)S(1)}, s32[64]{0:T(128)}, u32[]{:S(2)}) copy-start(s32[64]{0:T(128)} %reshape.16.index) | copy-start | bytes 772
  58.9 8.7 %collective-permute-start.9 = (bf16[400,128]{1,0:T(8,128)(2,1)S(1)}, bf16[400,128]{1,0:T(8,128)(2,1)S(1)}, u32[]{:S(2)}, u32[]{:S(2)}) collective-permute-start(bf16[400,128]{1,0:T(8,128)(2,1)S(1)} %get-tuple-element.43), channel_id=1, source_target_pairs={{0,6},{1,7},{2,4},{3,5},{4,2},{5,3},{6,0},{7,1},{8,14},{9,15},{10,... | collective-permute-start | bytes 307208 | tf_op jit(solution)/shard_map/ppermute | solution.py:286
  63.2 7.5 %collective-permute-start.10 = (bf16[400,128]{1,0:T(8,128)(2,1)S(1)}, bf16[400,128]{1,0:T(8,128)(2,1)S(1)}, u32[]{:S(2)}, u32[]{:S(2)}) collective-permute-start(bf16[400,128]{1,0:T(8,128)(2,1)S(1)} %get-tuple-element.44), channel_id=1, source_target_pairs={{0,7},{1,6},{2,5},{3,4},{4,3},{5,2},{6,1},{7,0},{8,15},{9,14},{10,... | collective-permute-start | bytes 307208 | tf_op jit(solution)/shard_map/ppermute | solution.py:286
  63.3 13.0 %collective-permute-start.11 = (bf16[768,128]{1,0:T(8,128)(2,1)S(1)}, bf16[768,128]{1,0:T(8,128)(2,1)S(1)}, u32[]{:S(2)}, u32[]{:S(2)}) collective-permute-start(bf16[768,128]{1,0:T(8,128)(2,1)S(1)} %get-tuple-element.46), channel_id=1, source_target_pairs={{0,1},{1,0},{2,3},{3,2},{4,5},{5,4},{6,7},{7,6},{8,9},{9,8},{10,11... | collective-permute-start | bytes 589832 | tf_op jit(solution)/shard_map/ppermute | solution.py:286
  64.8 11.5 %collective-permute-start.12 = (bf16[768,128]{1,0:T(8,128)(2,1)S(1)}, bf16[768,128]{1,0:T(8,128)(2,1)S(1)}, u32[]{:S(2)}, u32[]{:S(2)}) collective-permute-start(bf16[768,128]{1,0:T(8,128)(2,1)S(1)} %get-tuple-element.47), channel_id=1, source_target_pairs={{0,2},{1,3},{2,0},{3,1},{4,6},{5,7},{6,4},{7,5},{8,10},{9,11},{10,... | collective-permute-start | bytes 589832 | tf_op jit(solution)/shard_map/ppermute | solution.py:286
  64.8 11.5 %collective-permute-start.13 = (bf16[768,128]{1,0:T(8,128)(2,1)S(1)}, bf16[768,128]{1,0:T(8,128)(2,1)S(1)}, u32[]{:S(2)}, u32[]{:S(2)}) collective-permute-start(bf16[768,128]{1,0:T(8,128)(2,1)S(1)} %get-tuple-element.48), channel_id=1, source_target_pairs={{0,3},{1,2},{2,1},{3,0},{4,7},{5,6},{6,5},{7,4},{8,11},{9,10},{10,... | collective-permute-start | bytes 589832 | tf_op jit(solution)/shard_map/ppermute | solution.py:286
  71.5 3.1 %collective-permute-start.16 = (f32[2,12]{1,0:T(2,128)S(1)}, f32[2,12]{1,0:T(2,128)S(1)}, u32[]{:S(2)}, u32[]{:S(2)}) collective-permute-start(f32[2,12]{1,0:T(2,128)S(1)} %get-tuple-element.55), channel_id=1, source_target_pairs={{0,24},{8,16},{16,8},{24,0},{1,25},{9,17},{17,9},{25,1},{2,26},{10... | collective-permute-start | bytes 296 | tf_op jit(solution)/shard_map/ppermute | solution.py:286
  71.6 3.6 %collective-permute-start.15 = (f32[2,12]{1,0:T(2,128)S(1)}, f32[2,12]{1,0:T(2,128)S(1)}, u32[]{:S(2)}, u32[]{:S(2)}) collective-permute-start(f32[2,12]{1,0:T(2,128)S(1)} %get-tuple-element.54), channel_id=1, source_target_pairs={{0,16},{8,24},{16,0},{24,8},{1,17},{9,25},{17,1},{25,9},{2,18},{10... | collective-permute-start | bytes 296 | tf_op jit(solution)/shard_map/ppermute | solution.py:286
  74.6 1.1 %collective-permute-start.14 = (f32[2,12]{1,0:T(2,128)S(1)}, f32[2,12]{1,0:T(2,128)S(1)}, u32[]{:S(2)}, u32[]{:S(2)}) collective-permute-start(f32[2,12]{1,0:T(2,128)S(1)} %get-tuple-element.53), channel_id=1, source_target_pairs={{0,8},{8,0},{16,24},{24,16},{1,9},{9,1},{17,25},{25,17},{2,10},{10... | collective-permute-start | bytes 296 | tf_op jit(solution)/shard_map/ppermute | solution.py:286

commit v3 on v2

--- a/solution.py
+++ b/solution.py
@@ -12,7 +12,6 @@
 ROW_TILE = 16
 VMEM_LIMIT = 60 * 1024 * 1024
 STAGE_LIMIT = 40 * 1024 * 1024
-FAR_STAGES = 1
 LOG2E = math.log2(math.e)
 UNLISTED = -1e30
 
@@ -207,7 +206,8 @@
     blocks, members, share = plan["blocks"], plan["members"], plan["share"]
     head_size = plan["head_size"]
     pieces, owned = refs[:blocks], refs[blocks : blocks + members]
-    query_grad, key_grad, value_grad = refs[-3:]
+    query_grad, key_grad, value_grad, passed = refs[-4:]
+    passed[...] = refs[blocks + members][...]
     mine = lax.axis_index("gene") % members
     for hop in range(members):
         start = pl.multiple_of((mine ^ hop) * (share * head_size), head_size)
@@ -223,7 +223,7 @@
             value_grad[0, :, columns] = owned[hop][top + BLOCK : top + 2 * BLOCK, :]
 
 
-def call(kernel, outs, scratch=(), smem_in=0, smem_out=False, count=0, limit=VMEM_LIMIT):
+def call(kernel, outs, scratch=(), smem_in=0, smem_out=False, count=0, limit=VMEM_LIMIT, flops=None):
     places = [pl.BlockSpec(memory_space=pltpu.SMEM)] * smem_in
     places += [pl.BlockSpec(memory_space=pltpu.VMEM)] * count
     space = pltpu.SMEM if smem_out else pltpu.VMEM
@@ -234,6 +234,7 @@
         out_specs=[pl.BlockSpec(memory_space=space)] * len(outs),
         scratch_shapes=list(scratch),
         compiler_params=pltpu.CompilerParams(vmem_limit_bytes=limit),
+        cost_estimate=flops and pl.CostEstimate(flops=flops, bytes_accessed=0, transcendentals=0),
     )
 
 
@@ -331,14 +332,15 @@
         smem_in=1,
         count=blocks,
         limit=STAGE_LIMIT,
+        flops=40000000000,
     )(block_index.reshape(-1), *queries)
-    query_grad, key_grad, value_grad = call(
+    query_grad, key_grad, value_grad, own_part = call(
         functools.partial(unpack_kernel, plan),
-        [whole] * 3,
+        [whole] * 3 + [part_out],
         count=blocks + members + 1,
         limit=STAGE_LIMIT,
     )(*queries, *owned, parts[0])
-    parts = [parts[0]] + [move(parts[hop], hop, "cell", cells) for hop in range(1, cells)]
+    parts = [own_part] + [move(parts[hop], hop, "cell", cells) for hop in range(1, cells)]
     bias_grad = jnp.transpose(functools.reduce(jnp.add, parts))[None]
     return (query_grad, key_grad, value_grad, bias_grad)
 

time: 77.8 us -> 76.1 us (0.978)
  waiting for transfers between devices: 22.5 us -> 20.6 us
    ppermute x17, waiting for transfers between devices: 21.5 us -> 19.6 us  [move(): return lax.ppermute(array, axis, [(i, i ^ hop) for i in range(size)])]
  transfers between devices with their start and end apart: 18 -> 18, of which waited for: 7 -> 6; matrix products, arithmetic and copies ran while one was open for 3% -> 2% of each run, Pallas kernels for 12% -> 13%
where the time goes in v3:
time: 76.1 us; the launch traced here: 75.8 us
  starting transfers between devices  38.2 us (50%)
  waiting for transfers between devices  20.6 us (27%)
  Pallas kernels  13.6 us (18%)
  local copies, waits for them, and re-layouts  2.08 us (3%)
    ppermute x17, starting transfers between devices, move(): return lax.ppermute(array, axis, [(i, i ^ hop) for i in range(size)])  32.8 us
    ppermute x17, waiting for transfers between devices, move(): return lax.ppermute(array, axis, [(i, i ^ hop) for i in range(size)])  19.6 us
    pallas_call x2, Pallas kernels, stage(): call(functools.partial(stage_kernel, plan, places, first, last), [query_o...  6.43 us
    all_to_all x1, starting transfers between devices, exchange(): return lax.all_to_all(array, 'gene', 0, 0, axis_index_groups=groups)  5.39 us
    pallas_call x1, Pallas kernels, shards(): call(functools.partial(pack_kernel, plan), [far_in] * members + [near_in]...  3.35 us
    pallas_call x1, Pallas kernels, shards(): call(functools.partial(table_kernel, plan), [jax.ShapeDtypeStruct((blocks...  1.78 us
  transfers between devices with their start and end apart: 18, of which 6 were waited for; matrix products, arithmetic and copies ran while one was open for 2% of the time, Pallas kernels for 13%

profile of v3, /device:TPU:0, one launch (start us, length us, event | category | flops | bytes accessed | tf_op | source)
XLA Modules:
  0.0 75.8 jit_solution(5189576688016791533)
XLA Ops:
  0.6 3.3 %shard_map.121 = (bf16[784,128]{1,0:T(8,128)(2,1)}, bf16[784,128]{1,0:T(8,128)(2,1)}, bf16[784,128]{1,0:T(8,128)(2,1)}, bf16[784,128]{1,0:T(8,128)(2,1)}, bf16[4,1552,128]{2,1,0:T(8,128)(2,1)}) custom-call(bf16[1,128,1536]{2,1,0:T(8,128)(2,1)} %query.1, bf16[1,128,1536]{2,1,0:T(8,128)(2,1)} %key.1, bf16[1,128,1536]{2,1,0:T(8,128)(2,1)} %value.1, ...), custom_call_target="tpu_custom_call" | custom-call | tf_op jit(solution)/shard_map/pallas_call | solution.py:278
  4.0 0.0 copy-start.2
  4.0 0.0 copy-start.3
  4.0 5.4 %all-to-all-start = ((bf16[4,1552,128]{2,1,0:T(8,128)(2,1)}), bf16[4,1552,128]{2,1,0:T(8,128)(2,1)S(1)}, u32[]{:S(2)}, u32[]{:S(2)}) async-start(bf16[4,1552,128]{2,1,0:T(8,128)(2,1)} %get-tuple-element.31), calls=%async_computation | async-start | bytes 3178496 | tf_op jit(solution)/shard_map/all_to_all | solution.py:284
  9.4 2.6 %collective-permute-start = (bf16[784,128]{1,0:T(8,128)(2,1)S(1)}, bf16[784,128]{1,0:T(8,128)(2,1)S(1)}, u32[]{:S(2)}, u32[]{:S(2)}) collective-permute-start(bf16[784,128]{1,0:T(8,128)(2,1)S(1)} %copy-done.7), channel_id=1, source_target_pairs={{0,4},{1,5},{2,6},{3,7},{4,0},{5,1},{6,2},{7,3},{8,12},{9,13},{10,... | collective-permute-start | bytes 602120 | tf_op jit(solution)/shard_map/ppermute | solution.py:287
  12.0 1.8 %collective-permute-start.1 = (bf16[784,128]{1,0:T(8,128)(2,1)S(1)}, bf16[784,128]{1,0:T(8,128)(2,1)S(1)}, u32[]{:S(2)}, u32[]{:S(2)}) collective-permute-start(bf16[784,128]{1,0:T(8,128)(2,1)S(1)} %copy-done.6), channel_id=1, source_target_pairs={{0,5},{1,4},{2,7},{3,6},{4,1},{5,0},{6,3},{7,2},{8,13},{9,12},{10,... | collective-permute-start | bytes 602120 | tf_op jit(solution)/shard_map/ppermute | solution.py:287
  13.8 3.5 %collective-permute-start.7 = (bf16[784,128]{1,0:T(8,128)(2,1)S(1)}, bf16[784,128]{1,0:T(8,128)(2,1)S(1)}, u32[]{:S(2)}, u32[]{:S(2)}) collective-permute-start(bf16[784,128]{1,0:T(8,128)(2,1)S(1)} %copy-done.5), channel_id=1, source_target_pairs={{0,6},{1,7},{2,4},{3,5},{4,2},{5,3},{6,0},{7,1},{8,14},{9,15},{10,... | collective-permute-start | bytes 602120 | tf_op jit(solution)/shard_map/ppermute | solution.py:287
  17.3 0.1 collective-permute-start.8
  17.4 0.1 copy.13
  17.5 0.7 reshape.15.bias
  18.2 0.6 reshape.16.index
  18.8 1.8 %shard_map.120.shift = f32[96]{0:T(128)} custom-call(f32[768]{0:T(1024)} %reshape.15.bias, s32[64]{0:T(128)} %reshape.16.index, s32[8]{0:T(128)} %count.1), custom_call_target="tpu_custom_call" | custom-call | tf_op jit(solution)/shard_map/pallas_call | solution.py:291
  20.6 11.6 %collective-permute-done.refs_1_ = bf16[784,128]{1,0:T(8,128)(2,1)S(1)} collective-permute-done((bf16[784,128]{1,0:T(8,128)(2,1)S(1)}, bf16[784,128]{1,0:T(8,128)(2,1)S(1)}, u32[]{:S(2)}, u32[]{:S(2)}) %collective-permute-start) | collective-permute-done | bytes 200736 | tf_op jit(solution)/shard_map/ppermute | solution.py:287
  32.1 4.3 %collective-permute-done.1.refs_2_ = bf16[784,128]{1,0:T(8,128)(2,1)S(1)} collective-permute-done((bf16[784,128]{1,0:T(8,128)(2,1)S(1)}, bf16[784,128]{1,0:T(8,128)(2,1)S(1)}, u32[]{:S(2)}, u32[]{:S(2)}) %collective-permute-start.1) | collective-permute-done | bytes 200736 | tf_op jit(solution)/shard_map/ppermute | solution.py:287
  36.4 1.0 %all-to-all-done.refs_0_ = bf16[4,1552,128]{2,1,0:T(8,128)(2,1)S(1)} async-done(((bf16[4,1552,128]{2,1,0:T(8,128)(2,1)}), bf16[4,1552,128]{2,1,0:T(8,128)(2,1)S(1)}, u32[]{:S(2)}, u32[]{:S(2)}) %all-to-all-start) | async-done | bytes 1589280 | tf_op jit(solution)/shard_map/all_to_all | solution.py:284
  37.5 0.7 copy-done
  38.1 4.2 %shard_map.122 = (bf16[400,128]{1,0:T(8,128)(2,1)S(1)}, bf16[400,128]{1,0:T(8,128)(2,1)S(1)}, bf16[400,128]{1,0:T(8,128)(2,1)S(1)}, bf16[400,128]{1,0:T(8,128)(2...) custom-call(f32[96]{0:T(128)S(1)} %copy-done, ...), custom_call_target="tpu_custom_call" | custom-call | tf_op jit(solution)/shard_map/pallas_call | solution.py:305
  42.3 1.5 %collective-permute-start.2 = (bf16[400,128]{1,0:T(8,128)(2,1)S(1)}, bf16[400,128]{1,0:T(8,128)(2,1)S(1)}, u32[]{:S(2)}, u32[]{:S(2)}) collective-permute-start(bf16[400,128]{1,0:T(8,128)(2,1)S(1)} %get-tuple-element.35), channel_id=1, source_target_pairs={{0,1},{1,0},{2,3},{3,2},{4,5},{5,4},{6,7},{7,6},{8,9},{9,8},{10,11... | collective-permute-start | bytes 307208 | tf_op jit(solution)/shard_map/ppermute | solution.py:287
  43.8 4.0 %collective-permute-start.3 = (bf16[400,128]{1,0:T(8,128)(2,1)S(1)}, bf16[400,128]{1,0:T(8,128)(2,1)S(1)}, u32[]{:S(2)}, u32[]{:S(2)}) collective-permute-start(bf16[400,128]{1,0:T(8,128)(2,1)S(1)} %get-tuple-element.36), channel_id=1, source_target_pairs={{0,2},{1,3},{2,0},{3,1},{4,6},{5,7},{6,4},{7,5},{8,10},{9,11},{10,... | collective-permute-start | bytes 307208 | tf_op jit(solution)/shard_map/ppermute | solution.py:287
  47.8 0.9 %collective-permute-start.4 = (bf16[400,128]{1,0:T(8,128)(2,1)S(1)}, bf16[400,128]{1,0:T(8,128)(2,1)S(1)}, u32[]{:S(2)}, u32[]{:S(2)}) collective-permute-start(bf16[400,128]{1,0:T(8,128)(2,1)S(1)} %get-tuple-element.37), channel_id=1, source_target_pairs={{0,3},{1,2},{2,1},{3,0},{4,7},{5,6},{6,5},{7,4},{8,11},{9,10},{10,... | collective-permute-start | bytes 307208 | tf_op jit(solution)/shard_map/ppermute | solution.py:287
  48.7 0.0 collective-permute-done.7.refs_1_
  48.7 6.9 %collective-permute-start.5 = (bf16[400,128]{1,0:T(8,128)(2,1)S(1)}, bf16[400,128]{1,0:T(8,128)(2,1)S(1)}, u32[]{:S(2)}, u32[]{:S(2)}) collective-permute-start(bf16[400,128]{1,0:T(8,128)(2,1)S(1)} %get-tuple-element.38), channel_id=1, source_target_pairs={{0,4},{1,5},{2,6},{3,7},{4,0},{5,1},{6,2},{7,3},{8,12},{9,13},{10,... | collective-permute-start | bytes 307208 | tf_op jit(solution)/shard_map/ppermute | solution.py:287
  55.6 0.0 collective-permute-done.8.refs_2_
  55.6 1.0 %collective-permute-start.6 = (bf16[400,128]{1,0:T(8,128)(2,1)S(1)}, bf16[400,128]{1,0:T(8,128)(2,1)S(1)}, u32[]{:S(2)}, u32[]{:S(2)}) collective-permute-start(bf16[400,128]{1,0:T(8,128)(2,1)S(1)} %get-tuple-element.39), channel_id=1, source_target_pairs={{0,5},{1,4},{2,7},{3,6},{4,1},{5,0},{6,3},{7,2},{8,13},{9,12},{10,... | collective-permute-start | bytes 307208 | tf_op jit(solution)/shard_map/ppermute | solution.py:287
  56.6 2.3 %shard_map.123 = (bf16[400,128]{1,0:T(8,128)(2,1)S(1)}, bf16[400,128]{1,0:T(8,128)(2,1)S(1)}, bf16[768,128]{1,0:T(8,128)(2,1)S(1)}, bf16[768,128]{1,0:T(8,128)(2...) custom-call(f32[96]{0:T(128)S(1)} %copy-done, bf16[4,1552,128]{2,1,0:T(8,128)(2,1)S(1)} %all-to-all-done.refs_0_, ...), custom_call_target="tpu_custom_call" | custom-call | tf_op jit(solution)/shard_map/pallas_call | solution.py:305
  58.9 0.0 collective-permute-done.2.refs_1_
  58.9 4.4 %collective-permute-start.9 = (bf16[400,128]{1,0:T(8,128)(2,1)S(1)}, bf16[400,128]{1,0:T(8,128)(2,1)S(1)}, u32[]{:S(2)}, u32[]{:S(2)}) collective-permute-start(bf16[400,128]{1,0:T(8,128)(2,1)S(1)} %get-tuple-element.44), channel_id=1, source_target_pairs={{0,6},{1,7},{2,4},{3,5},{4,2},{5,3},{6,0},{7,1},{8,14},{9,15},{10,... | collective-permute-start | bytes 307208 | tf_op jit(solution)/shard_map/ppermute | solution.py:287
  63.2 0.0 collective-permute-done.3.refs_2_
  63.2 0.0 collective-permute-start.10
  63.3 1.5 %collective-permute-start.11 = (bf16[768,128]{1,0:T(8,128)(2,1)S(1)}, bf16[768,128]{1,0:T(8,128)(2,1)S(1)}, u32[]{:S(2)}, u32[]{:S(2)}) collective-permute-start(bf16[768,128]{1,0:T(8,128)(2,1)S(1)} %get-tuple-element.47), channel_id=1, source_target_pairs={{0,1},{1,0},{2,3},{3,2},{4,5},{5,4},{6,7},{7,6},{8,9},{9,8},{10,11... | collective-permute-start | bytes 589832 | tf_op jit(solution)/shard_map/ppermute | solution.py:287
  64.8 0.0 collective-permute-done.5.refs_4_
  64.8 0.0 collective-permute-start.12
  64.8 0.0 collective-permute-done.6.refs_5_
  64.8 2.7 %collective-permute-start.13 = (bf16[768,128]{1,0:T(8,128)(2,1)S(1)}, bf16[768,128]{1,0:T(8,128)(2,1)S(1)}, u32[]{:S(2)}, u32[]{:S(2)}) collective-permute-start(bf16[768,128]{1,0:T(8,128)(2,1)S(1)} %get-tuple-element.49), channel_id=1, source_target_pairs={{0,3},{1,2},{2,1},{3,0},{4,7},{5,6},{6,5},{7,4},{8,11},{9,10},{10,... | collective-permute-start | bytes 589832 | tf_op jit(solution)/shard_map/ppermute | solution.py:287
  67.5 0.0 collective-permute-done.9.refs_6_
  67.6 3.1 %collective-permute-done.10.refs_7_ = bf16[400,128]{1,0:T(8,128)(2,1)S(1)} collective-permute-done((bf16[400,128]{1,0:T(8,128)(2,1)S(1)}, bf16[400,128]{1,0:T(8,128)(2,1)S(1)}, u32[]{:S(2)}, u32[]{:S(2)}) %collective-permute-start.10) | collective-permute-done | bytes 102432 | tf_op jit(solution)/shard_map/ppermute | solution.py:287
  70.7 0.8 %shard_map.124 = (f32[2,12]{1,0:T(2,128)S(1)}, f32[2,12]{1,0:T(2,128)S(1)}, f32[2,12]{1,0:T(2,128)S(1)}, f32[2,12]{1,0:T(2,128)S(1)}) custom-call(s32[64]{0:T(128)S(1)} %copy-done.1, bf16[400,128]{1,0:T(8,128)(2,1)S(1)} %get-tuple-element.34.refs_0_, bf16[400,128]{1,0:T(8,128)(2,1)S(1)} %collective-permute-done.2.refs_1_, ...), custom_call_target="tpu_custom_call" | custom-call | flops 40000000000 | tf_op jit(solution)/shard_map/pallas_call | solution.py:324
  71.5 0.1 collective-permute-start.16
  71.6 1.6 %collective-permute-start.15 = (f32[2,12]{1,0:T(2,128)S(1)}, f32[2,12]{1,0:T(2,128)S(1)}, u32[]{:S(2)}, u32[]{:S(2)}) collective-permute-start(f32[2,12]{1,0:T(2,128)S(1)} %get-tuple-element.56), channel_id=1, source_target_pairs={{0,16},{8,24},{16,0},{24,8},{1,17},{9,25},{17,1},{25,9},{2,18},{10... | collective-permute-start | bytes 296 | tf_op jit(solution)/shard_map/ppermute | solution.py:287
  73.1 0.0 collective-permute-done.11.refs_9_
  73.1 0.3 collective-permute-start.14
  73.4 0.0 collective-permute-done.12.refs_10_
  73.4 0.3 collective-permute-done.13.refs_11_
  73.7 1.2 %shard_map.125 = (bf16[1,128,1536]{2,1,0:T(8,128)(2,1)}, bf16[1,128,1536]{2,1,0:T(8,128)(2,1)}, bf16[1,128,1536]{2,1,0:T(8,128)(2,1)}, f32[2,12]{1,0:T(2,128)S(1)}) custom-call(bf16[400,128]{1,0:T(8,128)(2,1)S(1)} %get-tuple-element.34.refs_0_, bf16[400,128]{1,0:T(8,128)(2,1)S(1)} %collective-permute-done.2.refs_1_, ...), custom_call_target="tpu_custom_call" | custom-call | tf_op jit(solution)/shard_map/pallas_call | solution.py:337
  74.9 0.0 collective-permute-done.16
  74.9 0.3 collective-permute-done.15
  75.2 0.0 collective-permute-done.14
  75.2 0.6 add_bitcast_fusion
  (14 shorter events, 0.0 us)
Async XLA Ops:
  4.0 5.4 %copy-start.7 = (bf16[784,128]{1,0:T(8,128)(2,1)S(1)}, bf16[784,128]{1,0:T(8,128)(2,1)}, u32[]{:S(2)}) copy-start(bf16[784,128]{1,0:T(8,128)(2,1)} %get-tuple-element.32) | copy-start | bytes 602116
  4.0 8.0 %copy-start.6 = (bf16[784,128]{1,0:T(8,128)(2,1)S(1)}, bf16[784,128]{1,0:T(8,128)(2,1)}, u32[]{:S(2)}) copy-start(bf16[784,128]{1,0:T(8,128)(2,1)} %get-tuple-element.33) | copy-start | bytes 602116
  4.0 9.8 %copy-start.5 = (bf16[784,128]{1,0:T(8,128)(2,1)S(1)}, bf16[784,128]{1,0:T(8,128)(2,1)}, u32[]{:S(2)}) copy-start(bf16[784,128]{1,0:T(8,128)(2,1)} %get-tuple-element.40) | copy-start | bytes 602116
  4.0 13.3 %copy-start.4 = (bf16[784,128]{1,0:T(8,128)(2,1)S(1)}, bf16[784,128]{1,0:T(8,128)(2,1)}, u32[]{:S(2)}) copy-start(bf16[784,128]{1,0:T(8,128)(2,1)} %get-tuple-element.41) | copy-start | bytes 602116
  4.0 13.4 %copy-start.2 = (f32[8,12,8]{1,2,0:T(8,128)S(1)}, f32[8,12,8]{1,2,0:T(8,128)}, u32[]{:S(2)}) copy-start(f32[8,12,8]{1,2,0:T(8,128)} %param.15) | copy-start | bytes 9220
  4.0 14.2 %copy-start.3 = (s32[8,8]{1,0:T(8,128)S(1)}, s32[8,8]{1,0:T(8,128)}, u32[]{:S(2)}) copy-start(s32[8,8]{1,0:T(8,128)} %param.16) | copy-start | bytes 772
  4.0 33.4 %all-to-all-start = ((bf16[4,1552,128]{2,1,0:T(8,128)(2,1)}), bf16[4,1552,128]{2,1,0:T(8,128)(2,1)S(1)}, u32[]{:S(2)}, u32[]{:S(2)}) async-start(bf16[4,1552,128]{2,1,0:T(8,128)(2,1)} %get-tuple-element.31), calls=%async_computation | async-start | bytes 3178496 | tf_op jit(solution)/shard_map/all_to_all | solution.py:284
  9.4 22.7 %collective-permute-start = (bf16[784,128]{1,0:T(8,128)(2,1)S(1)}, bf16[784,128]{1,0:T(8,128)(2,1)S(1)}, u32[]{:S(2)}, u32[]{:S(2)}) collective-permute-start(bf16[784,128]{1,0:T(8,128)(2,1)S(1)} %copy-done.7), channel_id=1, source_target_pairs={{0,4},{1,5},{2,6},{3,7},{4,0},{5,1},{6,2},{7,3},{8,12},{9,13},{10,... | collective-permute-start | bytes 602120 | tf_op jit(solution)/shard_map/ppermute | solution.py:287
  12.0 24.4 %collective-permute-start.1 = (bf16[784,128]{1,0:T(8,128)(2,1)S(1)}, bf16[784,128]{1,0:T(8,128)(2,1)S(1)}, u32[]{:S(2)}, u32[]{:S(2)}) collective-permute-start(bf16[784,128]{1,0:T(8,128)(2,1)S(1)} %copy-done.6), channel_id=1, source_target_pairs={{0,5},{1,4},{2,7},{3,6},{4,1},{5,0},{6,3},{7,2},{8,13},{9,12},{10,... | collective-permute-start | bytes 602120 | tf_op jit(solution)/shard_map/ppermute | solution.py:287
  13.8 34.9 %collective-permute-start.7 = (bf16[784,128]{1,0:T(8,128)(2,1)S(1)}, bf16[784,128]{1,0:T(8,128)(2,1)S(1)}, u32[]{:S(2)}, u32[]{:S(2)}) collective-permute-start(bf16[784,128]{1,0:T(8,128)(2,1)S(1)} %copy-done.5), channel_id=1, source_target_pairs={{0,6},{1,7},{2,4},{3,5},{4,2},{5,3},{6,0},{7,1},{8,14},{9,15},{10,... | collective-permute-start | bytes 602120 | tf_op jit(solution)/shard_map/ppermute | solution.py:287
  17.3 38.3 %collective-permute-start.8 = (bf16[784,128]{1,0:T(8,128)(2,1)S(1)}, bf16[784,128]{1,0:T(8,128)(2,1)S(1)}, u32[]{:S(2)}, u32[]{:S(2)}) collective-permute-start(bf16[784,128]{1,0:T(8,128)(2,1)S(1)} %copy-done.4), channel_id=1, source_target_pairs={{0,7},{1,6},{2,5},{3,4},{4,3},{5,2},{6,1},{7,0},{8,15},{9,14},{10,... | collective-permute-start | bytes 602120 | tf_op jit(solution)/shard_map/ppermute | solution.py:287
  37.5 0.7 copy-start
  42.3 16.6 %collective-permute-start.2 = (bf16[400,128]{1,0:T(8,128)(2,1)S(1)}, bf16[400,128]{1,0:T(8,128)(2,1)S(1)}, u32[]{:S(2)}, u32[]{:S(2)}) collective-permute-start(bf16[400,128]{1,0:T(8,128)(2,1)S(1)} %get-tuple-element.35), channel_id=1, source_target_pairs={{0,1},{1,0},{2,3},{3,2},{4,5},{5,4},{6,7},{7,6},{8,9},{9,8},{10,11... | collective-permute-start | bytes 307208 | tf_op jit(solution)/shard_map/ppermute | solution.py:287
  43.8 19.4 %collective-permute-start.3 = (bf16[400,128]{1,0:T(8,128)(2,1)S(1)}, bf16[400,128]{1,0:T(8,128)(2,1)S(1)}, u32[]{:S(2)}, u32[]{:S(2)}) collective-permute-start(bf16[400,128]{1,0:T(8,128)(2,1)S(1)} %get-tuple-element.36), channel_id=1, source_target_pairs={{0,2},{1,3},{2,0},{3,1},{4,6},{5,7},{6,4},{7,5},{8,10},{9,11},{10,... | collective-permute-start | bytes 307208 | tf_op jit(solution)/shard_map/ppermute | solution.py:287
  47.8 15.4 %collective-permute-start.4 = (bf16[400,128]{1,0:T(8,128)(2,1)S(1)}, bf16[400,128]{1,0:T(8,128)(2,1)S(1)}, u32[]{:S(2)}, u32[]{:S(2)}) collective-permute-start(bf16[400,128]{1,0:T(8,128)(2,1)S(1)} %get-tuple-element.37), channel_id=1, source_target_pairs={{0,3},{1,2},{2,1},{3,0},{4,7},{5,6},{6,5},{7,4},{8,11},{9,10},{10,... | collective-permute-start | bytes 307208 | tf_op jit(solution)/shard_map/ppermute | solution.py:287
  48.7 16.1 %collective-permute-start.5 = (bf16[400,128]{1,0:T(8,128)(2,1)S(1)}, bf16[400,128]{1,0:T(8,128)(2,1)S(1)}, u32[]{:S(2)}, u32[]{:S(2)}) collective-permute-start(bf16[400,128]{1,0:T(8,128)(2,1)S(1)} %get-tuple-element.38), channel_id=1, source_target_pairs={{0,4},{1,5},{2,6},{3,7},{4,0},{5,1},{6,2},{7,3},{8,12},{9,13},{10,... | collective-permute-start | bytes 307208 | tf_op jit(solution)/shard_map/ppermute | solution.py:287
  55.6 9.2 %collective-permute-start.6 = (bf16[400,128]{1,0:T(8,128)(2,1)S(1)}, bf16[400,128]{1,0:T(8,128)(2,1)S(1)}, u32[]{:S(2)}, u32[]{:S(2)}) collective-permute-start(bf16[400,128]{1,0:T(8,128)(2,1)S(1)} %get-tuple-element.39), channel_id=1, source_target_pairs={{0,5},{1,4},{2,7},{3,6},{4,1},{5,0},{6,3},{7,2},{8,13},{9,12},{10,... | collective-permute-start | bytes 307208 | tf_op jit(solution)/shard_map/ppermute | solution.py:287
  56.6 14.1 %copy-start.1 = (s32[64]{0:T(128)S(1)}, s32[64]{0:T(128)}, u32[]{:S(2)}) copy-start(s32[64]{0:T(128)} %reshape.16.index) | copy-start | bytes 772
  58.9 8.7 %collective-permute-start.9 = (bf16[400,128]{1,0:T(8,128)(2,1)S(1)}, bf16[400,128]{1,0:T(8,128)(2,1)S(1)}, u32[]{:S(2)}, u32[]{:S(2)}) collective-permute-start(bf16[400,128]{1,0:T(8,128)(2,1)S(1)} %get-tuple-element.44), channel_id=1, source_target_pairs={{0,6},{1,7},{2,4},{3,5},{4,2},{5,3},{6,0},{7,1},{8,14},{9,15},{10,... | collective-permute-start | bytes 307208 | tf_op jit(solution)/shard_map/ppermute | solution.py:287
  63.2 7.5 %collective-permute-start.10 = (bf16[400,128]{1,0:T(8,128)(2,1)S(1)}, bf16[400,128]{1,0:T(8,128)(2,1)S(1)}, u32[]{:S(2)}, u32[]{:S(2)}) collective-permute-start(bf16[400,128]{1,0:T(8,128)(2,1)S(1)} %get-tuple-element.45), channel_id=1, source_target_pairs={{0,7},{1,6},{2,5},{3,4},{4,3},{5,2},{6,1},{7,0},{8,15},{9,14},{10,... | collective-permute-start | bytes 307208 | tf_op jit(solution)/shard_map/ppermute | solution.py:287
  63.3 9.9 %collective-permute-start.11 = (bf16[768,128]{1,0:T(8,128)(2,1)S(1)}, bf16[768,128]{1,0:T(8,128)(2,1)S(1)}, u32[]{:S(2)}, u32[]{:S(2)}) collective-permute-start(bf16[768,128]{1,0:T(8,128)(2,1)S(1)} %get-tuple-element.47), channel_id=1, source_target_pairs={{0,1},{1,0},{2,3},{3,2},{4,5},{5,4},{6,7},{7,6},{8,9},{9,8},{10,11... | collective-permute-start | bytes 589832 | tf_op jit(solution)/shard_map/ppermute | solution.py:287
  64.8 8.6 %collective-permute-start.12 = (bf16[768,128]{1,0:T(8,128)(2,1)S(1)}, bf16[768,128]{1,0:T(8,128)(2,1)S(1)}, u32[]{:S(2)}, u32[]{:S(2)}) collective-permute-start(bf16[768,128]{1,0:T(8,128)(2,1)S(1)} %get-tuple-element.48), channel_id=1, source_target_pairs={{0,2},{1,3},{2,0},{3,1},{4,6},{5,7},{6,4},{7,5},{8,10},{9,11},{10,... | collective-permute-start | bytes 589832 | tf_op jit(solution)/shard_map/ppermute | solution.py:287
  64.8 8.9 %collective-permute-start.13 = (bf16[768,128]{1,0:T(8,128)(2,1)S(1)}, bf16[768,128]{1,0:T(8,128)(2,1)S(1)}, u32[]{:S(2)}, u32[]{:S(2)}) collective-permute-start(bf16[768,128]{1,0:T(8,128)(2,1)S(1)} %get-tuple-element.49), channel_id=1, source_target_pairs={{0,3},{1,2},{2,1},{3,0},{4,7},{5,6},{6,5},{7,4},{8,11},{9,10},{10,... | collective-permute-start | bytes 589832 | tf_op jit(solution)/shard_map/ppermute | solution.py:287
  71.5 3.4 %collective-permute-start.16 = (f32[2,12]{1,0:T(2,128)S(1)}, f32[2,12]{1,0:T(2,128)S(1)}, u32[]{:S(2)}, u32[]{:S(2)}) collective-permute-start(f32[2,12]{1,0:T(2,128)S(1)} %get-tuple-element.57), channel_id=1, source_target_pairs={{0,24},{8,16},{16,8},{24,0},{1,25},{9,17},{17,9},{25,1},{2,26},{10... | collective-permute-start | bytes 296 | tf_op jit(solution)/shard_map/ppermute | solution.py:287
  71.6 3.6 %collective-permute-start.15 = (f32[2,12]{1,0:T(2,128)S(1)}, f32[2,12]{1,0:T(2,128)S(1)}, u32[]{:S(2)}, u32[]{:S(2)}) collective-permute-start(f32[2,12]{1,0:T(2,128)S(1)} %get-tuple-element.56), channel_id=1, source_target_pairs={{0,16},{8,24},{16,0},{24,8},{1,17},{9,25},{17,1},{25,9},{2,18},{10... | collective-permute-start | bytes 296 | tf_op jit(solution)/shard_map/ppermute | solution.py:287
  73.1 2.1 %collective-permute-start.14 = (f32[2,12]{1,0:T(2,128)S(1)}, f32[2,12]{1,0:T(2,128)S(1)}, u32[]{:S(2)}, u32[]{:S(2)}) collective-permute-start(f32[2,12]{1,0:T(2,128)S(1)} %get-tuple-element.55), channel_id=1, source_target_pairs={{0,8},{8,0},{16,24},{24,16},{1,9},{9,1},{17,25},{25,17},{2,10},{10... | collective-permute-start | bytes 296 | tf_op jit(solution)/shard_map/ppermute | solution.py:287

commit v4 on v3

--- a/solution.py
+++ b/solution.py
@@ -313,7 +313,7 @@
         return made[:count], made[count:]
 
     queries, partials, begin = [], [], 0
-    for end in (members + (blocks - members) // 2, blocks):
+    for end in (members, blocks):
         places = tuple(range(begin, end))
         made, partials = stage(places, begin == 0, end == blocks, partials)
         queries += [move(piece, place) if place else piece for piece, place in zip(made, places)]

time: 76.1 us -> 76.1 us (level)
  waiting for transfers between devices: 20.6 us -> 29.7 us
  starting transfers between devices: 38.2 us -> 29.3 us
    all_to_all x1, waiting for transfers between devices: 1.01 us -> 16.9 us  [exchange(): return lax.all_to_all(array, 'gene', 0, 0, axis_index_groups=groups)]
    ppermute x17, starting transfers between devices: 32.8 us -> 24 us  [move(): return lax.ppermute(array, axis, [(i, i ^ hop) for i in range(size)])]
    ppermute x17, waiting for transfers between devices: 19.6 us -> 12.8 us  [move(): return lax.ppermute(array, axis, [(i, i ^ hop) for i in range(size)])]
  transfers between devices with their start and end apart: 18 -> 18, of which waited for: 6 -> 7; matrix products, arithmetic and copies ran while one was open for 2% -> 2% of each run, Pallas kernels for 13% -> 13%
where the time goes in v4:
time: 76.1 us; the launch traced here: 75.8 us
  waiting for transfers between devices  29.7 us (39%)
  starting transfers between devices  29.3 us (39%)
  Pallas kernels  13.4 us (18%)
  local copies, waits for them, and re-layouts  2.08 us (3%)
    ppermute x17, starting transfers between devices, move(): return lax.ppermute(array, axis, [(i, i ^ hop) for i in range(size)])  24 us
    all_to_all x1, waiting for transfers between devices, exchange(): return lax.all_to_all(array, 'gene', 0, 0, axis_index_groups=groups)  16.9 us
    ppermute x17, waiting for transfers between devices, move(): return lax.ppermute(array, axis, [(i, i ^ hop) for i in range(size)])  12.8 us
    pallas_call x2, Pallas kernels, stage(): call(functools.partial(stage_kernel, plan, places, first, last), [query_o...  6.28 us
    all_to_all x1, starting transfers between devices, exchange(): return lax.all_to_all(array, 'gene', 0, 0, axis_index_groups=groups)  5.39 us
    pallas_call x1, Pallas kernels, shards(): call(functools.partial(pack_kernel, plan), [far_in] * members + [near_in]...  3.35 us
    pallas_call x1, Pallas kernels, shards(): call(functools.partial(table_kernel, plan), [jax.ShapeDtypeStruct((blocks...  1.78 us
  transfers between devices with their start and end apart: 18, of which 7 were waited for; matrix products, arithmetic and copies ran while one was open for 2% of the time, Pallas kernels for 13%

profile of v4, /device:TPU:0, one launch (start us, length us, event | category | flops | bytes accessed | tf_op | source)
XLA Modules:
  0.0 75.8 jit_solution(2625768960955961564)
XLA Ops:
  0.6 3.3 %shard_map.121 = (bf16[784,128]{1,0:T(8,128)(2,1)}, bf16[784,128]{1,0:T(8,128)(2,1)}, bf16[784,128]{1,0:T(8,128)(2,1)}, bf16[784,128]{1,0:T(8,128)(2,1)}, bf16[4,1552,128]{2,1,0:T(8,128)(2,1)}) custom-call(bf16[1,128,1536]{2,1,0:T(8,128)(2,1)} %query.1, bf16[1,128,1536]{2,1,0:T(8,128)(2,1)} %key.1, bf16[1,128,1536]{2,1,0:T(8,128)(2,1)} %value.1, ...), custom_call_target="tpu_custom_call" | custom-call | tf_op jit(solution)/shard_map/pallas_call | solution.py:278
  4.0 0.0 copy-start.2
  4.0 0.0 copy-start.3
  4.0 5.4 %all-to-all-start = ((bf16[4,1552,128]{2,1,0:T(8,128)(2,1)}), bf16[4,1552,128]{2,1,0:T(8,128)(2,1)S(1)}, u32[]{:S(2)}, u32[]{:S(2)}) async-start(bf16[4,1552,128]{2,1,0:T(8,128)(2,1)} %get-tuple-element.31), calls=%async_computation | async-start | bytes 3178496 | tf_op jit(solution)/shard_map/all_to_all | solution.py:284
  9.4 2.6 %collective-permute-start.3 = (bf16[784,128]{1,0:T(8,128)(2,1)S(1)}, bf16[784,128]{1,0:T(8,128)(2,1)S(1)}, u32[]{:S(2)}, u32[]{:S(2)}) collective-permute-start(bf16[784,128]{1,0:T(8,128)(2,1)S(1)} %copy-done.7), channel_id=1, source_target_pairs={{0,4},{1,5},{2,6},{3,7},{4,0},{5,1},{6,2},{7,3},{8,12},{9,13},{10,... | collective-permute-start | bytes 602120 | tf_op jit(solution)/shard_map/ppermute | solution.py:287
  12.0 1.8 %collective-permute-start.4 = (bf16[784,128]{1,0:T(8,128)(2,1)S(1)}, bf16[784,128]{1,0:T(8,128)(2,1)S(1)}, u32[]{:S(2)}, u32[]{:S(2)}) collective-permute-start(bf16[784,128]{1,0:T(8,128)(2,1)S(1)} %copy-done.6), channel_id=1, source_target_pairs={{0,5},{1,4},{2,7},{3,6},{4,1},{5,0},{6,3},{7,2},{8,13},{9,12},{10,... | collective-permute-start | bytes 602120 | tf_op jit(solution)/shard_map/ppermute | solution.py:287
  13.8 3.5 %collective-permute-start.5 = (bf16[784,128]{1,0:T(8,128)(2,1)S(1)}, bf16[784,128]{1,0:T(8,128)(2,1)S(1)}, u32[]{:S(2)}, u32[]{:S(2)}) collective-permute-start(bf16[784,128]{1,0:T(8,128)(2,1)S(1)} %copy-done.5), channel_id=1, source_target_pairs={{0,6},{1,7},{2,4},{3,5},{4,2},{5,3},{6,0},{7,1},{8,14},{9,15},{10,... | collective-permute-start | bytes 602120 | tf_op jit(solution)/shard_map/ppermute | solution.py:287
  17.3 0.1 collective-permute-start.6
  17.4 0.1 copy.13
  17.5 0.7 reshape.15.bias
  18.2 0.6 reshape.16.index
  18.8 1.8 %shard_map.120.shift = f32[96]{0:T(128)} custom-call(f32[768]{0:T(1024)} %reshape.15.bias, s32[64]{0:T(128)} %reshape.16.index, s32[8]{0:T(128)} %count.1), custom_call_target="tpu_custom_call" | custom-call | tf_op jit(solution)/shard_map/pallas_call | solution.py:291
  20.6 16.9 %all-to-all-done.refs_0_ = bf16[4,1552,128]{2,1,0:T(8,128)(2,1)S(1)} async-done(((bf16[4,1552,128]{2,1,0:T(8,128)(2,1)}), bf16[4,1552,128]{2,1,0:T(8,128)(2,1)S(1)}, u32[]{:S(2)}, u32[]{:S(2)}) %all-to-all-start) | async-done | bytes 1589280 | tf_op jit(solution)/shard_map/all_to_all | solution.py:284
  37.5 0.7 copy-done
  38.1 3.1 %shard_map.122 = (bf16[400,128]{1,0:T(8,128)(2,1)S(1)}, bf16[400,128]{1,0:T(8,128)(2,1)S(1)}, bf16[400,128]{1,0:T(8,128)(2,1)S(1)}, bf16[400,128]{1,0:T(8,128)(2...) custom-call(f32[96]{0:T(128)S(1)} %copy-done, bf16[4,1552,128]{2,1,0:T(8,128)(2,1)S(1)} %all-to-all-done.refs_0_), custom_call_target="tpu_custom_call" | custom-call | tf_op jit(solution)/shard_map/pallas_call | solution.py:305
  41.3 1.5 %collective-permute-start = (bf16[400,128]{1,0:T(8,128)(2,1)S(1)}, bf16[400,128]{1,0:T(8,128)(2,1)S(1)}, u32[]{:S(2)}, u32[]{:S(2)}) collective-permute-start(bf16[400,128]{1,0:T(8,128)(2,1)S(1)} %get-tuple-element.33), channel_id=1, source_target_pairs={{0,1},{1,0},{2,3},{3,2},{4,5},{5,4},{6,7},{7,6},{8,9},{9,8},{10,11... | collective-permute-start | bytes 307208 | tf_op jit(solution)/shard_map/ppermute | solution.py:287
  42.8 0.0 collective-permute-done.3.refs_1_
  42.8 0.0 collective-permute-start.1
  42.8 0.0 collective-permute-done.4.refs_2_
  42.8 2.0 %collective-permute-start.2 = (bf16[400,128]{1,0:T(8,128)(2,1)S(1)}, bf16[400,128]{1,0:T(8,128)(2,1)S(1)}, u32[]{:S(2)}, u32[]{:S(2)}) collective-permute-start(bf16[400,128]{1,0:T(8,128)(2,1)S(1)} %get-tuple-element.35), channel_id=1, source_target_pairs={{0,3},{1,2},{2,1},{3,0},{4,7},{5,6},{6,5},{7,4},{8,11},{9,10},{10,... | collective-permute-start | bytes 307208 | tf_op jit(solution)/shard_map/ppermute | solution.py:287
  44.8 0.5 collective-permute-done.5.refs_3_
  45.3 5.1 %collective-permute-done.6.refs_4_ = bf16[784,128]{1,0:T(8,128)(2,1)S(1)} collective-permute-done((bf16[784,128]{1,0:T(8,128)(2,1)S(1)}, bf16[784,128]{1,0:T(8,128)(2,1)S(1)}, u32[]{:S(2)}, u32[]{:S(2)}) %collective-permute-start.6) | collective-permute-done | bytes 200736 | tf_op jit(solution)/shard_map/ppermute | solution.py:287
  50.4 3.1 %shard_map.123 = (bf16[400,128]{1,0:T(8,128)(2,1)S(1)}, bf16[400,128]{1,0:T(8,128)(2,1)S(1)}, bf16[400,128]{1,0:T(8,128)(2,1)S(1)}, bf16[400,128]{1,0:T(8,128)(2...) custom-call(f32[96]{0:T(128)S(1)} %copy-done, ...), custom_call_target="tpu_custom_call" | custom-call | tf_op jit(solution)/shard_map/pallas_call | solution.py:305
  53.6 3.2 %collective-permute-start.7 = (bf16[400,128]{1,0:T(8,128)(2,1)S(1)}, bf16[400,128]{1,0:T(8,128)(2,1)S(1)}, u32[]{:S(2)}, u32[]{:S(2)}) collective-permute-start(bf16[400,128]{1,0:T(8,128)(2,1)S(1)} %get-tuple-element.42), channel_id=1, source_target_pairs={{0,4},{1,5},{2,6},{3,7},{4,0},{5,1},{6,2},{7,3},{8,12},{9,13},{10,... | collective-permute-start | bytes 307208 | tf_op jit(solution)/shard_map/ppermute | solution.py:287
  56.8 0.9 %collective-permute-start.8 = (bf16[400,128]{1,0:T(8,128)(2,1)S(1)}, bf16[400,128]{1,0:T(8,128)(2,1)S(1)}, u32[]{:S(2)}, u32[]{:S(2)}) collective-permute-start(bf16[400,128]{1,0:T(8,128)(2,1)S(1)} %get-tuple-element.43), channel_id=1, source_target_pairs={{0,5},{1,4},{2,7},{3,6},{4,1},{5,0},{6,3},{7,2},{8,13},{9,12},{10,... | collective-permute-start | bytes 307208 | tf_op jit(solution)/shard_map/ppermute | solution.py:287
  57.6 0.0 collective-permute-done.refs_1_
  57.6 4.2 %collective-permute-start.9 = (bf16[400,128]{1,0:T(8,128)(2,1)S(1)}, bf16[400,128]{1,0:T(8,128)(2,1)S(1)}, u32[]{:S(2)}, u32[]{:S(2)}) collective-permute-start(bf16[400,128]{1,0:T(8,128)(2,1)S(1)} %get-tuple-element.44), channel_id=1, source_target_pairs={{0,6},{1,7},{2,4},{3,5},{4,2},{5,3},{6,0},{7,1},{8,14},{9,15},{10,... | collective-permute-start | bytes 307208 | tf_op jit(solution)/shard_map/ppermute | solution.py:287
  61.9 0.0 collective-permute-done.1.refs_2_
  61.9 0.2 collective-permute-start.10
  62.0 0.0 collective-permute-done.2.refs_3_
  62.0 1.3 %collective-permute-start.11 = (bf16[768,128]{1,0:T(8,128)(2,1)S(1)}, bf16[768,128]{1,0:T(8,128)(2,1)S(1)}, u32[]{:S(2)}, u32[]{:S(2)}) collective-permute-start(bf16[768,128]{1,0:T(8,128)(2,1)S(1)} %get-tuple-element.47), channel_id=1, source_target_pairs={{0,1},{1,0},{2,3},{3,2},{4,5},{5,4},{6,7},{7,6},{8,9},{9,8},{10,11... | collective-permute-start | bytes 589832 | tf_op jit(solution)/shard_map/ppermute | solution.py:287
  63.4 0.0 collective-permute-done.7.refs_4_
  63.4 0.7 collective-permute-start.12
  64.1 3.2 %collective-permute-done.8.refs_5_ = bf16[400,128]{1,0:T(8,128)(2,1)S(1)} collective-permute-done((bf16[400,128]{1,0:T(8,128)(2,1)S(1)}, bf16[400,128]{1,0:T(8,128)(2,1)S(1)}, u32[]{:S(2)}, u32[]{:S(2)}) %collective-permute-start.8) | collective-permute-done | bytes 102432 | tf_op jit(solution)/shard_map/ppermute | solution.py:287
  67.3 0.0 collective-permute-start.13
  67.3 0.2 collective-permute-done.9.refs_6_
  67.5 2.0 %collective-permute-done.10.refs_7_ = bf16[400,128]{1,0:T(8,128)(2,1)S(1)} collective-permute-done((bf16[400,128]{1,0:T(8,128)(2,1)S(1)}, bf16[400,128]{1,0:T(8,128)(2,1)S(1)}, u32[]{:S(2)}, u32[]{:S(2)}) %collective-permute-start.10) | collective-permute-done | bytes 102432 | tf_op jit(solution)/shard_map/ppermute | solution.py:287
  69.5 0.8 %shard_map.124 = (f32[2,12]{1,0:T(2,128)S(1)}, f32[2,12]{1,0:T(2,128)S(1)}, f32[2,12]{1,0:T(2,128)S(1)}, f32[2,12]{1,0:T(2,128)S(1)}) custom-call(s32[64]{0:T(128)S(1)} %copy-done.1, bf16[400,128]{1,0:T(8,128)(2,1)S(1)} %get-tuple-element.32.refs_0_, bf16[400,128]{1,0:T(8,128)(2,1)S(1)} %collective-permute-done.refs_1_, ...), custom_call_target="tpu_custom_call" | custom-call | flops 40000000000 | tf_op jit(solution)/shard_map/pallas_call | solution.py:324
  70.3 0.1 collective-permute-start.16
  70.4 1.6 %collective-permute-start.15 = (f32[2,12]{1,0:T(2,128)S(1)}, f32[2,12]{1,0:T(2,128)S(1)}, u32[]{:S(2)}, u32[]{:S(2)}) collective-permute-start(f32[2,12]{1,0:T(2,128)S(1)} %get-tuple-element.56), channel_id=1, source_target_pairs={{0,16},{8,24},{16,0},{24,8},{1,17},{9,25},{17,1},{25,9},{2,18},{10... | collective-permute-start | bytes 296 | tf_op jit(solution)/shard_map/ppermute | solution.py:287
  72.0 0.0 collective-permute-done.11.refs_9_
  72.0 0.3 collective-permute-start.14
  72.3 1.8 %collective-permute-done.13.refs_11_ = bf16[768,128]{1,0:T(8,128)(2,1)S(1)} collective-permute-done((bf16[768,128]{1,0:T(8,128)(2,1)S(1)}, bf16[768,128]{1,0:T(8,128)(2,1)S(1)}, u32[]{:S(2)}, u32[]{:S(2)}) %collective-permute-start.13) | collective-permute-done | bytes 196640 | tf_op jit(solution)/shard_map/ppermute | solution.py:287
  74.0 1.2 %shard_map.125 = (bf16[1,128,1536]{2,1,0:T(8,128)(2,1)}, bf16[1,128,1536]{2,1,0:T(8,128)(2,1)}, bf16[1,128,1536]{2,1,0:T(8,128)(2,1)}, f32[2,12]{1,0:T(2,128)S(1)}) custom-call(bf16[400,128]{1,0:T(8,128)(2,1)S(1)} %get-tuple-element.32.refs_0_, bf16[400,128]{1,0:T(8,128)(2,1)S(1)} %collective-permute-done.refs_1_, ...), custom_call_target="tpu_custom_call" | custom-call | tf_op jit(solution)/shard_map/pallas_call | solution.py:337
  75.2 0.0 collective-permute-done.16
  75.3 0.0 collective-permute-done.15
  75.3 0.0 collective-permute-done.14
  75.3 0.6 add_bitcast_fusion
  (14 shorter events, 0.0 us)
Async XLA Ops:
  4.0 5.4 %copy-start.7 = (bf16[784,128]{1,0:T(8,128)(2,1)S(1)}, bf16[784,128]{1,0:T(8,128)(2,1)}, u32[]{:S(2)}) copy-start(bf16[784,128]{1,0:T(8,128)(2,1)} %get-tuple-element.36) | copy-start | bytes 602116
  4.0 8.0 %copy-start.6 = (bf16[784,128]{1,0:T(8,128)(2,1)S(1)}, bf16[784,128]{1,0:T(8,128)(2,1)}, u32[]{:S(2)}) copy-start(bf16[784,128]{1,0:T(8,128)(2,1)} %get-tuple-element.37) | copy-start | bytes 602116
  4.0 9.8 %copy-start.5 = (bf16[784,128]{1,0:T(8,128)(2,1)S(1)}, bf16[784,128]{1,0:T(8,128)(2,1)}, u32[]{:S(2)}) copy-start(bf16[784,128]{1,0:T(8,128)(2,1)} %get-tuple-element.38) | copy-start | bytes 602116
  4.0 13.3 %copy-start.4 = (bf16[784,128]{1,0:T(8,128)(2,1)S(1)}, bf16[784,128]{1,0:T(8,128)(2,1)}, u32[]{:S(2)}) copy-start(bf16[784,128]{1,0:T(8,128)(2,1)} %get-tuple-element.39) | copy-start | bytes 602116
  4.0 13.4 %copy-start.2 = (f32[8,12,8]{1,2,0:T(8,128)S(1)}, f32[8,12,8]{1,2,0:T(8,128)}, u32[]{:S(2)}) copy-start(f32[8,12,8]{1,2,0:T(8,128)} %param.15) | copy-start | bytes 9220
  4.0 14.2 %copy-start.3 = (s32[8,8]{1,0:T(8,128)S(1)}, s32[8,8]{1,0:T(8,128)}, u32[]{:S(2)}) copy-start(s32[8,8]{1,0:T(8,128)} %param.16) | copy-start | bytes 772
  4.0 33.4 %all-to-all-start = ((bf16[4,1552,128]{2,1,0:T(8,128)(2,1)}), bf16[4,1552,128]{2,1,0:T(8,128)(2,1)S(1)}, u32[]{:S(2)}, u32[]{:S(2)}) async-start(bf16[4,1552,128]{2,1,0:T(8,128)(2,1)} %get-tuple-element.31), calls=%async_computation | async-start | bytes 3178496 | tf_op jit(solution)/shard_map/all_to_all | solution.py:284
  9.4 33.4 %collective-permute-start.3 = (bf16[784,128]{1,0:T(8,128)(2,1)S(1)}, bf16[784,128]{1,0:T(8,128)(2,1)S(1)}, u32[]{:S(2)}, u32[]{:S(2)}) collective-permute-start(bf16[784,128]{1,0:T(8,128)(2,1)S(1)} %copy-done.7), channel_id=1, source_target_pairs={{0,4},{1,5},{2,6},{3,7},{4,0},{5,1},{6,2},{7,3},{8,12},{9,13},{10,... | collective-permute-start | bytes 602120 | tf_op jit(solution)/shard_map/ppermute | solution.py:287
  12.0 30.8 %collective-permute-start.4 = (bf16[784,128]{1,0:T(8,128)(2,1)S(1)}, bf16[784,128]{1,0:T(8,128)(2,1)S(1)}, u32[]{:S(2)}, u32[]{:S(2)}) collective-permute-start(bf16[784,128]{1,0:T(8,128)(2,1)S(1)} %copy-done.6), channel_id=1, source_target_pairs={{0,5},{1,4},{2,7},{3,6},{4,1},{5,0},{6,3},{7,2},{8,13},{9,12},{10,... | collective-permute-start | bytes 602120 | tf_op jit(solution)/shard_map/ppermute | solution.py:287
  13.8 31.5 %collective-permute-start.5 = (bf16[784,128]{1,0:T(8,128)(2,1)S(1)}, bf16[784,128]{1,0:T(8,128)(2,1)S(1)}, u32[]{:S(2)}, u32[]{:S(2)}) collective-permute-start(bf16[784,128]{1,0:T(8,128)(2,1)S(1)} %copy-done.5), channel_id=1, source_target_pairs={{0,6},{1,7},{2,4},{3,5},{4,2},{5,3},{6,0},{7,1},{8,14},{9,15},{10,... | collective-permute-start | bytes 602120 | tf_op jit(solution)/shard_map/ppermute | solution.py:287
  17.3 33.1 %collective-permute-start.6 = (bf16[784,128]{1,0:T(8,128)(2,1)S(1)}, bf16[784,128]{1,0:T(8,128)(2,1)S(1)}, u32[]{:S(2)}, u32[]{:S(2)}) collective-permute-start(bf16[784,128]{1,0:T(8,128)(2,1)S(1)} %copy-done.4), channel_id=1, source_target_pairs={{0,7},{1,6},{2,5},{3,4},{4,3},{5,2},{6,1},{7,0},{8,15},{9,14},{10,... | collective-permute-start | bytes 602120 | tf_op jit(solution)/shard_map/ppermute | solution.py:287
  37.5 0.7 copy-start
  41.3 16.4 %collective-permute-start = (bf16[400,128]{1,0:T(8,128)(2,1)S(1)}, bf16[400,128]{1,0:T(8,128)(2,1)S(1)}, u32[]{:S(2)}, u32[]{:S(2)}) collective-permute-start(bf16[400,128]{1,0:T(8,128)(2,1)S(1)} %get-tuple-element.33), channel_id=1, source_target_pairs={{0,1},{1,0},{2,3},{3,2},{4,5},{5,4},{6,7},{7,6},{8,9},{9,8},{10,11... | collective-permute-start | bytes 307208 | tf_op jit(solution)/shard_map/ppermute | solution.py:287
  42.8 19.1 %collective-permute-start.1 = (bf16[400,128]{1,0:T(8,128)(2,1)S(1)}, bf16[400,128]{1,0:T(8,128)(2,1)S(1)}, u32[]{:S(2)}, u32[]{:S(2)}) collective-permute-start(bf16[400,128]{1,0:T(8,128)(2,1)S(1)} %get-tuple-element.34), channel_id=1, source_target_pairs={{0,2},{1,3},{2,0},{3,1},{4,6},{5,7},{6,4},{7,5},{8,10},{9,11},{10,... | collective-permute-start | bytes 307208 | tf_op jit(solution)/shard_map/ppermute | solution.py:287
  42.8 19.2 %collective-permute-start.2 = (bf16[400,128]{1,0:T(8,128)(2,1)S(1)}, bf16[400,128]{1,0:T(8,128)(2,1)S(1)}, u32[]{:S(2)}, u32[]{:S(2)}) collective-permute-start(bf16[400,128]{1,0:T(8,128)(2,1)S(1)} %get-tuple-element.35), channel_id=1, source_target_pairs={{0,3},{1,2},{2,1},{3,0},{4,7},{5,6},{6,5},{7,4},{8,11},{9,10},{10,... | collective-permute-start | bytes 307208 | tf_op jit(solution)/shard_map/ppermute | solution.py:287
  50.4 19.1 %copy-start.1 = (s32[64]{0:T(128)S(1)}, s32[64]{0:T(128)}, u32[]{:S(2)}) copy-start(s32[64]{0:T(128)} %reshape.16.index) | copy-start | bytes 772
  53.6 9.8 %collective-permute-start.7 = (bf16[400,128]{1,0:T(8,128)(2,1)S(1)}, bf16[400,128]{1,0:T(8,128)(2,1)S(1)}, u32[]{:S(2)}, u32[]{:S(2)}) collective-permute-start(bf16[400,128]{1,0:T(8,128)(2,1)S(1)} %get-tuple-element.42), channel_id=1, source_target_pairs={{0,4},{1,5},{2,6},{3,7},{4,0},{5,1},{6,2},{7,3},{8,12},{9,13},{10,... | collective-permute-start | bytes 307208 | tf_op jit(solution)/shard_map/ppermute | solution.py:287
  56.8 10.6 %collective-permute-start.8 = (bf16[400,128]{1,0:T(8,128)(2,1)S(1)}, bf16[400,128]{1,0:T(8,128)(2,1)S(1)}, u32[]{:S(2)}, u32[]{:S(2)}) collective-permute-start(bf16[400,128]{1,0:T(8,128)(2,1)S(1)} %get-tuple-element.43), channel_id=1, source_target_pairs={{0,5},{1,4},{2,7},{3,6},{4,1},{5,0},{6,3},{7,2},{8,13},{9,12},{10,... | collective-permute-start | bytes 307208 | tf_op jit(solution)/shard_map/ppermute | solution.py:287
  57.6 9.9 %collective-permute-start.9 = (bf16[400,128]{1,0:T(8,128)(2,1)S(1)}, bf16[400,128]{1,0:T(8,128)(2,1)S(1)}, u32[]{:S(2)}, u32[]{:S(2)}) collective-permute-start(bf16[400,128]{1,0:T(8,128)(2,1)S(1)} %get-tuple-element.44), channel_id=1, source_target_pairs={{0,6},{1,7},{2,4},{3,5},{4,2},{5,3},{6,0},{7,1},{8,14},{9,15},{10,... | collective-permute-start | bytes 307208 | tf_op jit(solution)/shard_map/ppermute | solution.py:287
  61.9 7.7 %collective-permute-start.10 = (bf16[400,128]{1,0:T(8,128)(2,1)S(1)}, bf16[400,128]{1,0:T(8,128)(2,1)S(1)}, u32[]{:S(2)}, u32[]{:S(2)}) collective-permute-start(bf16[400,128]{1,0:T(8,128)(2,1)S(1)} %get-tuple-element.45), channel_id=1, source_target_pairs={{0,7},{1,6},{2,5},{3,4},{4,3},{5,2},{6,1},{7,0},{8,15},{9,14},{10,... | collective-permute-start | bytes 307208 | tf_op jit(solution)/shard_map/ppermute | solution.py:287
  62.0 9.9 %collective-permute-start.11 = (bf16[768,128]{1,0:T(8,128)(2,1)S(1)}, bf16[768,128]{1,0:T(8,128)(2,1)S(1)}, u32[]{:S(2)}, u32[]{:S(2)}) collective-permute-start(bf16[768,128]{1,0:T(8,128)(2,1)S(1)} %get-tuple-element.47), channel_id=1, source_target_pairs={{0,1},{1,0},{2,3},{3,2},{4,5},{5,4},{6,7},{7,6},{8,9},{9,8},{10,11... | collective-permute-start | bytes 589832 | tf_op jit(solution)/shard_map/ppermute | solution.py:287
  63.4 8.9 %collective-permute-start.12 = (bf16[768,128]{1,0:T(8,128)(2,1)S(1)}, bf16[768,128]{1,0:T(8,128)(2,1)S(1)}, u32[]{:S(2)}, u32[]{:S(2)}) collective-permute-start(bf16[768,128]{1,0:T(8,128)(2,1)S(1)} %get-tuple-element.48), channel_id=1, source_target_pairs={{0,2},{1,3},{2,0},{3,1},{4,6},{5,7},{6,4},{7,5},{8,10},{9,11},{10,... | collective-permute-start | bytes 589832 | tf_op jit(solution)/shard_map/ppermute | solution.py:287
  67.3 6.7 %collective-permute-start.13 = (bf16[768,128]{1,0:T(8,128)(2,1)S(1)}, bf16[768,128]{1,0:T(8,128)(2,1)S(1)}, u32[]{:S(2)}, u32[]{:S(2)}) collective-permute-start(bf16[768,128]{1,0:T(8,128)(2,1)S(1)} %get-tuple-element.49), channel_id=1, source_target_pairs={{0,3},{1,2},{2,1},{3,0},{4,7},{5,6},{6,5},{7,4},{8,11},{9,10},{10,... | collective-permute-start | bytes 589832 | tf_op jit(solution)/shard_map/ppermute | solution.py:287
  70.3 4.9 %collective-permute-start.16 = (f32[2,12]{1,0:T(2,128)S(1)}, f32[2,12]{1,0:T(2,128)S(1)}, u32[]{:S(2)}, u32[]{:S(2)}) collective-permute-start(f32[2,12]{1,0:T(2,128)S(1)} %get-tuple-element.57), channel_id=1, source_target_pairs={{0,24},{8,16},{16,8},{24,0},{1,25},{9,17},{17,9},{25,1},{2,26},{10... | collective-permute-start | bytes 296 | tf_op jit(solution)/shard_map/ppermute | solution.py:287
  70.4 4.8 %collective-permute-start.15 = (f32[2,12]{1,0:T(2,128)S(1)}, f32[2,12]{1,0:T(2,128)S(1)}, u32[]{:S(2)}, u32[]{:S(2)}) collective-permute-start(f32[2,12]{1,0:T(2,128)S(1)} %get-tuple-element.56), channel_id=1, source_target_pairs={{0,16},{8,24},{16,0},{24,8},{1,17},{9,25},{17,1},{25,9},{2,18},{10... | collective-permute-start | bytes 296 | tf_op jit(solution)/shard_map/ppermute | solution.py:287
  72.0 3.3 %collective-permute-start.14 = (f32[2,12]{1,0:T(2,128)S(1)}, f32[2,12]{1,0:T(2,128)S(1)}, u32[]{:S(2)}, u32[]{:S(2)}) collective-permute-start(f32[2,12]{1,0:T(2,128)S(1)} %get-tuple-element.55), channel_id=1, source_target_pairs={{0,8},{8,0},{16,24},{24,16},{1,9},{9,1},{17,25},{25,17},{2,10},{10... | collective-permute-start | bytes 296 | tf_op jit(solution)/shard_map/ppermute | solution.py:287

commit v5 on v4

--- a/solution.py
+++ b/solution.py
@@ -27,7 +27,7 @@
     mine = lax.axis_index("gene") % members
     for hop in range(members):
         owner = mine ^ hop
-        near, far = outs[members].at[owner], outs[hop]
+        near, far = outs[hop], outs[members + hop]
         start = pl.multiple_of(owner * width, head_size)
         rows = []
         for head in range(share):
@@ -78,8 +78,7 @@
 def stage_kernel(plan, places, first, last, shift, *refs):
     members, share, scale = plan["members"], plan["share"], plan["scale"]
     count = len(places)
-    mine = lax.axis_index("gene") % members
-    near, rest = [refs[0].at[mine ^ hop] for hop in range(members)], refs[1:]
+    near, rest = refs[:members], refs[members:]
     fresh = [place for place in places if place >= members]
     pieces = [near[place] for place in places if place < members] + list(rest[: len(fresh)])
     steps = [(4 if place < members else 2) * BLOCK for place in places]
@@ -273,21 +272,17 @@
     cells = lax.axis_size("cell")
     plan["cells"] = cells
     near_rows = 4 * BLOCK * share + stat_rows
-    near_in = jax.ShapeDtypeStruct((members, near_rows, BLOCK), low)
+    near_in = jax.ShapeDtypeStruct((near_rows, BLOCK), low)
     far_in = jax.ShapeDtypeStruct((far_rows, BLOCK), low)
-    sent = call(functools.partial(pack_kernel, plan), [far_in] * members + [near_in], count=6)(
+    sent = call(functools.partial(pack_kernel, plan), [near_in] * members + [far_in] * members, count=6)(
         query_rows, key_rows, value_rows, output_rows, output_grad, jnp.transpose(row_lse, (2, 0, 1))
     )
-    groups = [list(range(at, at + members)) for at in range(0, blocks, members)]
-
-    def exchange(array):
-        return lax.all_to_all(array, "gene", 0, 0, axis_index_groups=groups)
 
     def move(array, hop, axis="gene", size=blocks):
         return lax.ppermute(array, axis, [(i, i ^ hop) for i in range(size)])
 
-    far = {hop: move(sent[hop % members], hop) for hop in range(members, blocks)}
-    near = exchange(sent[members])
+    far = {hop: move(sent[members + hop % members], hop) for hop in range(members, blocks)}
+    near = [sent[0]] + [move(sent[hop], hop) for hop in range(1, members)]
     (table,) = call(
         functools.partial(table_kernel, plan),
         [jax.ShapeDtypeStruct((blocks * members * share,), full)],
@@ -307,13 +302,13 @@
             [query_out] * count + ([owner_out] * members if last else [partial_out] * 2),
             scratch=[scratch, scratch, pltpu.VMEM((count, sum_rows, BLOCK), full)],
             smem_in=1,
-            count=1 + len(pieces) + len(partials),
+            count=members + len(pieces) + len(partials),
             limit=STAGE_LIMIT,
-        )(table, near, *pieces, *partials)
+        )(table, *near, *pieces, *partials)
         return made[:count], made[count:]
 
     queries, partials, begin = [], [], 0
-    for end in (members, blocks):
+    for end in (members, members + (blocks - members) // 2, blocks):
         places = tuple(range(begin, end))
         made, partials = stage(places, begin == 0, end == blocks, partials)
         queries += [move(piece, place) if place else piece for piece, place in zip(made, places)]

time: 76.1 us -> 75.9 us (level)
  waiting for transfers between devices: 29.7 us -> 20.2 us
  starting transfers between devices: 29.3 us -> 36.5 us
  Pallas kernels: 13.4 us -> 14.7 us
  local copies, waits for them, and re-layouts: 2.08 us -> 2.97 us
    all_to_all x1 -> x0, waiting for transfers between devices: 16.9 us -> none  [exchange(): return lax.all_to_all(array, 'gene', 0, 0, axis_index_groups=groups)]
    ppermute x17 -> x20, starting transfers between devices: 24 us -> 36.5 us  [move(): return lax.ppermute(array, axis, [(i, i ^ hop) for i in range(size)])]
    ppermute x17 -> x20, waiting for transfers between devices: 12.8 us -> 20.2 us  [move(): return lax.ppermute(array, axis, [(i, i ^ hop) for i in range(size)])]
    all_to_all x1 -> x0, starting transfers between devices: 5.39 us -> none  [exchange(): return lax.all_to_all(array, 'gene', 0, 0, axis_index_groups=groups)]
    pallas_call x2 -> x3, Pallas kernels: 6.28 us -> 7.68 us  [stage(): call(functools.partial(stage_kernel, plan, places, first, last), [query_o...]
    unnamed x17 -> x11, local copies, waits for them, and re-layouts: 0.8 us -> 1.7 us
  transfers between devices with their start and end apart: 18 -> 20, of which waited for: 7 -> 7; matrix products, arithmetic and copies ran while one was open for 2% -> 2% of each run, Pallas kernels for 13% -> 15%
where the time goes in v5:
time: 75.9 us; the launch traced here: 75.7 us
  starting transfers between devices  36.5 us (48%)
  waiting for transfers between devices  20.2 us (27%)
  Pallas kernels  14.7 us (19%)
  local copies, waits for them, and re-layouts  2.97 us (4%)
    ppermute x20, starting transfers between devices, move(): return lax.ppermute(array, axis, [(i, i ^ hop) for i in range(size)])  36.5 us
    ppermute x20, waiting for transfers between devices, move(): return lax.ppermute(array, axis, [(i, i ^ hop) for i in range(size)])  20.2 us
    pallas_call x3, Pallas kernels, stage(): call(functools.partial(stage_kernel, plan, places, first, last), [query_o...  7.68 us
    pallas_call x1, Pallas kernels, shards(): call(functools.partial(pack_kernel, plan), [near_in] * members + [far_in]...  3.26 us
    pallas_call x1, Pallas kernels, shards(): call(functools.partial(table_kernel, plan), [jax.ShapeDtypeStruct((blocks...  1.78 us
    unnamed x11, local copies, waits for them, and re-layouts  1.7 us
  transfers between devices with their start and end apart: 20, of which 7 were waited for; matrix products, arithmetic and copies ran while one was open for 2% of the time, Pallas kernels for 15%

profile of v5, /device:TPU:0, one launch (start us, length us, event | category | flops | bytes accessed | tf_op | source)
XLA Modules:
  0.0 75.7 jit_solution(10924302010957186353)
XLA Ops:
  0.6 3.3 %shard_map.121 = (bf16[1552,128]{1,0:T(8,128)(2,1)}, bf16[1552,128]{1,0:T(8,128)(2,1)}, bf16[1552,128]{1,0:T(8,128)(2,1)}, bf16[1552,128]{1,0:T(8,128)(2,1)}, bf...) custom-call(bf16[1,128,1536]{2,1,0:T(8,128)(2,1)} %query.1, ...), custom_call_target="tpu_custom_call" | custom-call | tf_op jit(solution)/shard_map/pallas_call | solution.py:277
  3.9 3.0 %collective-permute-start = (bf16[1552,128]{1,0:T(8,128)(2,1)}, bf16[1552,128]{1,0:T(8,128)(2,1)S(1)}, u32[]{:S(2)}, u32[]{:S(2)}) collective-permute-start(bf16[1552,128]{1,0:T(8,128)(2,1)} %get-tuple-element.37), channel_id=1, source_target_pairs={{0,1},{1,0},{2,3},{3,2},{4,5},{5,4},{6,7},{7,6},{8,9},{9,8},{10,11... | collective-permute-start | bytes 1191944 | tf_op jit(solution)/shard_map/ppermute | solution.py:282
  6.9 1.6 %collective-permute-start.1 = (bf16[1552,128]{1,0:T(8,128)(2,1)}, bf16[1552,128]{1,0:T(8,128)(2,1)S(1)}, u32[]{:S(2)}, u32[]{:S(2)}) collective-permute-start(bf16[1552,128]{1,0:T(8,128)(2,1)} %get-tuple-element.38), channel_id=1, source_target_pairs={{0,2},{1,3},{2,0},{3,1},{4,6},{5,7},{6,4},{7,5},{8,10},{9,11},{10,... | collective-permute-start | bytes 1191944 | tf_op jit(solution)/shard_map/ppermute | solution.py:282
  8.4 0.0 collective-permute-start.2
  8.4 3.0 %collective-permute-start.6 = (bf16[784,128]{1,0:T(8,128)(2,1)}, bf16[784,128]{1,0:T(8,128)(2,1)S(1)}, u32[]{:S(2)}, u32[]{:S(2)}) collective-permute-start(bf16[784,128]{1,0:T(8,128)(2,1)} %get-tuple-element.44), channel_id=1, source_target_pairs={{0,4},{1,5},{2,6},{3,7},{4,0},{5,1},{6,2},{7,3},{8,12},{9,13},{10,... | collective-permute-start | bytes 602120 | tf_op jit(solution)/shard_map/ppermute | solution.py:282
  11.4 1.3 %collective-permute-start.7 = (bf16[784,128]{1,0:T(8,128)(2,1)}, bf16[784,128]{1,0:T(8,128)(2,1)S(1)}, u32[]{:S(2)}, u32[]{:S(2)}) collective-permute-start(bf16[784,128]{1,0:T(8,128)(2,1)} %get-tuple-element.45), channel_id=1, source_target_pairs={{0,5},{1,4},{2,7},{3,6},{4,1},{5,0},{6,3},{7,2},{8,13},{9,12},{10,... | collective-permute-start | bytes 602120 | tf_op jit(solution)/shard_map/ppermute | solution.py:282
  12.7 6.9 %collective-permute-done.refs_1_ = bf16[1552,128]{1,0:T(8,128)(2,1)S(1)} collective-permute-done((bf16[1552,128]{1,0:T(8,128)(2,1)}, bf16[1552,128]{1,0:T(8,128)(2,1)S(1)}, u32[]{:S(2)}, u32[]{:S(2)}) %collective-permute-start) | collective-permute-done | bytes 397344 | tf_op jit(solution)/shard_map/ppermute | solution.py:282
  19.6 2.4 %collective-permute-start.10 = (bf16[784,128]{1,0:T(8,128)(2,1)}, bf16[784,128]{1,0:T(8,128)(2,1)S(1)}, u32[]{:S(2)}, u32[]{:S(2)}) collective-permute-start(bf16[784,128]{1,0:T(8,128)(2,1)} %get-tuple-element.50), channel_id=1, source_target_pairs={{0,6},{1,7},{2,4},{3,5},{4,2},{5,3},{6,0},{7,1},{8,14},{9,15},{10,... | collective-permute-start | bytes 602120 | tf_op jit(solution)/shard_map/ppermute | solution.py:282
  22.1 5.7 %collective-permute-done.1.refs_2_ = bf16[1552,128]{1,0:T(8,128)(2,1)S(1)} collective-permute-done((bf16[1552,128]{1,0:T(8,128)(2,1)}, bf16[1552,128]{1,0:T(8,128)(2,1)S(1)}, u32[]{:S(2)}, u32[]{:S(2)}) %collective-permute-start.1) | collective-permute-done | bytes 397344 | tf_op jit(solution)/shard_map/ppermute | solution.py:282
  27.8 3.5 %collective-permute-start.11 = (bf16[784,128]{1,0:T(8,128)(2,1)}, bf16[784,128]{1,0:T(8,128)(2,1)S(1)}, u32[]{:S(2)}, u32[]{:S(2)}) collective-permute-start(bf16[784,128]{1,0:T(8,128)(2,1)} %get-tuple-element.51), channel_id=1, source_target_pairs={{0,7},{1,6},{2,5},{3,4},{4,3},{5,2},{6,1},{7,0},{8,15},{9,14},{10,... | collective-permute-start | bytes 602120 | tf_op jit(solution)/shard_map/ppermute | solution.py:282
  31.4 0.6 reshape.16.index
  31.9 0.1 copy.13
  32.1 0.7 reshape.15.bias
  32.8 1.8 %shard_map.120.shift = f32[96]{0:T(128)} custom-call(f32[768]{0:T(1024)} %reshape.15.bias, s32[64]{0:T(128)} %reshape.16.index, s32[8]{0:T(128)} %count.1), custom_call_target="tpu_custom_call" | custom-call | tf_op jit(solution)/shard_map/pallas_call | solution.py:286
  34.5 0.1 collective-permute-done.2.refs_3_
  34.6 0.6 copy-done.1
  35.2 1.0 %copy-done = bf16[1552,128]{1,0:T(8,128)(2,1)S(1)} copy-done((bf16[1552,128]{1,0:T(8,128)(2,1)S(1)}, bf16[1552,128]{1,0:T(8,128)(2,1)}, u32[]{:S(2)}) %copy-start) | copy-done | bytes 397336
  36.2 3.1 %shard_map.122 = (bf16[400,128]{1,0:T(8,128)(2,1)S(1)}, bf16[400,128]{1,0:T(8,128)(2,1)S(1)}, bf16[400,128]{1,0:T(8,128)(2,1)S(1)}, bf16[400,128]{1,0:T(8,128)(2...) custom-call(f32[96]{0:T(128)S(1)} %copy-done.1, bf16[1552,128]{1,0:T(8,128)(2,1)S(1)} %copy-done, ...), custom_call_target="tpu_custom_call" | custom-call | tf_op jit(solution)/shard_map/pallas_call | solution.py:300
  39.3 1.6 %collective-permute-start.3 = (bf16[400,128]{1,0:T(8,128)(2,1)S(1)}, bf16[400,128]{1,0:T(8,128)(2,1)S(1)}, u32[]{:S(2)}, u32[]{:S(2)}) collective-permute-start(bf16[400,128]{1,0:T(8,128)(2,1)S(1)} %get-tuple-element.41), channel_id=1, source_target_pairs={{0,1},{1,0},{2,3},{3,2},{4,5},{5,4},{6,7},{7,6},{8,9},{9,8},{10,11... | collective-permute-start | bytes 307208 | tf_op jit(solution)/shard_map/ppermute | solution.py:282
  40.9 0.0 collective-permute-done.6.refs_4_
  40.9 0.0 collective-permute-start.4
  40.9 2.0 %collective-permute-start.5 = (bf16[400,128]{1,0:T(8,128)(2,1)S(1)}, bf16[400,128]{1,0:T(8,128)(2,1)S(1)}, u32[]{:S(2)}, u32[]{:S(2)}) collective-permute-start(bf16[400,128]{1,0:T(8,128)(2,1)S(1)} %get-tuple-element.43), channel_id=1, source_target_pairs={{0,3},{1,2},{2,1},{3,0},{4,7},{5,6},{6,5},{7,4},{8,11},{9,10},{10,... | collective-permute-start | bytes 307208 | tf_op jit(solution)/shard_map/ppermute | solution.py:282
  42.9 2.3 %shard_map.123 = (bf16[400,128]{1,0:T(8,128)(2,1)S(1)}, bf16[400,128]{1,0:T(8,128)(2,1)S(1)}, f32[3,512,128]{2,1,0:T(8,128)S(1)}, f32[3,512,128]{2,1,0:T(8,128)S(1)}) custom-call(f32[96]{0:T(128)S(1)} %copy-done.1, bf16[1552,128]{1,0:T(8,128)(2,1)S(1)} %copy-done, bf16[1552,128]{1,0:T(8,128)(2,1)S(1)} %collective-permute-done.refs_1_, ...), custom_call_target="tpu_custom_call" | custom-call | tf_op jit(solution)/shard_map/pallas_call | solution.py:300
  45.2 0.0 collective-permute-done.10.refs_4_
  45.2 9.3 %collective-permute-start.8 = (bf16[400,128]{1,0:T(8,128)(2,1)S(1)}, bf16[400,128]{1,0:T(8,128)(2,1)S(1)}, u32[]{:S(2)}, u32[]{:S(2)}) collective-permute-start(bf16[400,128]{1,0:T(8,128)(2,1)S(1)} %get-tuple-element.48), channel_id=1, source_target_pairs={{0,4},{1,5},{2,6},{3,7},{4,0},{5,1},{6,2},{7,3},{8,12},{9,13},{10,... | collective-permute-start | bytes 307208 | tf_op jit(solution)/shard_map/ppermute | solution.py:282
  54.5 0.0 collective-permute-done.11.refs_5_
  54.5 1.0 %collective-permute-start.9 = (bf16[400,128]{1,0:T(8,128)(2,1)S(1)}, bf16[400,128]{1,0:T(8,128)(2,1)S(1)}, u32[]{:S(2)}, u32[]{:S(2)}) collective-permute-start(bf16[400,128]{1,0:T(8,128)(2,1)S(1)} %get-tuple-element.49), channel_id=1, source_target_pairs={{0,5},{1,4},{2,7},{3,6},{4,1},{5,0},{6,3},{7,2},{8,13},{9,12},{10,... | collective-permute-start | bytes 307208 | tf_op jit(solution)/shard_map/ppermute | solution.py:282
  55.5 2.3 %shard_map.124 = (bf16[400,128]{1,0:T(8,128)(2,1)S(1)}, bf16[400,128]{1,0:T(8,128)(2,1)S(1)}, bf16[768,128]{1,0:T(8,128)(2,1)S(1)}, bf16[768,128]{1,0:T(8,128)(2...) custom-call(f32[96]{0:T(128)S(1)} %copy-done.1, bf16[1552,128]{1,0:T(8,128)(2,1)S(1)} %copy-done, ...), custom_call_target="tpu_custom_call" | custom-call | tf_op jit(solution)/shard_map/pallas_call | solution.py:300
  57.8 4.3 %collective-permute-start.12 = (bf16[400,128]{1,0:T(8,128)(2,1)S(1)}, bf16[400,128]{1,0:T(8,128)(2,1)S(1)}, u32[]{:S(2)}, u32[]{:S(2)}) collective-permute-start(bf16[400,128]{1,0:T(8,128)(2,1)S(1)} %get-tuple-element.54), channel_id=1, source_target_pairs={{0,6},{1,7},{2,4},{3,5},{4,2},{5,3},{6,0},{7,1},{8,14},{9,15},{10,... | collective-permute-start | bytes 307208 | tf_op jit(solution)/shard_map/ppermute | solution.py:282
  62.1 0.0 collective-permute-done.4.refs_2_
  62.1 0.0 collective-permute-start.13
  62.1 1.5 %collective-permute-start.14 = (bf16[768,128]{1,0:T(8,128)(2,1)S(1)}, bf16[768,128]{1,0:T(8,128)(2,1)S(1)}, u32[]{:S(2)}, u32[]{:S(2)}) collective-permute-start(bf16[768,128]{1,0:T(8,128)(2,1)S(1)} %get-tuple-element.57), channel_id=1, source_target_pairs={{0,1},{1,0},{2,3},{3,2},{4,5},{5,4},{6,7},{7,6},{8,9},{9,8},{10,11... | collective-permute-start | bytes 589832 | tf_op jit(solution)/shard_map/ppermute | solution.py:282
  63.7 0.0 collective-permute-done.8.refs_4_
  63.7 0.0 collective-permute-start.15
  63.7 2.0 %collective-permute-done.9.refs_5_ = bf16[400,128]{1,0:T(8,128)(2,1)S(1)} collective-permute-done((bf16[400,128]{1,0:T(8,128)(2,1)S(1)}, bf16[400,128]{1,0:T(8,128)(2,1)S(1)}, u32[]{:S(2)}, u32[]{:S(2)}) %collective-permute-start.9) | collective-permute-done | bytes 102432 | tf_op jit(solution)/shard_map/ppermute | solution.py:282
  65.7 0.2 collective-permute-done.12.refs_6_
  65.9 3.7 %collective-permute-done.13.refs_7_ = bf16[400,128]{1,0:T(8,128)(2,1)S(1)} collective-permute-done((bf16[400,128]{1,0:T(8,128)(2,1)S(1)}, bf16[400,128]{1,0:T(8,128)(2,1)S(1)}, u32[]{:S(2)}, u32[]{:S(2)}) %collective-permute-start.13) | collective-permute-done | bytes 102432 | tf_op jit(solution)/shard_map/ppermute | solution.py:282
  69.6 0.8 %shard_map.125 = (f32[2,12]{1,0:T(2,128)S(1)}, f32[2,12]{1,0:T(2,128)S(1)}, f32[2,12]{1,0:T(2,128)S(1)}, f32[2,12]{1,0:T(2,128)S(1)}) custom-call(s32[64]{0:T(128)S(1)} %copy-done.2, bf16[400,128]{1,0:T(8,128)(2,1)S(1)} %get-tuple-element.40.refs_0_, bf16[400,128]{1,0:T(8,128)(2,1)S(1)} %collective-permute-done.3.refs_1_, ...), custom_call_target="tpu_custom_call" | custom-call | flops 40000000000 | tf_op jit(solution)/shard_map/pallas_call | solution.py:319
  70.4 0.1 collective-permute-start.17
  70.5 1.6 %collective-permute-start.18 = (f32[2,12]{1,0:T(2,128)S(1)}, f32[2,12]{1,0:T(2,128)S(1)}, u32[]{:S(2)}, u32[]{:S(2)}) collective-permute-start(f32[2,12]{1,0:T(2,128)S(1)} %get-tuple-element.66), channel_id=1, source_target_pairs={{0,16},{8,24},{16,0},{24,8},{1,17},{9,25},{17,1},{25,9},{2,18},{10... | collective-permute-start | bytes 296 | tf_op jit(solution)/shard_map/ppermute | solution.py:282
  72.1 0.0 collective-permute-done.14.refs_9_
  72.1 0.3 collective-permute-start.19
  72.4 1.5 %collective-permute-done.16.refs_11_ = bf16[768,128]{1,0:T(8,128)(2,1)S(1)} collective-permute-done((bf16[768,128]{1,0:T(8,128)(2,1)S(1)}, bf16[768,128]{1,0:T(8,128)(2,1)S(1)}, u32[]{:S(2)}, u32[]{:S(2)}) %collective-permute-start.16) | collective-permute-done | bytes 196640 | tf_op jit(solution)/shard_map/ppermute | solution.py:282
  73.9 1.2 %shard_map.126 = (bf16[1,128,1536]{2,1,0:T(8,128)(2,1)}, bf16[1,128,1536]{2,1,0:T(8,128)(2,1)}, bf16[1,128,1536]{2,1,0:T(8,128)(2,1)}, f32[2,12]{1,0:T(2,128)S(1)}) custom-call(bf16[400,128]{1,0:T(8,128)(2,1)S(1)} %get-tuple-element.40.refs_0_, bf16[400,128]{1,0:T(8,128)(2,1)S(1)} %collective-permute-done.3.refs_1_, ...), custom_call_target="tpu_custom_call" | custom-call | tf_op jit(solution)/shard_map/pallas_call | solution.py:332
  75.1 0.0 collective-permute-done.17
  75.1 0.0 collective-permute-done.18
  75.1 0.0 collective-permute-done.19
  75.1 0.6 add_bitcast_fusion
  (13 shorter events, 0.0 us)
Async XLA Ops:
  0.6 31.3 %copy-start.3 = (f32[8,12,8]{1,2,0:T(8,128)S(1)}, f32[8,12,8]{1,2,0:T(8,128)}, u32[]{:S(2)}) copy-start(f32[8,12,8]{1,2,0:T(8,128)} %param.15) | copy-start | bytes 9220
  3.9 15.7 %collective-permute-start = (bf16[1552,128]{1,0:T(8,128)(2,1)}, bf16[1552,128]{1,0:T(8,128)(2,1)S(1)}, u32[]{:S(2)}, u32[]{:S(2)}) collective-permute-start(bf16[1552,128]{1,0:T(8,128)(2,1)} %get-tuple-element.37), channel_id=1, source_target_pairs={{0,1},{1,0},{2,3},{3,2},{4,5},{5,4},{6,7},{7,6},{8,9},{9,8},{10,11... | collective-permute-start | bytes 1191944 | tf_op jit(solution)/shard_map/ppermute | solution.py:282
  6.9 20.9 %collective-permute-start.1 = (bf16[1552,128]{1,0:T(8,128)(2,1)}, bf16[1552,128]{1,0:T(8,128)(2,1)S(1)}, u32[]{:S(2)}, u32[]{:S(2)}) collective-permute-start(bf16[1552,128]{1,0:T(8,128)(2,1)} %get-tuple-element.38), channel_id=1, source_target_pairs={{0,2},{1,3},{2,0},{3,1},{4,6},{5,7},{6,4},{7,5},{8,10},{9,11},{10,... | collective-permute-start | bytes 1191944 | tf_op jit(solution)/shard_map/ppermute | solution.py:282
  8.4 22.9 %copy-start.4 = (s32[8,8]{1,0:T(8,128)S(1)}, s32[8,8]{1,0:T(8,128)}, u32[]{:S(2)}) copy-start(s32[8,8]{1,0:T(8,128)} %param.16) | copy-start | bytes 772
  8.4 26.2 %collective-permute-start.2 = (bf16[1552,128]{1,0:T(8,128)(2,1)}, bf16[1552,128]{1,0:T(8,128)(2,1)S(1)}, u32[]{:S(2)}, u32[]{:S(2)}) collective-permute-start(bf16[1552,128]{1,0:T(8,128)(2,1)} %get-tuple-element.39), channel_id=1, source_target_pairs={{0,3},{1,2},{2,1},{3,0},{4,7},{5,6},{6,5},{7,4},{8,11},{9,10},{10,... | collective-permute-start | bytes 1191944 | tf_op jit(solution)/shard_map/ppermute | solution.py:282
  8.4 32.5 %collective-permute-start.6 = (bf16[784,128]{1,0:T(8,128)(2,1)}, bf16[784,128]{1,0:T(8,128)(2,1)S(1)}, u32[]{:S(2)}, u32[]{:S(2)}) collective-permute-start(bf16[784,128]{1,0:T(8,128)(2,1)} %get-tuple-element.44), channel_id=1, source_target_pairs={{0,4},{1,5},{2,6},{3,7},{4,0},{5,1},{6,2},{7,3},{8,12},{9,13},{10,... | collective-permute-start | bytes 602120 | tf_op jit(solution)/shard_map/ppermute | solution.py:282
  11.4 29.5 %collective-permute-start.7 = (bf16[784,128]{1,0:T(8,128)(2,1)}, bf16[784,128]{1,0:T(8,128)(2,1)S(1)}, u32[]{:S(2)}, u32[]{:S(2)}) collective-permute-start(bf16[784,128]{1,0:T(8,128)(2,1)} %get-tuple-element.45), channel_id=1, source_target_pairs={{0,5},{1,4},{2,7},{3,6},{4,1},{5,0},{6,3},{7,2},{8,13},{9,12},{10,... | collective-permute-start | bytes 602120 | tf_op jit(solution)/shard_map/ppermute | solution.py:282
  19.6 25.5 %collective-permute-start.10 = (bf16[784,128]{1,0:T(8,128)(2,1)}, bf16[784,128]{1,0:T(8,128)(2,1)S(1)}, u32[]{:S(2)}, u32[]{:S(2)}) collective-permute-start(bf16[784,128]{1,0:T(8,128)(2,1)} %get-tuple-element.50), channel_id=1, source_target_pairs={{0,6},{1,7},{2,4},{3,5},{4,2},{5,3},{6,0},{7,1},{8,14},{9,15},{10,... | collective-permute-start | bytes 602120 | tf_op jit(solution)/shard_map/ppermute | solution.py:282
  27.8 26.7 %collective-permute-start.11 = (bf16[784,128]{1,0:T(8,128)(2,1)}, bf16[784,128]{1,0:T(8,128)(2,1)S(1)}, u32[]{:S(2)}, u32[]{:S(2)}) collective-permute-start(bf16[784,128]{1,0:T(8,128)(2,1)} %get-tuple-element.51), channel_id=1, source_target_pairs={{0,7},{1,6},{2,5},{3,4},{4,3},{5,2},{6,1},{7,0},{8,15},{9,14},{10,... | collective-permute-start | bytes 602120 | tf_op jit(solution)/shard_map/ppermute | solution.py:282
  34.5 0.7 copy-start.1
  35.2 1.0 %copy-start = (bf16[1552,128]{1,0:T(8,128)(2,1)S(1)}, bf16[1552,128]{1,0:T(8,128)(2,1)}, u32[]{:S(2)}) copy-start(bf16[1552,128]{1,0:T(8,128)(2,1)} %get-tuple-element.36.refs_0_) | copy-start | bytes 1191940
  39.3 18.5 %collective-permute-start.3 = (bf16[400,128]{1,0:T(8,128)(2,1)S(1)}, bf16[400,128]{1,0:T(8,128)(2,1)S(1)}, u32[]{:S(2)}, u32[]{:S(2)}) collective-permute-start(bf16[400,128]{1,0:T(8,128)(2,1)S(1)} %get-tuple-element.41), channel_id=1, source_target_pairs={{0,1},{1,0},{2,3},{3,2},{4,5},{5,4},{6,7},{7,6},{8,9},{9,8},{10,11... | collective-permute-start | bytes 307208 | tf_op jit(solution)/shard_map/ppermute | solution.py:282
  40.9 21.2 %collective-permute-start.4 = (bf16[400,128]{1,0:T(8,128)(2,1)S(1)}, bf16[400,128]{1,0:T(8,128)(2,1)S(1)}, u32[]{:S(2)}, u32[]{:S(2)}) collective-permute-start(bf16[400,128]{1,0:T(8,128)(2,1)S(1)} %get-tuple-element.42), channel_id=1, source_target_pairs={{0,2},{1,3},{2,0},{3,1},{4,6},{5,7},{6,4},{7,5},{8,10},{9,11},{10,... | collective-permute-start | bytes 307208 | tf_op jit(solution)/shard_map/ppermute | solution.py:282
  40.9 21.2 %collective-permute-start.5 = (bf16[400,128]{1,0:T(8,128)(2,1)S(1)}, bf16[400,128]{1,0:T(8,128)(2,1)S(1)}, u32[]{:S(2)}, u32[]{:S(2)}) collective-permute-start(bf16[400,128]{1,0:T(8,128)(2,1)S(1)} %get-tuple-element.43), channel_id=1, source_target_pairs={{0,3},{1,2},{2,1},{3,0},{4,7},{5,6},{6,5},{7,4},{8,11},{9,10},{10,... | collective-permute-start | bytes 307208 | tf_op jit(solution)/shard_map/ppermute | solution.py:282
  45.2 18.5 %collective-permute-start.8 = (bf16[400,128]{1,0:T(8,128)(2,1)S(1)}, bf16[400,128]{1,0:T(8,128)(2,1)S(1)}, u32[]{:S(2)}, u32[]{:S(2)}) collective-permute-start(bf16[400,128]{1,0:T(8,128)(2,1)S(1)} %get-tuple-element.48), channel_id=1, source_target_pairs={{0,4},{1,5},{2,6},{3,7},{4,0},{5,1},{6,2},{7,3},{8,12},{9,13},{10,... | collective-permute-start | bytes 307208 | tf_op jit(solution)/shard_map/ppermute | solution.py:282
  54.5 11.2 %collective-permute-start.9 = (bf16[400,128]{1,0:T(8,128)(2,1)S(1)}, bf16[400,128]{1,0:T(8,128)(2,1)S(1)}, u32[]{:S(2)}, u32[]{:S(2)}) collective-permute-start(bf16[400,128]{1,0:T(8,128)(2,1)S(1)} %get-tuple-element.49), channel_id=1, source_target_pairs={{0,5},{1,4},{2,7},{3,6},{4,1},{5,0},{6,3},{7,2},{8,13},{9,12},{10,... | collective-permute-start | bytes 307208 | tf_op jit(solution)/shard_map/ppermute | solution.py:282
  57.8 8.1 %collective-permute-start.12 = (bf16[400,128]{1,0:T(8,128)(2,1)S(1)}, bf16[400,128]{1,0:T(8,128)(2,1)S(1)}, u32[]{:S(2)}, u32[]{:S(2)}) collective-permute-start(bf16[400,128]{1,0:T(8,128)(2,1)S(1)} %get-tuple-element.54), channel_id=1, source_target_pairs={{0,6},{1,7},{2,4},{3,5},{4,2},{5,3},{6,0},{7,1},{8,14},{9,15},{10,... | collective-permute-start | bytes 307208 | tf_op jit(solution)/shard_map/ppermute | solution.py:282
  62.1 7.5 %collective-permute-start.13 = (bf16[400,128]{1,0:T(8,128)(2,1)S(1)}, bf16[400,128]{1,0:T(8,128)(2,1)S(1)}, u32[]{:S(2)}, u32[]{:S(2)}) collective-permute-start(bf16[400,128]{1,0:T(8,128)(2,1)S(1)} %get-tuple-element.55), channel_id=1, source_target_pairs={{0,7},{1,6},{2,5},{3,4},{4,3},{5,2},{6,1},{7,0},{8,15},{9,14},{10,... | collective-permute-start | bytes 307208 | tf_op jit(solution)/shard_map/ppermute | solution.py:282
  62.1 9.9 %collective-permute-start.14 = (bf16[768,128]{1,0:T(8,128)(2,1)S(1)}, bf16[768,128]{1,0:T(8,128)(2,1)S(1)}, u32[]{:S(2)}, u32[]{:S(2)}) collective-permute-start(bf16[768,128]{1,0:T(8,128)(2,1)S(1)} %get-tuple-element.57), channel_id=1, source_target_pairs={{0,1},{1,0},{2,3},{3,2},{4,5},{5,4},{6,7},{7,6},{8,9},{9,8},{10,11... | collective-permute-start | bytes 589832 | tf_op jit(solution)/shard_map/ppermute | solution.py:282
  63.7 8.7 %collective-permute-start.15 = (bf16[768,128]{1,0:T(8,128)(2,1)S(1)}, bf16[768,128]{1,0:T(8,128)(2,1)S(1)}, u32[]{:S(2)}, u32[]{:S(2)}) collective-permute-start(bf16[768,128]{1,0:T(8,128)(2,1)S(1)} %get-tuple-element.58), channel_id=1, source_target_pairs={{0,2},{1,3},{2,0},{3,1},{4,6},{5,7},{6,4},{7,5},{8,10},{9,11},{10,... | collective-permute-start | bytes 589832 | tf_op jit(solution)/shard_map/ppermute | solution.py:282
  65.7 3.9 %copy-start.2 = (s32[64]{0:T(128)S(1)}, s32[64]{0:T(128)}, u32[]{:S(2)}) copy-start(s32[64]{0:T(128)} %reshape.16.index) | copy-start | bytes 772
  65.7 8.2 %collective-permute-start.16 = (bf16[768,128]{1,0:T(8,128)(2,1)S(1)}, bf16[768,128]{1,0:T(8,128)(2,1)S(1)}, u32[]{:S(2)}, u32[]{:S(2)}) collective-permute-start(bf16[768,128]{1,0:T(8,128)(2,1)S(1)} %get-tuple-element.59), channel_id=1, source_target_pairs={{0,3},{1,2},{2,1},{3,0},{4,7},{5,6},{6,5},{7,4},{8,11},{9,10},{10,... | collective-permute-start | bytes 589832 | tf_op jit(solution)/shard_map/ppermute | solution.py:282
  70.4 4.7 %collective-permute-start.17 = (f32[2,12]{1,0:T(2,128)S(1)}, f32[2,12]{1,0:T(2,128)S(1)}, u32[]{:S(2)}, u32[]{:S(2)}) collective-permute-start(f32[2,12]{1,0:T(2,128)S(1)} %get-tuple-element.65), channel_id=1, source_target_pairs={{0,8},{8,0},{16,24},{24,16},{1,9},{9,1},{17,25},{25,17},{2,10},{10... | collective-permute-start | bytes 296 | tf_op jit(solution)/shard_map/ppermute | solution.py:282
  70.5 4.6 %collective-permute-start.18 = (f32[2,12]{1,0:T(2,128)S(1)}, f32[2,12]{1,0:T(2,128)S(1)}, u32[]{:S(2)}, u32[]{:S(2)}) collective-permute-start(f32[2,12]{1,0:T(2,128)S(1)} %get-tuple-element.66), channel_id=1, source_target_pairs={{0,16},{8,24},{16,0},{24,8},{1,17},{9,25},{17,1},{25,9},{2,18},{10... | collective-permute-start | bytes 296 | tf_op jit(solution)/shard_map/ppermute | solution.py:282
  72.1 3.0 %collective-permute-start.19 = (f32[2,12]{1,0:T(2,128)S(1)}, f32[2,12]{1,0:T(2,128)S(1)}, u32[]{:S(2)}, u32[]{:S(2)}) collective-permute-start(f32[2,12]{1,0:T(2,128)S(1)} %get-tuple-element.67), channel_id=1, source_target_pairs={{0,24},{8,16},{16,8},{24,0},{1,25},{9,17},{17,9},{25,1},{2,26},{10... | collective-permute-start | bytes 296 | tf_op jit(solution)/shard_map/ppermute | solution.py:282
